TPU v7x, 32 devices: a whole 2x2x4 slice. The times are simulated.
32 devices in a mesh: grp: 2 (over y), seq: 16 (over z, x, core).
Axes of the slice: x: 2, y: 2, z: 4, core: 2. Of those that a mesh axis runs over, the one named last changes fastest.
Arguments:
- queries: bfloat16 [4096, 2048], P(('grp', 'seq')), parts along dimension 0, may hold values from -6 to 6
- keys: bfloat16 [4096, 2048], P(('grp', 'seq')), parts along dimension 0, may hold values from -6 to 6
- values: bfloat16 [4096, 2048], P(('grp', 'seq')), parts along dimension 0, may hold values from -6 to 6
- out_grad: bfloat16 [4096, 2048], P(('grp', 'seq')), parts along dimension 0, may hold values from -6 to 6
- filter_taps: float32 [256, 2048], P('seq'), may hold values from -0.375 to 0.375
Outputs:
- q_grad: bfloat16 [4096, 2048], P(('grp', 'seq')), parts along dimension 0
- k_grad: bfloat16 [4096, 2048], P(('grp', 'seq')), parts along dimension 0
- v_grad: bfloat16 [4096, 2048], P(('grp', 'seq')), parts along dimension 0
- filter_grad: float32 [512, 2048], P(('grp', 'seq')), parts along dimension 0
There are 2 independent parts, one for each index of `grp`. A program takes and returns all parts, laid end to end along the dimension named above; an argument that names none is the same for every part. Nothing has to cross between parts.
All inputs are finite; a program needn't handle non-finite values.
Results may differ from a plain program's by a relative error of at most 0.005.
Values may be sent and summed in bfloat16 or wider, within the bound.
No kernel may reach another device: no remote copies, remote signals or barrier semaphores. Data moves between devices by JAX's collectives and lax.ppermute only.
A program may use at most 64 MiB of HBM per device.

v0:
```python
import math

import jax
import jax.numpy as jnp
import numpy as np
from jax import lax
from jax.experimental import pallas as pl
from jax.experimental.pallas import tpu as pltpu
from jax.sharding import PartitionSpec as P

PLANE = 4
VMEM_BYTES = 32 * 1024 * 1024
LONG = 10**10


def tables(block):
    half = np.concatenate([np.arange(0, block, 2), np.arange(1, block, 2)])
    angle = np.pi * (half[:, None] + 0.5) * np.arange(block)[None, :] / block
    forward = np.concatenate([np.cos(angle), -np.sin(angle)], 0)
    inverse = forward.T / block
    return forward, inverse


def pair(table):
    high = table.astype(np.float32).astype(jnp.bfloat16)
    low = (table - high.astype(np.float64)).astype(np.float32).astype(jnp.bfloat16)
    return jnp.asarray(high), jnp.asarray(low)


def dot(left, right):
    return jnp.dot(left, right, preferred_element_type=jnp.float32)


def spectrum(high, low, block):
    return dot(high[...], block) + dot(low[...], block)


def restore(high, low, real, imag):
    spec = jnp.concatenate([real, imag], 0)
    top = spec.astype(jnp.bfloat16)
    rest = (spec - top.astype(jnp.float32)).astype(jnp.bfloat16)
    return dot(high[...], top) + dot(low[...], top) + dot(high[...], rest)


def parts(spec):
    half = spec.shape[0] // 2
    return spec[:half], spec[half:]


def turned(spec, sign):
    real, imag = parts(spec)
    quarter = real.shape[0] // 2
    flip = lambda a, s: jnp.concatenate([s * a[:quarter], -s * a[quarter:]], 0)
    return flip(imag, -sign), flip(real, sign)


def window(near, far, sign):
    real, imag = parts(near)
    other_real, other_imag = turned(far, sign)
    return real + other_real, imag + other_imag


def times(left, right):
    return left[0] * right[0] - left[1] * right[1], left[0] * right[1] + left[1] * right[0]


def times_conj(left, right):
    return left[0] * right[0] + left[1] * right[1], left[1] * right[0] - left[0] * right[1]


def call(body, outs, args, scratch=(), spaces=None, after=(), flops=1):
    specs = [
        pl.BlockSpec(memory_space=pltpu.SMEM if a.ndim == 1 else pltpu.VMEM) for a in args
    ]
    specs += [pl.BlockSpec(memory_space=pl.ANY)] * len(after)

    def run(*refs):
        body(*refs[: len(args)], *refs[len(args) + len(after) :])

    spaces = spaces or [pltpu.VMEM] * len(outs)
    return pl.pallas_call(
        run,
        out_shape=outs,
        in_specs=specs,
        out_specs=[pl.BlockSpec(memory_space=space) for space in spaces],
        scratch_shapes=scratch,
        compiler_params=pltpu.CompilerParams(vmem_limit_bytes=VMEM_BYTES),
        cost_estimate=pl.CostEstimate(flops=flops, bytes_accessed=1, transcendentals=0),
    )(*args, *after)


def shards(queries, keys, values, out_grad, filter_taps):
    f32, bf16 = jnp.float32, jnp.bfloat16
    rows, channels = queries.shape
    nseq = lax.axis_size("seq")
    own_taps = filter_taps.shape[0]
    taps = own_taps * nseq
    planes = nseq // PLANE
    width = channels // PLANE
    tokens = rows * PLANE
    pad_taps = max(16, own_taps)
    plane_taps = taps // planes
    column = planes * pad_taps
    assert tokens == 2 * taps
    me = lax.axis_index("seq")
    place = jnp.stack([me % PLANE, me // PLANE]).astype(jnp.int32)
    devices = range(nseq)

    forward, inverse = tables(taps)
    fwd = pair(forward)
    inv = pair(inverse)
    lag_of = np.full((planes * PLANE, pad_taps), -1)
    lag_of[:, :own_taps] = np.arange(taps).reshape(planes * PLANE, own_taps)
    lag_of = lag_of.reshape(planes, PLANE, pad_taps).transpose(1, 0, 2).reshape(-1)
    fwd_lag = pair(np.where(lag_of[None, :] >= 0, forward[:, np.maximum(lag_of, 0)], 0.0))

    def swap(array, distance):
        return lax.ppermute(array, "seq", [(i, i ^ distance) for i in devices])

    def shift(array, distance):
        return lax.ppermute(
            array, "seq", [(i, i + distance) for i in devices if i + distance in devices]
        )

    def struct(r, c, dtype):
        return jax.ShapeDtypeStruct((r, c), dtype)

    def block_at(index, size):
        return pl.ds(pl.multiple_of(index * size, size), size)

    def lay_taps(place_ref, *refs):
        ins, (keep, side, full) = refs[:planes], refs[planes:]
        q, z = place_ref[0], place_ref[1]
        for step in range(planes):
            full[block_at(z ^ step, pad_taps)] = ins[step][...]
        for step, (out, half) in enumerate(((keep, 0), (side, 0), (keep, 1), (side, 1))):
            out[half * column : (half + 1) * column] = full[:, block_at(q ^ step, width)]

    def narrow_taps(taps_ref, out):
        out[:own_taps] = taps_ref[...].astype(bf16)
        if pad_taps > own_taps:
            out[own_taps:] = jnp.zeros((pad_taps - own_taps, channels), bf16)

    def gate_grad(place_ref, o_ref, q_ref, p_ref, keep, side):
        q = place_ref[0]
        side[:rows] = p_ref[...]
        for step, (out, first) in enumerate(((keep, 0), (side, rows), (keep, rows), (side, 2 * rows))):
            at = block_at(q ^ step, width)
            out[first : first + rows] = (
                o_ref[:, at].astype(f32) * q_ref[:, at].astype(f32)
            ).astype(bf16)

    def join(left, right, after=()):
        def body(left_ref, right_ref, out):
            out[:rows] = left_ref[left.shape[0] - rows :]
            out[rows:] = right_ref[right.shape[0] - rows :]

        return call(body, [struct(2 * rows, width, bf16)], [left, right], after=after)[0]

    def gather_product(place_ref, *refs):
        ins, (product, top) = refs[:PLANE], refs[PLANE:]
        q = place_ref[0]
        for step in range(PLANE):
            product[block_at(q ^ step, rows)] = ins[step][:rows]
        top[...] = product[tokens - taps :]

    def join_taps(keep, near, ship):
        ship[:column] = keep[column:]
        ship[column:] = near[column:]

    def gather_grad(place_ref, keep, near, far, grad, bottom):
        q = place_ref[0]
        grad[block_at(q, rows)] = keep[:rows]
        grad[block_at(q ^ 1, rows)] = near[rows : 2 * rows]
        grad[block_at(q ^ 2, rows)] = far[:rows]
        grad[block_at(q ^ 3, rows)] = far[rows:]
        bottom[...] = grad[:taps]

    def own_spectra(array):
        def body(high, low, ref, *outs):
            for block in range(2):
                outs[block][...] = spectrum(high, low, ref[block * taps : (block + 1) * taps])

        return call(body, [struct(2 * taps, width, f32)] * 2, [*fwd, array])

    def lags(place_ref, inv_high, inv_low, p0, p1, g0, g1, behind, *refs):
        outs, full = refs[:-1], refs[-1]
        one = times_conj(parts(g0[...]), window(p0[...], behind[...], 1.0))
        two = times_conj(parts(g1[...]), window(p1[...], p0[...], 1.0))
        full[...] = restore(inv_high, inv_low, one[0] + two[0], one[1] + two[1])
        for step in range(planes):
            block = full[block_at(place_ref[1] ^ step, plane_taps)]
            outs[step][...] = block.astype(outs[step].dtype)

    def mix(place_ref, high, low, lag_high, lag_low, inv_high, inv_low, p0, p1, halo, *refs):
        keep, near, far, spec, spec_behind, own, side, ship, filt, mixed = refs
        q = place_ref[0]
        filt[block_at(q, column)] = keep[:column]
        filt[block_at(q ^ 1, column)] = near[:column]
        filt[block_at(q ^ 2, column)] = far[:column]
        filt[block_at(q ^ 3, column)] = far[column:]
        taps_spec = spectrum(lag_high, lag_low, filt[...])
        spec[...] = taps_spec
        spec_behind[...] = spectrum(high, low, halo[...])
        behind = (spec_behind, p0, p1)
        for block in range(2):
            value = times(parts(taps_spec), window(behind[block + 1][...], behind[block][...], 1.0))
            at = slice(block * taps, (block + 1) * taps)
            mixed[at] = restore(inv_high, inv_low, *value).astype(bf16)
        split(q, mixed, own, side, ship)

    def pick(ref, index):
        if own_taps % 8 == 0:
            return ref[block_at(index, own_taps)]
        value = ref[:own_taps]
        for n in range(1, PLANE):
            value = jnp.where(index == n, ref[n * own_taps : (n + 1) * own_taps], value)
        return value

    def split(q, source, own, side, ship):
        own[...] = source[block_at(q, rows)]
        side[...] = source[block_at(q ^ 1, rows)]
        ship[:rows] = source[block_at(q ^ 2, rows)]
        ship[rows:] = source[block_at(q ^ 3, rows)]

    def correlate(place_ref, high, low, inv_high, inv_low, g0, g1, halo, taps_ref, *refs):
        corr = refs[3]
        taps_spec = parts(taps_ref[...])
        ahead = (g0[...], g1[...], spectrum(high, low, halo[...]))
        for block in range(2):
            value = times_conj(window(ahead[block], ahead[block + 1], -1.0), taps_spec)
            at = slice(block * taps, (block + 1) * taps)
            corr[at] = restore(inv_high, inv_low, *value).astype(bf16)
        split(place_ref[0], corr, *refs[:3])

    def add_lags(place_ref, *refs):
        ins, outs, full = refs[:planes], refs[planes:-1], refs[-1]
        total = ins[0][...]
        for ref in ins[1:]:
            total = total + ref[...].astype(f32)
        full[...] = total * (1.0 / math.sqrt(rows * nseq))
        for step, out in enumerate(outs):
            out[...] = pick(full, place_ref[0] ^ step)

    def write(place_ref, blocks, gates, outs, held, sems):
        copies = []
        for step in range(PLANE):
            at = block_at(place_ref[0] ^ step, width)
            value = blocks[step].astype(f32)
            for n, (gate, out) in enumerate(zip(gates, outs)):
                held[n, step] = (value * gate[:, at].astype(f32)).astype(bf16)
                copy = pltpu.make_async_copy(held.at[n, step], out.at[:, at], sems.at[n, step])
                copy.start()
                copies.append(copy)
        return copies

    def finish_mixed(place_ref, own, near, far, o_ref, out, mark, held, sems):
        blocks = (own[...], near[:rows], far[:rows], near[rows:])
        copies = write(place_ref, blocks, [o_ref], [out], held, sems)
        mark[...] = jnp.zeros_like(mark)
        for copy in copies:
            copy.wait()

    def finish_corr(place_ref, own, near, far, v_ref, k_ref, *refs):
        lag_refs, (dk, dv, df, held, full, sems, sem) = refs[:PLANE], refs[PLANE:]
        q = place_ref[0]
        blocks = (own[...], near[:rows], far[:rows], near[rows:])
        copies = write(place_ref, blocks, [v_ref, k_ref], [dk, dv], held, sems)
        for step in range(PLANE):
            full[:, block_at(q ^ step, width)] = lag_refs[step][...]
        copy = pltpu.make_async_copy(full, df, sem)
        copy.start()
        for copy in copies + [copy]:
            copy.wait()

    block = struct(rows, width, bf16)
    double = struct(2 * rows, width, bf16)
    spectral = struct(2 * taps, width, f32)
    halo = struct(taps, width, bf16)

    def product_block(step):
        start = (place[0] ^ step) * width
        left = lax.dynamic_slice_in_dim(keys, start, width, 1).astype(f32)
        right = lax.dynamic_slice_in_dim(values, start, width, 1).astype(f32)
        return (left * right).astype(bf16)

    sent = [product_block(step) for step in range(PLANE)]
    far_p = [swap(sent[step], step) for step in (2, 3)]
    keep, side = call(
        gate_grad,
        [double, struct(3 * rows, width, bf16)],
        [place, out_grad, queries, sent[1]],
    )
    near = swap(side, 1)
    far = swap(join(keep, near), 2)

    (narrow,) = call(
        narrow_taps, [struct(pad_taps, channels, bf16)], [filter_taps], after=[near]
    )
    far_taps = [swap(narrow, PLANE * step) for step in range(1, planes)]
    taps_keep, taps_side = call(
        lay_taps,
        [struct(2 * column, width, bf16)] * 2,
        [place, narrow, *far_taps],
        scratch=[pltpu.VMEM((column, channels), bf16)],
        after=far_p,
    )
    taps_near = swap(taps_side, 1)
    (taps_ship,) = call(join_taps, [struct(2 * column, width, bf16)], [taps_keep, taps_near])
    taps_far = swap(taps_ship, 2)

    product, top = call(
        gather_product,
        [struct(tokens, width, bf16), halo],
        [place, sent[0], near, *far_p],
    )
    behind = shift(top, PLANE)
    p_spec = own_spectra(product)

    grad, bottom = call(
        gather_grad,
        [struct(tokens, width, bf16), halo],
        [place, keep, near, far],
        after=[taps_ship],
    )
    ahead = shift(bottom, -PLANE)
    g_spec = own_spectra(grad)

    taps_spec, behind_spec, own, side, ship = call(
        mix,
        [spectral, spectral, block, block, double],
        [place, *fwd, *fwd_lag, *inv, *p_spec, behind, taps_keep, taps_near, taps_far],
        scratch=[
            pltpu.VMEM((PLANE * column, width), bf16),
            pltpu.VMEM((tokens, width), bf16),
        ],
    )
    own_lags, *away = call(
        lags,
        [struct(plane_taps, width, f32)] + [struct(plane_taps, width, bf16)] * (planes - 1),
        [place, *inv, *p_spec, *g_spec, behind_spec],
        scratch=[pltpu.VMEM((taps, width), f32)],
    )
    far = swap(ship, 2)
    away = [swap(part, PLANE * (step + 1)) for step, part in enumerate(away)]
    corr_own, corr_side, corr_ship = call(
        correlate,
        [block, block, double],
        [place, *fwd, *inv, *g_spec, ahead, taps_spec],
        scratch=[pltpu.VMEM((tokens, width), bf16)],
        flops=LONG,
    )
    corr_far = swap(corr_ship, 2)
    near = swap(join(side, far, after=[corr_own]), 1)
    lag_blocks = call(
        add_lags,
        [struct(own_taps, width, f32)] * PLANE,
        [place, own_lags, *away],
        scratch=[pltpu.VMEM((plane_taps, width), f32)],
        after=[corr_own],
        flops=LONG,
    )
    lag_got = {step: swap(lag_blocks[step], step) for step in (2, 3, 1)}

    whole = struct(rows, channels, bf16)
    q_grad, mark = call(
        finish_mixed,
        [whole, struct(8, 128, f32)],
        [place, own, near, far, out_grad],
        scratch=[
            pltpu.VMEM((1, PLANE, rows, width), bf16),
            pltpu.SemaphoreType.DMA((1, PLANE)),
        ],
        spaces=[pl.ANY, pltpu.VMEM],
    )
    corr_near = swap(join(corr_side, corr_far, after=[mark, lag_blocks[0]]), 1)
    k_grad, v_grad, filter_grad = call(
        finish_corr,
        [whole, whole, struct(own_taps, channels, f32)],
        [place, corr_own, corr_near, corr_far, values, keys, lag_blocks[0]]
        + [lag_got[step] for step in range(1, PLANE)],
        scratch=[
            pltpu.VMEM((2, PLANE, rows, width), bf16),
            pltpu.VMEM((own_taps, channels), f32),
            pltpu.SemaphoreType.DMA((2, PLANE)),
            pltpu.SemaphoreType.DMA,
        ],
        spaces=[pl.ANY] * 3,
    )
    return (q_grad, k_grad, v_grad, filter_grad)


def solution(mesh):
    placed = (
        P(("grp", "seq"), None),
        P(("grp", "seq"), None),
        P(("grp", "seq"), None),
        P(("grp", "seq"), None),
        P("seq", None),
    )
    return jax.shard_map(
        shards,
        mesh=mesh,
        in_specs=placed,
        out_specs=(
            P(("grp", "seq"), None),
            P(("grp", "seq"), None),
            P(("grp", "seq"), None),
            P(("grp", "seq"), None),
        ),
        check_vma=False,
    )
```

profile of v0, /device:TPU:0, one launch (start us, length us, event | category | flops | bytes accessed | tf_op | source)
XLA Modules:
  0.0 56.2 jit_solution(15445418262786688557)
XLA Ops:
  0.7 0.1 pad_add_fusion.refs_0_
  0.7 1.5 %multiply_convert_fusion = (bf16[128,512]{1,0:T(8,128)(2,1)S(1)}, bf16[128,512]{1,0:T(8,128)(2,1)S(1)}, bf16[128,512]{1,0:T(8,128)(2,1)S(1)}, bf16[128,512]{1,0:T(8,128)(2,1)S(1)}) fusion(bf16[128,2048]{1,0:T(8,128)(2,1)} %refs_4_.5, s32[]{:T(128)S(6)} %select_n.32, bf16[128,2048]{1,0:T(8,128)(2,1)} %refs_5_.2, s32[]{:T(128)S(6)} %select_n.31, ...), kind=kLoop, calls=%fused_computation | loop fusion | flops 1048576 | bytes 1572880 | tf_op jit(solution)/shard_map/convert_element_type | solution.py:285
  2.3 0.1 copy-done.7
  2.4 0.7 %shard_map.138 = (bf16[256,512]{1,0:T(8,128)(2,1)S(1)}, bf16[384,512]{1,0:T(8,128)(2,1)S(1)}) custom-call(s32[2]{0:T(128)S(1)} %pad_add_fusion.refs_0_, bf16[128,2048]{1,0:T(8,128)(2,1)S(1)} %copy-done.2, bf16[128,2048]{1,0:T(8,128)(2,1)S(1)} %copy-done.7, bf16[128,512]{1,0:T(8,128)(2,1)S(1)} %get-tuple-element.72.refs_3_), custom_call_target="tpu_custom_call" | custom-call | flops 1 | bytes 1 | tf_op jit(solution)/shard_map/pallas_call | solution.py:81
  3.0 0.5 collective-permute-start
  3.6 2.6 %collective-permute-start.1 = (bf16[128,512]{1,0:T(8,128)(2,1)S(1)}, bf16[128,512]{1,0:T(8,128)(2,1)S(1)}, u32[]{:S(2)}, u32[]{:S(2)}) collective-permute-start(bf16[128,512]{1,0:T(8,128)(2,1)S(1)} %get-tuple-element.71), channel_id=1, source_target_pairs={{0,2},{1,3},{2,0},{3,1},{4,6},{5,7},{6,4},{7,5},{8,10},{9,11},{10,... | collective-permute-start | bytes 393224 | tf_op jit(solution)/shard_map/ppermute | solution.py:118
  6.1 0.1 collective-permute-start.2
  6.2 1.8 %collective-permute-start.10 = (bf16[256,512]{1,0:T(8,128)(2,1)S(1)}, bf16[256,512]{1,0:T(8,128)(2,1)S(1)}, u32[]{:S(2)}, u32[]{:S(2)}) collective-permute-start(bf16[256,512]{1,0:T(8,128)(2,1)S(1)} %shard_map.145), channel_id=1, source_target_pairs={{0,2},{1,3},{2,0},{3,1},{4,6},{5,7},{6,4},{7,5},{8,10},{9,11},{10,... | collective-permute-start | bytes 786440 | tf_op jit(solution)/shard_map/ppermute | solution.py:118
  8.0 1.6 %collective-permute-start.4 = (bf16[16,2048]{1,0:T(8,128)(2,1)S(1)}, bf16[16,2048]{1,0:T(8,128)(2,1)S(1)}, u32[]{:S(2)}, u32[]{:S(2)}) collective-permute-start(bf16[16,2048]{1,0:T(8,128)(2,1)S(1)} %shard_map.141.refs_1_), channel_id=1, source_target_pairs={{0,4},{1,5},{2,6},{3,7},{4,0},{5,1},{6,2},{7,3},{8,12},{9,13},{10,... | collective-permute-start | bytes 196616 | tf_op jit(solution)/shard_map/ppermute | solution.py:118
  9.7 2.6 %collective-permute-start.5 = (bf16[16,2048]{1,0:T(8,128)(2,1)S(1)}, bf16[16,2048]{1,0:T(8,128)(2,1)S(1)}, u32[]{:S(2)}, u32[]{:S(2)}) collective-permute-start(bf16[16,2048]{1,0:T(8,128)(2,1)S(1)} %shard_map.141.refs_1_), channel_id=1, source_target_pairs={{0,8},{1,9},{2,10},{3,11},{4,12},{5,13},{6,14},{7,15},{8,0},{9,1},... | collective-permute-start | bytes 196616 | tf_op jit(solution)/shard_map/ppermute | solution.py:118
  12.3 2.3 %collective-permute-start.6 = (bf16[16,2048]{1,0:T(8,128)(2,1)S(1)}, bf16[16,2048]{1,0:T(8,128)(2,1)S(1)}, u32[]{:S(2)}, u32[]{:S(2)}) collective-permute-start(bf16[16,2048]{1,0:T(8,128)(2,1)S(1)} %shard_map.141.refs_1_), channel_id=1, source_target_pairs={{0,12},{1,13},{2,14},{3,15},{4,8},{5,9},{6,10},{7,11},{8,4},{9,5},... | collective-permute-start | bytes 196616 | tf_op jit(solution)/shard_map/ppermute | solution.py:118
  14.5 2.6 %collective-permute-done.5.refs_3_ = bf16[16,2048]{1,0:T(8,128)(2,1)S(1)} collective-permute-done((bf16[16,2048]{1,0:T(8,128)(2,1)S(1)}, bf16[16,2048]{1,0:T(8,128)(2,1)S(1)}, u32[]{:S(2)}, u32[]{:S(2)}) %collective-permute-start.5) | collective-permute-done | bytes 65568 | tf_op jit(solution)/shard_map/ppermute | solution.py:118
  17.2 1.3 %collective-permute-done.6.refs_4_ = bf16[16,2048]{1,0:T(8,128)(2,1)S(1)} collective-permute-done((bf16[16,2048]{1,0:T(8,128)(2,1)S(1)}, bf16[16,2048]{1,0:T(8,128)(2,1)S(1)}, u32[]{:S(2)}, u32[]{:S(2)}) %collective-permute-start.6) | collective-permute-done | bytes 65568 | tf_op jit(solution)/shard_map/ppermute | solution.py:118
  18.4 0.6 %shard_map.142 = (bf16[128,512]{1,0:T(8,128)(2,1)S(1)}, bf16[128,512]{1,0:T(8,128)(2,1)S(1)}) custom-call(s32[2]{0:T(128)S(1)} %pad_add_fusion.refs_0_, bf16[16,2048]{1,0:T(8,128)(2,1)S(1)} %shard_map.141.refs_1_, bf16[16,2048]{1,0:T(8,128)(2,1)S(1)} %collective-permute-done.4.refs_2_, bf16[16,2048]{1,0:T(8,128)(2,1)S(1)} %collective-permute-done.5.refs_3_, ...), custom_call_target="tpu_custom_call" | custom-call | flops 1 | bytes 1 | tf_op jit(solution)/shard_map/pallas_call | solution.py:81
  19.0 0.1 collective-permute-start.7
  19.1 0.6 %shard_map.139 = (bf16[512,512]{1,0:T(8,128)(2,1)S(1)}, bf16[256,512]{1,0:T(8,128)(2,1)S(1)}) custom-call(s32[2]{0:T(128)S(1)} %pad_add_fusion.refs_0_, bf16[128,512]{1,0:T(8,128)(2,1)S(1)} %get-tuple-element.73.refs_1_, bf16[384,512]{1,0:T(8,128)(2,1)S(1)} %collective-permute-done.refs_2_.refs_1_, ...), custom_call_target="tpu_custom_call" | custom-call | flops 1 | bytes 1 | tf_op jit(solution)/shard_map/pallas_call | solution.py:81
  19.7 2.7 %collective-permute-start.3 = (bf16[256,512]{1,0:T(8,128)(2,1)S(1)}, bf16[256,512]{1,0:T(8,128)(2,1)S(1)}, u32[]{:S(2)}, u32[]{:S(2)}) collective-permute-start(bf16[256,512]{1,0:T(8,128)(2,1)S(1)} %get-tuple-element.41), channel_id=1, source_target_pairs={{0,4},{1,5},{2,6},{3,7},{4,8},{5,9},{6,10},{7,11},{8,12},{9,13},{1... | collective-permute-start | bytes 786440 | tf_op jit(solution)/shard_map/ppermute | solution.py:121
  22.4 0.0 copy-start
  22.4 0.0 copy-start.1
  22.4 0.6 %shard_map.146 = (bf16[512,512]{1,0:T(8,128)(2,1)S(1)}, bf16[256,512]{1,0:T(8,128)(2,1)S(1)}) custom-call(s32[2]{0:T(128)S(1)} %pad_add_fusion.refs_0_, bf16[256,512]{1,0:T(8,128)(2,1)S(1)} %get-tuple-element.47.refs_0_.refs_1_, bf16[384,512]{1,0:T(8,128)(2,1)S(1)} %collective-permute-done.refs_2_.refs_1_, ...), custom_call_target="tpu_custom_call" | custom-call | flops 1 | bytes 1 | tf_op jit(solution)/shard_map/pallas_call | solution.py:81
  23.1 1.3 %collective-permute-start.11 = (bf16[256,512]{1,0:T(8,128)(2,1)S(1)}, bf16[256,512]{1,0:T(8,128)(2,1)S(1)}, u32[]{:S(2)}, u32[]{:S(2)}) collective-permute-start(bf16[256,512]{1,0:T(8,128)(2,1)S(1)} %get-tuple-element.51), channel_id=1, source_target_pairs={{4,0},{5,1},{6,2},{7,3},{8,4},{9,5},{10,6},{11,7},{12,8},{13,9},{1... | collective-permute-start | bytes 786440 | tf_op jit(solution)/shard_map/ppermute | solution.py:121
  24.4 1.2 %collective-permute-start.8 = (bf16[128,512]{1,0:T(8,128)(2,1)S(1)}, bf16[128,512]{1,0:T(8,128)(2,1)S(1)}, u32[]{:S(2)}, u32[]{:S(2)}) collective-permute-start(bf16[128,512]{1,0:T(8,128)(2,1)S(1)} %shard_map.143.refs_4_), channel_id=1, source_target_pairs={{0,2},{1,3},{2,0},{3,1},{4,6},{5,7},{6,4},{7,5},{8,10},{9,11},{10,... | collective-permute-start | bytes 393224 | tf_op jit(solution)/shard_map/ppermute | solution.py:118
  25.5 0.7 %shard_map.140 = (f32[512,512]{1,0:T(8,128)S(1)}, f32[512,512]{1,0:T(8,128)S(1)}) custom-call(bf16[512,256]{1,0:T(8,128)(2,1)S(1)} %copy-done, bf16[512,256]{1,0:T(8,128)(2,1)S(1)} %copy-done.1, bf16[512,512]{1,0:T(8,128)(2,1)S(1)} %get-tuple-element.38.refs_2_), custom_call_target="tpu_custom_call" | custom-call | flops 1 | bytes 1 | tf_op jit(solution)/shard_map/pallas_call | solution.py:81
  26.3 0.0 copy-start.5
  26.3 0.7 %shard_map.147 = (f32[512,512]{1,0:T(8,128)S(1)}, f32[512,512]{1,0:T(8,128)S(1)}) custom-call(bf16[512,256]{1,0:T(8,128)(2,1)S(1)} %copy-done, bf16[512,256]{1,0:T(8,128)(2,1)S(1)} %copy-done.1, bf16[512,512]{1,0:T(8,128)(2,1)S(1)} %get-tuple-element.48.refs_2_), custom_call_target="tpu_custom_call" | custom-call | flops 1 | bytes 1 | tf_op jit(solution)/shard_map/pallas_call | solution.py:81
  27.0 1.6 %collective-permute-done.3.refs_9_ = bf16[256,512]{1,0:T(8,128)(2,1)S(1)} collective-permute-done((bf16[256,512]{1,0:T(8,128)(2,1)S(1)}, bf16[256,512]{1,0:T(8,128)(2,1)S(1)}, u32[]{:S(2)}, u32[]{:S(2)}) %collective-permute-start.3) | collective-permute-done | bytes 262176 | tf_op jit(solution)/shard_map/ppermute | solution.py:121
  28.6 1.5 %collective-permute-done.8.refs_12_ = bf16[128,512]{1,0:T(8,128)(2,1)S(1)} collective-permute-done((bf16[128,512]{1,0:T(8,128)(2,1)S(1)}, bf16[128,512]{1,0:T(8,128)(2,1)S(1)}, u32[]{:S(2)}, u32[]{:S(2)}) %collective-permute-start.8) | collective-permute-done | bytes 131104 | tf_op jit(solution)/shard_map/ppermute | solution.py:118
  30.1 2.7 %shard_map.144 = (f32[512,512]{1,0:T(8,128)S(1)}, f32[512,512]{1,0:T(8,128)S(1)}, bf16[128,512]{1,0:T(8,128)(2,1)S(1)}, bf16[128,512]{1,0:T(8,128)(2,1)S(1)}, bf16[256,512]{1,0:T(8,128)(2,1)S(1)}) custom-call(s32[2]{0:T(128)S(1)} %pad_add_fusion.refs_0_, bf16[512,256]{1,0:T(8,128)(2,1)S(1)} %copy-done, bf16[512,256]{1,0:T(8,128)(2,1)S(1)} %copy-done.1, ...), custom_call_target="tpu_custom_call" | custom-call | flops 1 | bytes 1 | tf_op jit(solution)/shard_map/pallas_call | solution.py:81
  32.7 1.2 %collective-permute-start.9 = (bf16[256,512]{1,0:T(8,128)(2,1)S(1)}, bf16[256,512]{1,0:T(8,128)(2,1)S(1)}, u32[]{:S(2)}, u32[]{:S(2)}) collective-permute-start(bf16[256,512]{1,0:T(8,128)(2,1)S(1)} %get-tuple-element.46), channel_id=1, source_target_pairs={{0,2},{1,3},{2,0},{3,1},{4,6},{5,7},{6,4},{7,5},{8,10},{9,11},{10,... | collective-permute-start | bytes 786440 | tf_op jit(solution)/shard_map/ppermute | solution.py:118
  33.9 1.7 %shard_map.151 = (f32[64,512]{1,0:T(8,128)S(1)}, bf16[64,512]{1,0:T(8,128)(2,1)S(1)}, bf16[64,512]{1,0:T(8,128)(2,1)S(1)}, bf16[64,512]{1,0:T(8,128)(2,1)S(1)}) custom-call(s32[2]{0:T(128)S(1)} %pad_add_fusion.refs_0_, bf16[256,512]{1,0:T(8,128)(2,1)S(1)} %copy-done.5, bf16[256,512]{1,0:T(8,128)(2,1)S(1)} %copy-done.6, ...), custom_call_target="tpu_custom_call" | custom-call | flops 1 | bytes 1 | tf_op jit(solution)/shard_map/pallas_call | solution.py:81
  35.7 2.4 %collective-permute-start.14 = (bf16[64,512]{1,0:T(8,128)(2,1)S(1)}, bf16[64,512]{1,0:T(8,128)(2,1)S(1)}, u32[]{:S(2)}, u32[]{:S(2)}) collective-permute-start(bf16[64,512]{1,0:T(8,128)(2,1)S(1)} %get-tuple-element.60), channel_id=1, source_target_pairs={{0,4},{1,5},{2,6},{3,7},{4,0},{5,1},{6,2},{7,3},{8,12},{9,13},{10,... | collective-permute-start | bytes 196616 | tf_op jit(solution)/shard_map/ppermute | solution.py:118
  38.1 2.4 %collective-permute-start.15 = (bf16[64,512]{1,0:T(8,128)(2,1)S(1)}, bf16[64,512]{1,0:T(8,128)(2,1)S(1)}, u32[]{:S(2)}, u32[]{:S(2)}) collective-permute-start(bf16[64,512]{1,0:T(8,128)(2,1)S(1)} %get-tuple-element.61), channel_id=1, source_target_pairs={{0,8},{1,9},{2,10},{3,11},{4,12},{5,13},{6,14},{7,15},{8,0},{9,1},... | collective-permute-start | bytes 196616 | tf_op jit(solution)/shard_map/ppermute | solution.py:118
  40.5 0.1 collective-permute-start.16
  40.7 2.2 %shard_map.148 = (bf16[128,512]{1,0:T(8,128)(2,1)S(1)}, bf16[128,512]{1,0:T(8,128)(2,1)S(1)}, bf16[256,512]{1,0:T(8,128)(2,1)S(1)}) custom-call(s32[2]{0:T(128)S(1)} %pad_add_fusion.refs_0_, bf16[512,256]{1,0:T(8,128)(2,1)S(1)} %copy-done, bf16[512,256]{1,0:T(8,128)(2,1)S(1)} %copy-done.1, bf16[256,512]{1,0:T(8,128)(2,1)S(1)} %copy-done.5, ...), custom_call_target="tpu_custom_call" | custom-call | flops 10000000000 | bytes 1 | tf_op jit(solution)/shard_map/pallas_call | solution.py:81
  42.9 0.9 %collective-permute-start.13 = (bf16[256,512]{1,0:T(8,128)(2,1)S(1)}, bf16[256,512]{1,0:T(8,128)(2,1)S(1)}, u32[]{:S(2)}, u32[]{:S(2)}) collective-permute-start(bf16[256,512]{1,0:T(8,128)(2,1)S(1)} %get-tuple-element.56), channel_id=1, source_target_pairs={{0,2},{1,3},{2,0},{3,1},{4,6},{5,7},{6,4},{7,5},{8,10},{9,11},{10,... | collective-permute-start | bytes 786440 | tf_op jit(solution)/shard_map/ppermute | solution.py:118
  43.8 0.1 collective-permute-start.12
  43.9 0.7 %collective-permute-done.15.refs_3_ = bf16[64,512]{1,0:T(8,128)(2,1)S(1)} collective-permute-done((bf16[64,512]{1,0:T(8,128)(2,1)S(1)}, bf16[64,512]{1,0:T(8,128)(2,1)S(1)}, u32[]{:S(2)}, u32[]{:S(2)}) %collective-permute-start.15) | collective-permute-done | bytes 65568 | tf_op jit(solution)/shard_map/ppermute | solution.py:118
  44.7 1.9 %collective-permute-done.16.refs_4_ = bf16[64,512]{1,0:T(8,128)(2,1)S(1)} collective-permute-done((bf16[64,512]{1,0:T(8,128)(2,1)S(1)}, bf16[64,512]{1,0:T(8,128)(2,1)S(1)}, u32[]{:S(2)}, u32[]{:S(2)}) %collective-permute-start.16) | collective-permute-done | bytes 65568 | tf_op jit(solution)/shard_map/ppermute | solution.py:118
  46.6 0.6 %shard_map.152 = (f32[16,512]{1,0:T(8,128)S(1)}, f32[16,512]{1,0:T(8,128)S(1)}, f32[16,512]{1,0:T(8,128)S(1)}, f32[16,512]{1,0:T(8,128)S(1)}) custom-call(s32[2]{0:T(128)S(1)} %pad_add_fusion.refs_0_, f32[64,512]{1,0:T(8,128)S(1)} %get-tuple-element.59.refs_1_, bf16[64,512]{1,0:T(8,128)(2,1)S(1)} %collective-permute-done.14.refs_2_, ...), custom_call_target="tpu_custom_call" | custom-call | flops 10000000000 | bytes 1 | tf_op jit(solution)/shard_map/pallas_call | solution.py:81
  47.2 1.4 %shard_map.150 = (bf16[128,2048]{1,0:T(8,128)(2,1)}, f32[8,128]{1,0:T(8,128)S(1)}) custom-call(s32[2]{0:T(128)S(1)} %pad_add_fusion.refs_0_, bf16[128,512]{1,0:T(8,128)(2,1)S(1)} %get-tuple-element.44.refs_1_, bf16[256,512]{1,0:T(8,128)(2,1)S(1)} %collective-permute-done.12.refs_2_, bf16[256,512]{1,0:T(8,128)(2,1)S(1)} %collective-permute-done.9.refs_1_.refs_3_, ...), custom_call_target="tpu_custom_call" | custom-call | flops 1 | bytes 1 | tf_op jit(solution)/shard_map/pallas_call | solution.py:81
  48.6 0.8 %collective-permute-done.13.refs_1_.refs_3_ = bf16[256,512]{1,0:T(8,128)(2,1)S(1)} collective-permute-done((bf16[256,512]{1,0:T(8,128)(2,1)S(1)}, bf16[256,512]{1,0:T(8,128)(2,1)S(1)}, u32[]{:S(2)}, u32[]{:S(2)}) %collective-permute-start.13) | collective-permute-done | bytes 262176 | tf_op jit(solution)/shard_map/ppermute | solution.py:118
  49.5 0.1 collective-permute-start.17
  49.5 0.5 collective-permute-start.18
  50.0 0.8 %collective-permute-start.19 = (f32[16,512]{1,0:T(8,128)S(1)}, f32[16,512]{1,0:T(8,128)S(1)}, u32[]{:S(2)}, u32[]{:S(2)}) collective-permute-start(f32[16,512]{1,0:T(8,128)S(1)} %get-tuple-element.65), channel_id=1, source_target_pairs={{0,2},{1,3},{2,0},{3,1},{4,6},{5,7},{6,4},{7,5},{8,10},{9,11},{10,... | collective-permute-start | bytes 98312 | tf_op jit(solution)/shard_map/ppermute | solution.py:118
  50.9 0.6 %collective-permute-start.20 = (f32[16,512]{1,0:T(8,128)S(1)}, f32[16,512]{1,0:T(8,128)S(1)}, u32[]{:S(2)}, u32[]{:S(2)}) collective-permute-start(f32[16,512]{1,0:T(8,128)S(1)} %get-tuple-element.66), channel_id=1, source_target_pairs={{0,3},{1,2},{2,1},{3,0},{4,7},{5,6},{6,5},{7,4},{8,11},{9,10},{10,... | collective-permute-start | bytes 98312 | tf_op jit(solution)/shard_map/ppermute | solution.py:118
  51.5 2.6 %collective-permute-done.19.refs_8_ = f32[16,512]{1,0:T(8,128)S(1)} collective-permute-done((f32[16,512]{1,0:T(8,128)S(1)}, f32[16,512]{1,0:T(8,128)S(1)}, u32[]{:S(2)}, u32[]{:S(2)}) %collective-permute-start.19) | collective-permute-done | bytes 32800 | tf_op jit(solution)/shard_map/ppermute | solution.py:118
  54.0 0.5 collective-permute-done.20.refs_9_
  54.6 1.7 %shard_map.154 = (bf16[128,2048]{1,0:T(8,128)(2,1)}, bf16[128,2048]{1,0:T(8,128)(2,1)}, f32[16,2048]{1,0:T(8,128)}) custom-call(s32[2]{0:T(128)S(1)} %pad_add_fusion.refs_0_, bf16[128,512]{1,0:T(8,128)(2,1)S(1)} %get-tuple-element.53.refs_2_.refs_5_.refs_1_, bf16[256,512]{1,0:T(8,128)(2,1)S(1)} %collective-permute-done.17.refs_2_, ...), custom_call_target="tpu_custom_call" | custom-call | flops 1 | bytes 1 | tf_op jit(solution)/shard_map/pallas_call | solution.py:81
  (35 shorter events, 0.2 us)
Async XLA Ops:
  0.7 1.5 %copy-start.2 = (bf16[128,2048]{1,0:T(8,128)(2,1)S(1)}, bf16[128,2048]{1,0:T(8,128)(2,1)}, u32[]{:S(2)}) copy-start(bf16[128,2048]{1,0:T(8,128)(2,1)} %refs_4_.4) | copy-start | bytes 1572868
  0.7 1.6 %copy-start.7 = (bf16[128,2048]{1,0:T(8,128)(2,1)S(1)}, bf16[128,2048]{1,0:T(8,128)(2,1)}, u32[]{:S(2)}) copy-start(bf16[128,2048]{1,0:T(8,128)(2,1)} %refs_2_.4) | copy-start | bytes 1572868
  3.0 3.2 %collective-permute-start = (bf16[384,512]{1,0:T(8,128)(2,1)S(1)}, bf16[384,512]{1,0:T(8,128)(2,1)S(1)}, u32[]{:S(2)}, u32[]{:S(2)}) collective-permute-start(bf16[384,512]{1,0:T(8,128)(2,1)S(1)} %get-tuple-element.37), channel_id=1, source_target_pairs={{0,1},{1,0},{2,3},{3,2},{4,5},{5,4},{6,7},{7,6},{8,9},{9,8},{10,11... | collective-permute-start | bytes 1179656 | tf_op jit(solution)/shard_map/ppermute | solution.py:118
  3.6 8.7 %collective-permute-start.1 = (bf16[128,512]{1,0:T(8,128)(2,1)S(1)}, bf16[128,512]{1,0:T(8,128)(2,1)S(1)}, u32[]{:S(2)}, u32[]{:S(2)}) collective-permute-start(bf16[128,512]{1,0:T(8,128)(2,1)S(1)} %get-tuple-element.71), channel_id=1, source_target_pairs={{0,2},{1,3},{2,0},{3,1},{4,6},{5,7},{6,4},{7,5},{8,10},{9,11},{10,... | collective-permute-start | bytes 393224 | tf_op jit(solution)/shard_map/ppermute | solution.py:118
  6.1 8.4 %collective-permute-start.2 = (bf16[128,512]{1,0:T(8,128)(2,1)S(1)}, bf16[128,512]{1,0:T(8,128)(2,1)S(1)}, u32[]{:S(2)}, u32[]{:S(2)}) collective-permute-start(bf16[128,512]{1,0:T(8,128)(2,1)S(1)} %get-tuple-element.70), channel_id=1, source_target_pairs={{0,3},{1,2},{2,1},{3,0},{4,7},{5,6},{6,5},{7,4},{8,11},{9,10},{10,... | collective-permute-start | bytes 393224 | tf_op jit(solution)/shard_map/ppermute | solution.py:118
  6.2 1.8 %copy-start.10 = (f32[16,2048]{1,0:T(8,128)S(1)}, f32[16,2048]{1,0:T(8,128)}, u32[]{:S(2)}) copy-start(f32[16,2048]{1,0:T(8,128)} %refs_0_.3) | copy-start | bytes 393220
  6.2 16.2 %collective-permute-start.10 = (bf16[256,512]{1,0:T(8,128)(2,1)S(1)}, bf16[256,512]{1,0:T(8,128)(2,1)S(1)}, u32[]{:S(2)}, u32[]{:S(2)}) collective-permute-start(bf16[256,512]{1,0:T(8,128)(2,1)S(1)} %shard_map.145), channel_id=1, source_target_pairs={{0,2},{1,3},{2,0},{3,1},{4,6},{5,7},{6,4},{7,5},{8,10},{9,11},{10,... | collective-permute-start | bytes 786440 | tf_op jit(solution)/shard_map/ppermute | solution.py:118
  8.0 6.5 %collective-permute-start.4 = (bf16[16,2048]{1,0:T(8,128)(2,1)S(1)}, bf16[16,2048]{1,0:T(8,128)(2,1)S(1)}, u32[]{:S(2)}, u32[]{:S(2)}) collective-permute-start(bf16[16,2048]{1,0:T(8,128)(2,1)S(1)} %shard_map.141.refs_1_), channel_id=1, source_target_pairs={{0,4},{1,5},{2,6},{3,7},{4,0},{5,1},{6,2},{7,3},{8,12},{9,13},{10,... | collective-permute-start | bytes 196616 | tf_op jit(solution)/shard_map/ppermute | solution.py:118
  9.7 7.5 %collective-permute-start.5 = (bf16[16,2048]{1,0:T(8,128)(2,1)S(1)}, bf16[16,2048]{1,0:T(8,128)(2,1)S(1)}, u32[]{:S(2)}, u32[]{:S(2)}) collective-permute-start(bf16[16,2048]{1,0:T(8,128)(2,1)S(1)} %shard_map.141.refs_1_), channel_id=1, source_target_pairs={{0,8},{1,9},{2,10},{3,11},{4,12},{5,13},{6,14},{7,15},{8,0},{9,1},... | collective-permute-start | bytes 196616 | tf_op jit(solution)/shard_map/ppermute | solution.py:118
  12.3 6.2 %collective-permute-start.6 = (bf16[16,2048]{1,0:T(8,128)(2,1)S(1)}, bf16[16,2048]{1,0:T(8,128)(2,1)S(1)}, u32[]{:S(2)}, u32[]{:S(2)}) collective-permute-start(bf16[16,2048]{1,0:T(8,128)(2,1)S(1)} %shard_map.141.refs_1_), channel_id=1, source_target_pairs={{0,12},{1,13},{2,14},{3,15},{4,8},{5,9},{6,10},{7,11},{8,4},{9,5},... | collective-permute-start | bytes 196616 | tf_op jit(solution)/shard_map/ppermute | solution.py:118
  19.0 3.4 %collective-permute-start.7 = (bf16[128,512]{1,0:T(8,128)(2,1)S(1)}, bf16[128,512]{1,0:T(8,128)(2,1)S(1)}, u32[]{:S(2)}, u32[]{:S(2)}) collective-permute-start(bf16[128,512]{1,0:T(8,128)(2,1)S(1)} %get-tuple-element.43), channel_id=1, source_target_pairs={{0,1},{1,0},{2,3},{3,2},{4,5},{5,4},{6,7},{7,6},{8,9},{9,8},{10,11... | collective-permute-start | bytes 393224 | tf_op jit(solution)/shard_map/ppermute | solution.py:118
  19.7 8.9 %collective-permute-start.3 = (bf16[256,512]{1,0:T(8,128)(2,1)S(1)}, bf16[256,512]{1,0:T(8,128)(2,1)S(1)}, u32[]{:S(2)}, u32[]{:S(2)}) collective-permute-start(bf16[256,512]{1,0:T(8,128)(2,1)S(1)} %get-tuple-element.41), channel_id=1, source_target_pairs={{0,4},{1,5},{2,6},{3,7},{4,8},{5,9},{6,10},{7,11},{8,12},{9,13},{1... | collective-permute-start | bytes 786440 | tf_op jit(solution)/shard_map/ppermute | solution.py:121
  22.4 3.1 %copy-start = (bf16[512,256]{1,0:T(8,128)(2,1)S(1)}, bf16[512,256]{1,0:T(8,128)(2,1)}, u32[]{:S(2)}) copy-start(bf16[512,256]{1,0:T(8,128)(2,1)} %constant.50.clone.refs_0_.refs_1_) | copy-start | bytes 786436
  22.4 3.1 %copy-start.1 = (bf16[512,256]{1,0:T(8,128)(2,1)S(1)}, bf16[512,256]{1,0:T(8,128)(2,1)}, u32[]{:S(2)}) copy-start(bf16[512,256]{1,0:T(8,128)(2,1)} %constant.51.clone.refs_1_.refs_2_) | copy-start | bytes 786436
  23.1 17.6 %collective-permute-start.11 = (bf16[256,512]{1,0:T(8,128)(2,1)S(1)}, bf16[256,512]{1,0:T(8,128)(2,1)S(1)}, u32[]{:S(2)}, u32[]{:S(2)}) collective-permute-start(bf16[256,512]{1,0:T(8,128)(2,1)S(1)} %get-tuple-element.51), channel_id=1, source_target_pairs={{4,0},{5,1},{6,2},{7,3},{8,4},{9,5},{10,6},{11,7},{12,8},{13,9},{1... | collective-permute-start | bytes 786440 | tf_op jit(solution)/shard_map/ppermute | solution.py:121
  24.4 5.7 %collective-permute-start.8 = (bf16[128,512]{1,0:T(8,128)(2,1)S(1)}, bf16[128,512]{1,0:T(8,128)(2,1)S(1)}, u32[]{:S(2)}, u32[]{:S(2)}) collective-permute-start(bf16[128,512]{1,0:T(8,128)(2,1)S(1)} %shard_map.143.refs_4_), channel_id=1, source_target_pairs={{0,2},{1,3},{2,0},{3,1},{4,6},{5,7},{6,4},{7,5},{8,10},{9,11},{10,... | collective-permute-start | bytes 393224 | tf_op jit(solution)/shard_map/ppermute | solution.py:118
  26.3 3.8 %copy-start.5 = (bf16[256,512]{1,0:T(8,128)(2,1)S(1)}, bf16[256,512]{1,0:T(8,128)(2,1)}, u32[]{:S(2)}) copy-start(bf16[256,512]{1,0:T(8,128)(2,1)} %constant.52.clone.refs_5_.refs_3_.refs_1_) | copy-start | bytes 786436
  26.3 3.8 %copy-start.6 = (bf16[256,512]{1,0:T(8,128)(2,1)S(1)}, bf16[256,512]{1,0:T(8,128)(2,1)}, u32[]{:S(2)}) copy-start(bf16[256,512]{1,0:T(8,128)(2,1)} %constant.53.clone.refs_6_.refs_4_.refs_2_) | copy-start | bytes 786436
  26.3 3.8 %copy-start.8 = (bf16[512,256]{1,0:T(8,128)(2,1)S(1)}, bf16[512,256]{1,0:T(8,128)(2,1)}, u32[]{:S(2)}) copy-start(bf16[512,256]{1,0:T(8,128)(2,1)} %constant.54.clone.refs_3_) | copy-start | bytes 786436
  26.3 3.8 %copy-start.9 = (bf16[512,256]{1,0:T(8,128)(2,1)S(1)}, bf16[512,256]{1,0:T(8,128)(2,1)}, u32[]{:S(2)}) copy-start(bf16[512,256]{1,0:T(8,128)(2,1)} %constant.55.clone.refs_4_) | copy-start | bytes 786436
  32.7 11.1 %collective-permute-start.9 = (bf16[256,512]{1,0:T(8,128)(2,1)S(1)}, bf16[256,512]{1,0:T(8,128)(2,1)S(1)}, u32[]{:S(2)}, u32[]{:S(2)}) collective-permute-start(bf16[256,512]{1,0:T(8,128)(2,1)S(1)} %get-tuple-element.46), channel_id=1, source_target_pairs={{0,2},{1,3},{2,0},{3,1},{4,6},{5,7},{6,4},{7,5},{8,10},{9,11},{10,... | collective-permute-start | bytes 786440 | tf_op jit(solution)/shard_map/ppermute | solution.py:118
  35.7 8.3 %collective-permute-start.14 = (bf16[64,512]{1,0:T(8,128)(2,1)S(1)}, bf16[64,512]{1,0:T(8,128)(2,1)S(1)}, u32[]{:S(2)}, u32[]{:S(2)}) collective-permute-start(bf16[64,512]{1,0:T(8,128)(2,1)S(1)} %get-tuple-element.60), channel_id=1, source_target_pairs={{0,4},{1,5},{2,6},{3,7},{4,0},{5,1},{6,2},{7,3},{8,12},{9,13},{10,... | collective-permute-start | bytes 196616 | tf_op jit(solution)/shard_map/ppermute | solution.py:118
  38.1 6.6 %collective-permute-start.15 = (bf16[64,512]{1,0:T(8,128)(2,1)S(1)}, bf16[64,512]{1,0:T(8,128)(2,1)S(1)}, u32[]{:S(2)}, u32[]{:S(2)}) collective-permute-start(bf16[64,512]{1,0:T(8,128)(2,1)S(1)} %get-tuple-element.61), channel_id=1, source_target_pairs={{0,8},{1,9},{2,10},{3,11},{4,12},{5,13},{6,14},{7,15},{8,0},{9,1},... | collective-permute-start | bytes 196616 | tf_op jit(solution)/shard_map/ppermute | solution.py:118
  40.5 6.1 %collective-permute-start.16 = (bf16[64,512]{1,0:T(8,128)(2,1)S(1)}, bf16[64,512]{1,0:T(8,128)(2,1)S(1)}, u32[]{:S(2)}, u32[]{:S(2)}) collective-permute-start(bf16[64,512]{1,0:T(8,128)(2,1)S(1)} %get-tuple-element.62), channel_id=1, source_target_pairs={{0,12},{1,13},{2,14},{3,15},{4,8},{5,9},{6,10},{7,11},{8,4},{9,5},... | collective-permute-start | bytes 196616 | tf_op jit(solution)/shard_map/ppermute | solution.py:118
  42.9 6.5 %collective-permute-start.13 = (bf16[256,512]{1,0:T(8,128)(2,1)S(1)}, bf16[256,512]{1,0:T(8,128)(2,1)S(1)}, u32[]{:S(2)}, u32[]{:S(2)}) collective-permute-start(bf16[256,512]{1,0:T(8,128)(2,1)S(1)} %get-tuple-element.56), channel_id=1, source_target_pairs={{0,2},{1,3},{2,0},{3,1},{4,6},{5,7},{6,4},{7,5},{8,10},{9,11},{10,... | collective-permute-start | bytes 786440 | tf_op jit(solution)/shard_map/ppermute | solution.py:118
  43.8 3.4 %collective-permute-start.12 = (bf16[256,512]{1,0:T(8,128)(2,1)S(1)}, bf16[256,512]{1,0:T(8,128)(2,1)S(1)}, u32[]{:S(2)}, u32[]{:S(2)}) collective-permute-start(bf16[256,512]{1,0:T(8,128)(2,1)S(1)} %shard_map.149), channel_id=1, source_target_pairs={{0,1},{1,0},{2,3},{3,2},{4,5},{5,4},{6,7},{7,6},{8,9},{9,8},{10,11... | collective-permute-start | bytes 786440 | tf_op jit(solution)/shard_map/ppermute | solution.py:118
  47.2 7.3 %copy-start.4 = (bf16[128,2048]{1,0:T(8,128)(2,1)S(1)}, bf16[128,2048]{1,0:T(8,128)(2,1)}, u32[]{:S(2)}) copy-start(bf16[128,2048]{1,0:T(8,128)(2,1)} %refs_5_.2) | copy-start | bytes 1572868
  48.6 5.9 %copy-start.3 = (bf16[128,2048]{1,0:T(8,128)(2,1)S(1)}, bf16[128,2048]{1,0:T(8,128)(2,1)}, u32[]{:S(2)}) copy-start(bf16[128,2048]{1,0:T(8,128)(2,1)} %refs_4_.5) | copy-start | bytes 1572868
  49.5 5.1 %collective-permute-start.17 = (bf16[256,512]{1,0:T(8,128)(2,1)S(1)}, bf16[256,512]{1,0:T(8,128)(2,1)S(1)}, u32[]{:S(2)}, u32[]{:S(2)}) collective-permute-start(bf16[256,512]{1,0:T(8,128)(2,1)S(1)} %shard_map.153), channel_id=1, source_target_pairs={{0,1},{1,0},{2,3},{3,2},{4,5},{5,4},{6,7},{7,6},{8,9},{9,8},{10,11... | collective-permute-start | bytes 786440 | tf_op jit(solution)/shard_map/ppermute | solution.py:118
  49.5 1.9 %collective-permute-start.18 = (f32[16,512]{1,0:T(8,128)S(1)}, f32[16,512]{1,0:T(8,128)S(1)}, u32[]{:S(2)}, u32[]{:S(2)}) collective-permute-start(f32[16,512]{1,0:T(8,128)S(1)} %get-tuple-element.64), channel_id=1, source_target_pairs={{0,1},{1,0},{2,3},{3,2},{4,5},{5,4},{6,7},{7,6},{8,9},{9,8},{10,11... | collective-permute-start | bytes 98312 | tf_op jit(solution)/shard_map/ppermute | solution.py:118
  50.0 4.0 %collective-permute-start.19 = (f32[16,512]{1,0:T(8,128)S(1)}, f32[16,512]{1,0:T(8,128)S(1)}, u32[]{:S(2)}, u32[]{:S(2)}) collective-permute-start(f32[16,512]{1,0:T(8,128)S(1)} %get-tuple-element.65), channel_id=1, source_target_pairs={{0,2},{1,3},{2,0},{3,1},{4,6},{5,7},{6,4},{7,5},{8,10},{9,11},{10,... | collective-permute-start | bytes 98312 | tf_op jit(solution)/shard_map/ppermute | solution.py:118
  50.9 3.7 %collective-permute-start.20 = (f32[16,512]{1,0:T(8,128)S(1)}, f32[16,512]{1,0:T(8,128)S(1)}, u32[]{:S(2)}, u32[]{:S(2)}) collective-permute-start(f32[16,512]{1,0:T(8,128)S(1)} %get-tuple-element.66), channel_id=1, source_target_pairs={{0,3},{1,2},{2,1},{3,0},{4,7},{5,6},{6,5},{7,4},{8,11},{9,10},{10,... | collective-permute-start | bytes 98312 | tf_op jit(solution)/shard_map/ppermute | solution.py:118
where the time goes:
time: 56.4 us; the launch traced here: 56.2 us
  starting transfers between devices  25.8 us (46%)
  Pallas kernels  14.2 us (25%)
  waiting for transfers between devices  13.5 us (24%)
  other arithmetic  1.58 us (3%)
  between operations  0.95 us (2%)
    ppermute x19, starting transfers between devices, swap(): return lax.ppermute(array, 'seq', [(i, i ^ distance) for i in devices])  21.8 us
    pallas_call x17, Pallas kernels, call(): pl.pallas_call(run, out_shape=outs, in_specs=specs, out_specs=[pl.BlockSp...  14.2 us
    ppermute x19, waiting for transfers between devices, swap(): return lax.ppermute(array, 'seq', [(i, i ^ distance) for i in devices])  11.9 us
    ppermute x2, starting transfers between devices, shift(): lax.ppermute(array, 'seq', [(i, i + distance) for i in devices if i + dis...  3.97 us
    ppermute x2, waiting for transfers between devices, shift(): lax.ppermute(array, 'seq', [(i, i + distance) for i in devices if i + dis...  1.56 us
    convert_element_type x1, other arithmetic, product_block(): return (left * right).astype(bf16)  1.51 us
  transfers between devices with their start and end apart: 21, of which 9 were waited for; matrix products, arithmetic and copies ran while one was open for 0% of the time, Pallas kernels for 21%

commit v1 on v0

v1 whole, which is shorter than its diff:
```python
import math

import jax
import jax.numpy as jnp
import numpy as np
from jax import lax
from jax.experimental import pallas as pl
from jax.experimental.pallas import tpu as pltpu
from jax.sharding import PartitionSpec as P

PLANE = 4
VMEM_BYTES = 32 * 1024 * 1024


def tables(block):
    half = np.concatenate([np.arange(0, block, 2), np.arange(1, block, 2)])
    angle = np.pi * (half[:, None] + 0.5) * np.arange(block)[None, :] / block
    forward = np.concatenate([np.cos(angle), -np.sin(angle)], 0)
    inverse = forward.T / block
    return forward, inverse


def pair(table):
    high = table.astype(np.float32).astype(jnp.bfloat16)
    low = (table - high.astype(np.float64)).astype(np.float32).astype(jnp.bfloat16)
    return jnp.asarray(high), jnp.asarray(low)


def dot(left, right):
    return jnp.dot(left, right, preferred_element_type=jnp.float32)


def spectrum(high, low, block):
    return dot(high[...], block) + dot(low[...], block)


def restore(high, low, real, imag):
    spec = jnp.concatenate([real, imag], 0)
    top = spec.astype(jnp.bfloat16)
    rest = (spec - top.astype(jnp.float32)).astype(jnp.bfloat16)
    return dot(high[...], top) + dot(low[...], top) + dot(high[...], rest)


def parts(spec):
    half = spec.shape[0] // 2
    return spec[:half], spec[half:]


def turned(spec, sign):
    real, imag = parts(spec)
    quarter = real.shape[0] // 2
    flip = lambda a, s: jnp.concatenate([s * a[:quarter], -s * a[quarter:]], 0)
    return flip(imag, -sign), flip(real, sign)


def window(near, far, sign):
    real, imag = parts(near)
    other_real, other_imag = turned(far, sign)
    return real + other_real, imag + other_imag


def times(left, right):
    return left[0] * right[0] - left[1] * right[1], left[0] * right[1] + left[1] * right[0]


def times_conj(left, right):
    return left[0] * right[0] + left[1] * right[1], left[1] * right[0] - left[0] * right[1]


def call(body, outs, args, scratch=(), spaces=None, after=(), flops=1, aliases=()):
    specs = [
        pl.BlockSpec(memory_space=pltpu.SMEM if a.ndim == 1 else pltpu.VMEM) for a in args
    ]
    after = [*after, *aliases]
    specs += [pl.BlockSpec(memory_space=pl.ANY)] * len(after)
    base = len(args) + len(after) - len(aliases)

    def run(*refs):
        body(*refs[: len(args)], *refs[len(args) + len(after) :])

    spaces = spaces or [pltpu.VMEM] * len(outs)
    return pl.pallas_call(
        run,
        out_shape=outs,
        in_specs=specs,
        out_specs=[pl.BlockSpec(memory_space=space) for space in spaces],
        scratch_shapes=scratch,
        input_output_aliases={base + n: n for n in range(len(aliases))},
        compiler_params=pltpu.CompilerParams(vmem_limit_bytes=VMEM_BYTES),
        cost_estimate=pl.CostEstimate(flops=flops, bytes_accessed=1, transcendentals=0),
    )(*args, *after)


def shards(queries, keys, values, out_grad, filter_taps):
    f32, bf16 = jnp.float32, jnp.bfloat16
    rows, channels = queries.shape
    nseq = lax.axis_size("seq")
    own_taps = filter_taps.shape[0]
    taps = own_taps * nseq
    planes = nseq // PLANE
    width = channels // PLANE
    tokens = rows * PLANE
    pad_taps = max(16, own_taps)
    plane_taps = taps // planes
    column = planes * pad_taps
    assert tokens == 2 * taps
    me = lax.axis_index("seq")
    place = jnp.stack([me % PLANE, me // PLANE]).astype(jnp.int32)
    devices = range(nseq)

    forward, inverse = tables(taps)
    fwd = pair(forward)
    inv = pair(inverse)
    lag_of = np.full((planes * PLANE, pad_taps), -1)
    lag_of[:, :own_taps] = np.arange(taps).reshape(planes * PLANE, own_taps)
    lag_of = lag_of.reshape(planes, PLANE, pad_taps).transpose(1, 0, 2).reshape(-1)
    fwd_lag = pair(np.where(lag_of[None, :] >= 0, forward[:, np.maximum(lag_of, 0)], 0.0))

    def swap(array, distance):
        return lax.ppermute(array, "seq", [(i, i ^ distance) for i in devices])

    def shift(array, distance):
        return lax.ppermute(
            array, "seq", [(i, i + distance) for i in devices if i + distance in devices]
        )

    def struct(r, c, dtype):
        return jax.ShapeDtypeStruct((r, c), dtype)

    def block_at(index, size):
        return pl.ds(pl.multiple_of(index * size, size), size)

    def lay_taps(place_ref, *refs):
        ins, (keep, side, full) = refs[:planes], refs[planes:]
        q, z = place_ref[0], place_ref[1]
        for step in range(planes):
            full[block_at(z ^ step, pad_taps)] = ins[step][...]
        for step, (out, half) in enumerate(((keep, 0), (side, 0), (keep, 1), (side, 1))):
            out[half * column : (half + 1) * column] = full[:, block_at(q ^ step, width)]

    def narrow_taps(taps_ref, out):
        out[:own_taps] = taps_ref[...].astype(bf16)
        if pad_taps > own_taps:
            out[own_taps:] = jnp.zeros((pad_taps - own_taps, channels), bf16)

    def gate_grad(place_ref, o_ref, q_ref, p_ref, keep, side):
        q = place_ref[0]
        side[:rows] = p_ref[...]
        for step, (out, first) in enumerate(((keep, 0), (side, rows), (keep, rows), (side, 2 * rows))):
            at = block_at(q ^ step, width)
            out[first : first + rows] = (
                o_ref[:, at].astype(f32) * q_ref[:, at].astype(f32)
            ).astype(bf16)

    def join(left, right, after=(), flops=1):
        def body(left_ref, right_ref, out):
            out[:rows] = left_ref[left.shape[0] - rows :]
            out[rows:] = right_ref[right.shape[0] - rows :]

        return call(body, [struct(2 * rows, width, bf16)], [left, right], after=after, flops=flops)[0]

    def gather_product(place_ref, *refs):
        ins, (product, top) = refs[:PLANE], refs[PLANE:]
        q = place_ref[0]
        for step in range(PLANE):
            product[block_at(q ^ step, rows)] = ins[step][:rows]
        top[...] = product[tokens - taps :]

    def join_taps(keep, near, ship):
        ship[:column] = keep[column:]
        ship[column:] = near[column:]

    def gather_grad(place_ref, keep, near, far, grad, bottom):
        q = place_ref[0]
        grad[block_at(q, rows)] = keep[:rows]
        grad[block_at(q ^ 1, rows)] = near[rows : 2 * rows]
        grad[block_at(q ^ 2, rows)] = far[:rows]
        grad[block_at(q ^ 3, rows)] = far[rows:]
        bottom[...] = grad[:taps]

    def own_spectra(array, flops, after):
        def body(high, low, ref, *outs):
            for block in range(2):
                outs[block][...] = spectrum(high, low, ref[block * taps : (block + 1) * taps])

        return call(body, [struct(2 * taps, width, f32)] * 2, [*fwd, array], flops=flops, after=after)

    def lags(place_ref, high, low, inv_high, inv_low, p0, p1, g0, g1, halo, *refs):
        spec, outs, full = refs[0], refs[1:-1], refs[-1]
        behind = spectrum(high, low, halo[...])
        spec[...] = behind
        one = times_conj(parts(g0[...]), window(p0[...], behind, 1.0))
        two = times_conj(parts(g1[...]), window(p1[...], p0[...], 1.0))
        full[...] = restore(inv_high, inv_low, one[0] + two[0], one[1] + two[1])
        for step in range(planes):
            block = full[block_at(place_ref[1] ^ step, plane_taps)]
            outs[step][...] = block.astype(outs[step].dtype)

    def signal(inv_refs, taps_spec, near, far, sign):
        real, imag = parts(taps_spec)
        value = times((real, sign * imag), window(near, far, sign))
        return restore(*inv_refs, *value).astype(bf16)

    def inner(place_ref, high, low, inv_high, inv_low, p0, p1, g0, g1, *refs):
        keep, near_taps, far_taps, spec, ship, filt, held = refs
        q = place_ref[0]
        filt[block_at(q, column)] = keep[:column]
        filt[block_at(q ^ 1, column)] = near_taps[:column]
        filt[block_at(q ^ 2, column)] = far_taps[:column]
        filt[block_at(q ^ 3, column)] = far_taps[column:]
        taps_spec = spectrum(high, low, filt[...])
        spec[...] = taps_spec
        left = q < 2
        near = jnp.where(left, p1[...], g0[...])
        far = jnp.where(left, p0[...], g1[...])
        held[...] = signal((inv_high, inv_low), taps_spec, near, far, jnp.where(left, 1.0, -1.0))
        ship[:rows] = held[block_at(q % 2, rows)]
        ship[rows:] = held[block_at(1 - q % 2, rows)]

    def outer(place_ref, high, low, inv_high, inv_low, p0, g1, behind, halo, taps_ref, *refs):
        spec, ship, held = refs
        q = place_ref[0]
        ahead = spectrum(high, low, halo[...])
        spec[...] = ahead
        left = q < 2
        near = jnp.where(left, g1[...], p0[...])
        far = jnp.where(left, ahead, behind[...])
        sign = jnp.where(left, -1.0, 1.0)
        held[...] = signal((inv_high, inv_low), taps_ref[...], near, far, sign)
        ship[:rows] = held[block_at(q % 2, rows)]
        ship[rows:] = held[block_at(1 - q % 2, rows)]

    def kept(place_ref, inv_high, inv_low, p0, p1, g0, g1, behind, ahead, taps_ref, *refs):
        mixed_own, corr_own, side, held = refs
        q = place_ref[0]
        left = q < 2
        inv_refs = (inv_high, inv_low)
        near = jnp.where(left, p0[...], p1[...])
        far = jnp.where(left, behind[...], p0[...])
        held[...] = signal(inv_refs, taps_ref[...], near, far, 1.0)
        mixed_own[...] = held[block_at(q % 2, rows)]
        side[:rows] = held[block_at(1 - q % 2, rows)]
        near = jnp.where(left, g0[...], g1[...])
        far = jnp.where(left, g1[...], ahead[...])
        held[...] = signal(inv_refs, taps_ref[...], near, far, -1.0)
        corr_own[...] = held[block_at(q % 2, rows)]
        side[rows:] = held[block_at(1 - q % 2, rows)]

    def pick(ref, index):
        if own_taps % 8 == 0:
            return ref[block_at(index, own_taps)]
        value = ref[:own_taps]
        for n in range(1, PLANE):
            value = jnp.where(index == n, ref[n * own_taps : (n + 1) * own_taps], value)
        return value

    def add_lags(place_ref, *refs):
        ins, (own, side, ship, full) = refs[:planes], refs[planes:]
        q = place_ref[0]
        total = ins[0][...]
        for ref in ins[1:]:
            total = total + ref[...].astype(f32)
        full[...] = total * (1.0 / math.sqrt(rows * nseq))
        own[...] = pick(full, q)
        side[...] = pick(full, q ^ 1)
        ship[:own_taps] = pick(full, q ^ 2)
        ship[own_taps:] = pick(full, q ^ 3)

    def join_first(side, far, out):
        out[: 2 * rows] = side[...]
        out[2 * rows :] = far[rows:]

    def join_second(far, lag_side, lag_far, out, lag_out):
        out[...] = far[rows:]
        lag_out[:own_taps] = lag_side[...]
        lag_out[own_taps:] = lag_far[own_taps:]

    def write(place_ref, steps, values, gates, outs, held, sems):
        copies = []
        for n, step in enumerate(steps):
            at = block_at(place_ref[0] ^ step, width)
            for m, (gate, out) in enumerate(zip(gates, outs)):
                value = values[n][min(m, 1)].astype(f32)
                held[m, n] = (value * gate[:, at].astype(f32)).astype(bf16)
                copy = pltpu.make_async_copy(held.at[m, n], out.at[:, at], sems.at[m, n])
                copy.start()
                copies.append(copy)
        return copies

    def finish_near(place_ref, mixed, corr, near, o_ref, v_ref, k_ref, *refs):
        outs, (mark, held, sems) = refs[:3], refs[3:]
        values = ((mixed[...], corr[...]), (near[:rows], near[rows : 2 * rows]))
        copies = write(place_ref, (0, 1), values, (o_ref, v_ref, k_ref), outs, held, sems)
        mark[...] = jnp.zeros_like(mark)
        for copy in copies:
            copy.wait()

    def finish_far(place_ref, first, second, near, last, o_ref, v_ref, k_ref, *refs):
        lag_own, lag_near, lag_far, dq, dk, dv, df, held, full, sems, sem = refs
        q = place_ref[0]
        left = q < 2
        values = []
        for one, two in ((first[:rows], second[:rows]), (near[2 * rows :], last[...])):
            values.append((jnp.where(left, two, one), jnp.where(left, one, two)))
        copies = write(place_ref, (2, 3), values, (o_ref, v_ref, k_ref), (dq, dk, dv), held, sems)
        full[:, block_at(q, width)] = lag_own[...]
        full[:, block_at(q ^ 1, width)] = lag_near[:own_taps]
        full[:, block_at(q ^ 2, width)] = lag_far[:own_taps]
        full[:, block_at(q ^ 3, width)] = lag_near[own_taps:]
        copy = pltpu.make_async_copy(full, df, sem)
        copy.start()
        for copy in copies + [copy]:
            copy.wait()

    block = struct(rows, width, bf16)
    double = struct(2 * rows, width, bf16)
    spectral = struct(2 * taps, width, f32)
    halo = struct(taps, width, bf16)

    def product_block(step):
        start = (place[0] ^ step) * width
        left = lax.dynamic_slice_in_dim(keys, start, width, 1).astype(f32)
        right = lax.dynamic_slice_in_dim(values, start, width, 1).astype(f32)
        return (left * right).astype(bf16)

    sent = [product_block(step) for step in range(PLANE)]
    far_p = [swap(sent[step], step) for step in (2, 3)]
    keep, side = call(
        gate_grad,
        flops=1,
        outs=[double, struct(3 * rows, width, bf16)],
        args=[place, out_grad, queries, sent[1]],
        after=[],
    )
    near = swap(side, 1)
    far = swap(join(keep, near, after=[far_p[1]], flops=1000000000), 2)

    product, top = call(
        gather_product,
        [struct(tokens, width, bf16), halo],
        [place, sent[0], near, *far_p],
        flops=1,
    )
    (narrow,) = call(
        narrow_taps,
        [struct(pad_taps, channels, bf16)],
        [filter_taps],
        after=[near],
        flops=1,
    )
    far_taps = [swap(narrow, PLANE * step) for step in range(1, planes)]
    taps_keep, taps_side = call(
        lay_taps,
        [struct(2 * column, width, bf16)] * 2,
        [place, narrow, *far_taps],
        scratch=[pltpu.VMEM((column, channels), bf16)],
        after=[product],
        flops=1,
    )
    taps_near = swap(taps_side, 1)
    (taps_ship,) = call(
        join_taps,
        [struct(2 * column, width, bf16)],
        [taps_keep, taps_near],
        flops=1,
    )
    taps_far = swap(taps_ship, 2)

    behind = shift(top, PLANE)
    p_spec = own_spectra(product, 1, [])

    grad, bottom = call(
        gather_grad,
        [struct(tokens, width, bf16), halo],
        [place, keep, near, far],
        after=[taps_ship],
        flops=1,
    )
    ahead = shift(bottom, -PLANE)
    g_spec = own_spectra(grad, 1, [])

    taps_spec, ship = call(
        inner,
        [spectral, double],
        [place, *fwd_lag, *inv, *p_spec, *g_spec, taps_keep, taps_near, taps_far],
        scratch=[pltpu.VMEM((PLANE * column, width), bf16), pltpu.VMEM((taps, width), bf16)],
        after=[],
        flops=10000000000,
    )
    first = swap(ship, 2)
    behind_spec, own_lags, *away = call(
        lags,
        [spectral, struct(plane_taps, width, f32)]
        + [struct(plane_taps, width, bf16)] * (planes - 1),
        [place, *fwd, *inv, *p_spec, *g_spec, behind],
        scratch=[pltpu.VMEM((taps, width), f32)],
        after=[taps_spec],
        flops=1,
    )
    away = [swap(part, PLANE * (step + 1)) for step, part in enumerate(away)]
    ahead_spec, ship = call(
        outer,
        [spectral, double],
        [place, *fwd, *inv, p_spec[0], g_spec[1], behind_spec, ahead, taps_spec],
        scratch=[pltpu.VMEM((taps, width), bf16)],
        after=[taps_spec],
        flops=1,
    )
    second = swap(ship, 2)
    mixed_own, corr_own, side = call(
        kept,
        [block, block, double],
        [place, *inv, *p_spec, *g_spec, behind_spec, ahead_spec, taps_spec],
        scratch=[pltpu.VMEM((taps, width), bf16)],
        after=[first],
        flops=1,
    )
    triple = struct(3 * rows, width, bf16)
    (joined,) = call(
        join_first, [triple], [side, first], after=[], flops=1
    )
    near = swap(joined, 1)
    lag_double = struct(2 * own_taps, width, f32)
    lag_own, lag_side, lag_ship = call(
        add_lags,
        [struct(own_taps, width, f32)] * 2 + [lag_double],
        [place, own_lags, *away],
        scratch=[pltpu.VMEM((plane_taps, width), f32)],
        after=[corr_own],
        flops=10000000000,
    )
    lag_far = swap(lag_ship, 2)
    whole = struct(rows, channels, bf16)
    *partial, mark = call(
        finish_near,
        [whole] * 3 + [struct(8, 128, f32)],
        [place, mixed_own, corr_own, near, out_grad, values, keys],
        scratch=[
            pltpu.VMEM((3, 2, rows, width), bf16),
            pltpu.SemaphoreType.DMA((3, 2)),
        ],
        spaces=[pl.ANY] * 3 + [pltpu.VMEM],
        flops=1,
    )
    joined, lag_joined = call(
        join_second,
        [block, lag_double],
        [second, lag_side, lag_far],
        after=[mark],
        flops=1,
    )
    last = swap(joined, 1)
    lag_near = swap(lag_joined, 1)
    return call(
        finish_far,
        [whole] * 3 + [struct(own_taps, channels, f32)],
        [place, first, second, near, last, out_grad, values, keys, lag_own, lag_near, lag_far],
        scratch=[
            pltpu.VMEM((3, 2, rows, width), bf16),
            pltpu.VMEM((own_taps, channels), f32),
            pltpu.SemaphoreType.DMA((3, 2)),
            pltpu.SemaphoreType.DMA,
        ],
        spaces=[pl.ANY] * 4,
        aliases=partial,
    )


def solution(mesh):
    placed = (
        P(("grp", "seq"), None),
        P(("grp", "seq"), None),
        P(("grp", "seq"), None),
        P(("grp", "seq"), None),
        P("seq", None),
    )
    return jax.shard_map(
        shards,
        mesh=mesh,
        in_specs=placed,
        out_specs=(
            P(("grp", "seq"), None),
            P(("grp", "seq"), None),
            P(("grp", "seq"), None),
            P(("grp", "seq"), None),
        ),
        check_vma=False,
    )
```

time: 56.4 us -> 50.2 us (0.89)
  waiting for transfers between devices: 13.5 us -> 6.37 us
  Pallas kernels: 14.2 us -> 15.5 us
  starting transfers between devices: 25.8 us -> 25.1 us
    ppermute x19 -> x18, waiting for transfers between devices: 11.9 us -> 6.37 us  [swap(): return lax.ppermute(array, 'seq', [(i, i ^ distance) for i in devices])]
    ppermute x2, waiting for transfers between devices: 1.56 us -> 0.01 us  [shift(): lax.ppermute(array, 'seq', [(i, i + distance) for i in devices if i + dis...]
    pallas_call x17 -> x18, Pallas kernels: 14.2 us -> 15.5 us  [call(): pl.pallas_call(run, out_shape=outs, in_specs=specs, out_specs=[pl.BlockSp...]
    ppermute x19 -> x18, starting transfers between devices: 21.8 us -> 20.8 us  [swap(): return lax.ppermute(array, 'seq', [(i, i ^ distance) for i in devices])]
  transfers between devices with their start and end apart: 21 -> 20, of which waited for: 9 -> 5; matrix products, arithmetic and copies ran while one was open for 0% -> 0% of each run, Pallas kernels for 21% -> 27%
where the time goes in v1:
time: 50.2 us; the launch traced here: 50 us
  starting transfers between devices  25.1 us (50%)
  Pallas kernels  15.5 us (31%)
  waiting for transfers between devices  6.37 us (13%)
  other arithmetic  1.58 us (3%)
  between operations  0.96 us (2%)
  local copies, waits for them, and re-layouts  0.57 us (1%)
    ppermute x18, starting transfers between devices, swap(): return lax.ppermute(array, 'seq', [(i, i ^ distance) for i in devices])  20.8 us
    pallas_call x18, Pallas kernels, call(): pl.pallas_call(run, out_shape=outs, in_specs=specs, out_specs=[pl.BlockSp...  15.5 us
    ppermute x18, waiting for transfers between devices, swap(): return lax.ppermute(array, 'seq', [(i, i ^ distance) for i in devices])  6.37 us
    ppermute x2, starting transfers between devices, shift(): lax.ppermute(array, 'seq', [(i, i + distance) for i in devices if i + dis...  4.25 us
    convert_element_type x1, other arithmetic, product_block(): return (left * right).astype(bf16)  1.51 us
  transfers between devices with their start and end apart: 20, of which 5 were waited for; matrix products, arithmetic and copies ran while one was open for 0% of the time, Pallas kernels for 27%

profile of v1, /device:TPU:0, one launch (start us, length us, event | category | flops | bytes accessed | tf_op | source)
XLA Modules:
  0.0 50.0 jit_solution(5046192476252169828)
XLA Ops:
  0.7 0.1 pad_add_fusion.refs_0_
  0.8 1.5 %multiply_convert_fusion = (bf16[128,512]{1,0:T(8,128)(2,1)S(1)}, bf16[128,512]{1,0:T(8,128)(2,1)S(1)}, bf16[128,512]{1,0:T(8,128)(2,1)S(1)}, bf16[128,512]{1,0:T(8,128)(2,1)S(1)}) fusion(bf16[128,2048]{1,0:T(8,128)(2,1)} %refs_6_.3, s32[]{:T(128)S(6)} %select_n.32, bf16[128,2048]{1,0:T(8,128)(2,1)} %refs_7_.1, s32[]{:T(128)S(6)} %select_n.31, ...), kind=kLoop, calls=%fused_computation | loop fusion | flops 1048576 | bytes 1572880 | tf_op jit(solution)/shard_map/convert_element_type | solution.py:324
  2.3 0.1 copy-done.7
  2.4 0.7 %shard_map.138 = (bf16[256,512]{1,0:T(8,128)(2,1)S(1)}, bf16[384,512]{1,0:T(8,128)(2,1)S(1)}) custom-call(s32[2]{0:T(128)S(1)} %pad_add_fusion.refs_0_, bf16[128,2048]{1,0:T(8,128)(2,1)S(1)} %copy-done.2, bf16[128,2048]{1,0:T(8,128)(2,1)S(1)} %copy-done.7, bf16[128,512]{1,0:T(8,128)(2,1)S(1)} %get-tuple-element.72.refs_3_), custom_call_target="tpu_custom_call" | custom-call | flops 1 | bytes 1 | tf_op jit(solution)/shard_map/pallas_call | solution.py:82
  3.0 0.5 %collective-permute-start = (bf16[384,512]{1,0:T(8,128)(2,1)S(1)}, bf16[384,512]{1,0:T(8,128)(2,1)S(1)}, u32[]{:S(2)}, u32[]{:S(2)}) collective-permute-start(bf16[384,512]{1,0:T(8,128)(2,1)S(1)} %get-tuple-element.37), channel_id=1, source_target_pairs={{0,1},{1,0},{2,3},{3,2},{4,5},{5,4},{6,7},{7,6},{8,9},{9,8},{10,11... | collective-permute-start | bytes 1179656 | tf_op jit(solution)/shard_map/ppermute | solution.py:120
  3.6 2.6 %collective-permute-start.2 = (bf16[128,512]{1,0:T(8,128)(2,1)S(1)}, bf16[128,512]{1,0:T(8,128)(2,1)S(1)}, u32[]{:S(2)}, u32[]{:S(2)}) collective-permute-start(bf16[128,512]{1,0:T(8,128)(2,1)S(1)} %get-tuple-element.70), channel_id=1, source_target_pairs={{0,3},{1,2},{2,1},{3,0},{4,7},{5,6},{6,5},{7,4},{8,11},{9,10},{10,... | collective-permute-start | bytes 393224 | tf_op jit(solution)/shard_map/ppermute | solution.py:120
  6.2 0.0 collective-permute-start.1
  6.2 4.2 %collective-permute-start.6 = (bf16[16,2048]{1,0:T(8,128)(2,1)S(1)}, bf16[16,2048]{1,0:T(8,128)(2,1)S(1)}, u32[]{:S(2)}, u32[]{:S(2)}) collective-permute-start(bf16[16,2048]{1,0:T(8,128)(2,1)S(1)} %shard_map.142.refs_1_), channel_id=1, source_target_pairs={{0,12},{1,13},{2,14},{3,15},{4,8},{5,9},{6,10},{7,11},{8,4},{9,5},... | collective-permute-start | bytes 196616 | tf_op jit(solution)/shard_map/ppermute | solution.py:120
  10.4 0.6 %collective-permute-start.4 = (bf16[16,2048]{1,0:T(8,128)(2,1)S(1)}, bf16[16,2048]{1,0:T(8,128)(2,1)S(1)}, u32[]{:S(2)}, u32[]{:S(2)}) collective-permute-start(bf16[16,2048]{1,0:T(8,128)(2,1)S(1)} %shard_map.142.refs_1_), channel_id=1, source_target_pairs={{0,4},{1,5},{2,6},{3,7},{4,0},{5,1},{6,2},{7,3},{8,12},{9,13},{10,... | collective-permute-start | bytes 196616 | tf_op jit(solution)/shard_map/ppermute | solution.py:120
  11.1 1.7 %collective-permute-start.3 = (bf16[256,512]{1,0:T(8,128)(2,1)S(1)}, bf16[256,512]{1,0:T(8,128)(2,1)S(1)}, u32[]{:S(2)}, u32[]{:S(2)}) collective-permute-start(bf16[256,512]{1,0:T(8,128)(2,1)S(1)} %shard_map.141), channel_id=1, source_target_pairs={{0,2},{1,3},{2,0},{3,1},{4,6},{5,7},{6,4},{7,5},{8,10},{9,11},{10,... | collective-permute-start | bytes 786440 | tf_op jit(solution)/shard_map/ppermute | solution.py:120
  12.8 0.3 collective-permute-done.1.refs_3_
  13.0 0.6 %shard_map.139 = (bf16[512,512]{1,0:T(8,128)(2,1)S(1)}, bf16[256,512]{1,0:T(8,128)(2,1)S(1)}) custom-call(s32[2]{0:T(128)S(1)} %pad_add_fusion.refs_0_, bf16[128,512]{1,0:T(8,128)(2,1)S(1)} %get-tuple-element.73.refs_1_, bf16[384,512]{1,0:T(8,128)(2,1)S(1)} %collective-permute-done.refs_2_.refs_1_, bf16[128,512]{1,0:T(8,128)(2,1)S(1)} %collective-permute-done.1.refs_3_, ...), custom_call_target="tpu_custom_call" | custom-call | flops 1 | bytes 1 | tf_op jit(solution)/shard_map/pallas_call | solution.py:82
  13.6 2.3 %collective-permute-done.5.refs_3_ = bf16[16,2048]{1,0:T(8,128)(2,1)S(1)} collective-permute-done((bf16[16,2048]{1,0:T(8,128)(2,1)S(1)}, bf16[16,2048]{1,0:T(8,128)(2,1)S(1)}, u32[]{:S(2)}, u32[]{:S(2)}) %collective-permute-start.5) | collective-permute-done | bytes 65568 | tf_op jit(solution)/shard_map/ppermute | solution.py:120
  16.0 0.6 %shard_map.143 = (bf16[128,512]{1,0:T(8,128)(2,1)S(1)}, bf16[128,512]{1,0:T(8,128)(2,1)S(1)}) custom-call(s32[2]{0:T(128)S(1)} %pad_add_fusion.refs_0_, bf16[16,2048]{1,0:T(8,128)(2,1)S(1)} %shard_map.142.refs_1_, bf16[16,2048]{1,0:T(8,128)(2,1)S(1)} %collective-permute-done.4.refs_2_, bf16[16,2048]{1,0:T(8,128)(2,1)S(1)} %collective-permute-done.5.refs_3_, ...), custom_call_target="tpu_custom_call" | custom-call | flops 1 | bytes 1 | tf_op jit(solution)/shard_map/pallas_call | solution.py:82
  16.5 0.0 copy-start.3
  16.6 0.1 collective-permute-start.7
  16.6 1.3 %collective-permute-done.7.refs_1_.refs_10_ = bf16[128,512]{1,0:T(8,128)(2,1)S(1)} collective-permute-done((bf16[128,512]{1,0:T(8,128)(2,1)S(1)}, bf16[128,512]{1,0:T(8,128)(2,1)S(1)}, u32[]{:S(2)}, u32[]{:S(2)}) %collective-permute-start.7) | collective-permute-done | bytes 131104 | tf_op jit(solution)/shard_map/ppermute | solution.py:120
  18.0 1.6 %collective-permute-start.8 = (bf16[128,512]{1,0:T(8,128)(2,1)S(1)}, bf16[128,512]{1,0:T(8,128)(2,1)S(1)}, u32[]{:S(2)}, u32[]{:S(2)}) collective-permute-start(bf16[128,512]{1,0:T(8,128)(2,1)S(1)} %shard_map.144.refs_4_), channel_id=1, source_target_pairs={{0,2},{1,3},{2,0},{3,1},{4,6},{5,7},{6,4},{7,5},{8,10},{9,11},{10,... | collective-permute-start | bytes 393224 | tf_op jit(solution)/shard_map/ppermute | solution.py:120
  19.6 3.0 %collective-permute-start.10 = (bf16[256,512]{1,0:T(8,128)(2,1)S(1)}, bf16[256,512]{1,0:T(8,128)(2,1)S(1)}, u32[]{:S(2)}, u32[]{:S(2)}) collective-permute-start(bf16[256,512]{1,0:T(8,128)(2,1)S(1)} %get-tuple-element.48), channel_id=1, source_target_pairs={{0,4},{1,5},{2,6},{3,7},{4,8},{5,9},{6,10},{7,11},{8,12},{9,13},{1... | collective-permute-start | bytes 786440 | tf_op jit(solution)/shard_map/ppermute | solution.py:123
  22.6 0.7 %shard_map.140 = (f32[512,512]{1,0:T(8,128)S(1)}, f32[512,512]{1,0:T(8,128)S(1)}) custom-call(bf16[512,256]{1,0:T(8,128)(2,1)S(1)} %copy-done.4, bf16[512,256]{1,0:T(8,128)(2,1)S(1)} %copy-done.3, bf16[512,512]{1,0:T(8,128)(2,1)S(1)} %get-tuple-element.38.refs_2_.refs_5_), custom_call_target="tpu_custom_call" | custom-call | flops 1 | bytes 1 | tf_op jit(solution)/shard_map/pallas_call | solution.py:82
  23.3 0.6 %shard_map.145 = (bf16[512,512]{1,0:T(8,128)(2,1)S(1)}, bf16[256,512]{1,0:T(8,128)(2,1)S(1)}) custom-call(s32[2]{0:T(128)S(1)} %pad_add_fusion.refs_0_, bf16[256,512]{1,0:T(8,128)(2,1)S(1)} %get-tuple-element.41.refs_0_.refs_1_, bf16[384,512]{1,0:T(8,128)(2,1)S(1)} %collective-permute-done.refs_2_.refs_1_, ...), custom_call_target="tpu_custom_call" | custom-call | flops 1 | bytes 1 | tf_op jit(solution)/shard_map/pallas_call | solution.py:82
  23.9 1.3 %collective-permute-start.11 = (bf16[256,512]{1,0:T(8,128)(2,1)S(1)}, bf16[256,512]{1,0:T(8,128)(2,1)S(1)}, u32[]{:S(2)}, u32[]{:S(2)}) collective-permute-start(bf16[256,512]{1,0:T(8,128)(2,1)S(1)} %get-tuple-element.51), channel_id=1, source_target_pairs={{4,0},{5,1},{6,2},{7,3},{8,4},{9,5},{10,6},{11,7},{12,8},{13,9},{1... | collective-permute-start | bytes 786440 | tf_op jit(solution)/shard_map/ppermute | solution.py:123
  25.2 0.0 copy-start.5
  25.2 0.0 copy-start.6
  25.2 0.7 %shard_map.146 = (f32[512,512]{1,0:T(8,128)S(1)}, f32[512,512]{1,0:T(8,128)S(1)}) custom-call(bf16[512,256]{1,0:T(8,128)(2,1)S(1)} %copy-done.4, bf16[512,256]{1,0:T(8,128)(2,1)S(1)} %copy-done.3, bf16[512,512]{1,0:T(8,128)(2,1)S(1)} %get-tuple-element.44.refs_2_), custom_call_target="tpu_custom_call" | custom-call | flops 1 | bytes 1 | tf_op jit(solution)/shard_map/pallas_call | solution.py:82
  26.0 0.2 copy-done.5
  26.1 0.1 copy-done.6
  26.2 0.1 copy-done.9
  26.3 0.1 copy-done.10
  26.4 1.9 %shard_map.147 = (f32[512,512]{1,0:T(8,128)S(1)}, bf16[256,512]{1,0:T(8,128)(2,1)S(1)}) custom-call(s32[2]{0:T(128)S(1)} %pad_add_fusion.refs_0_, bf16[512,256]{1,0:T(8,128)(2,1)S(1)} %copy-done.10, bf16[512,256]{1,0:T(8,128)(2,1)S(1)} %copy-done.9, bf16[256,512]{1,0:T(8,128)(2,1)S(1)} %copy-done.6, bf16[256,512]{1,0:T(8,128)(2,1)S(1)} %copy-done.5, ...), custom_call_target="tpu_custom_call" | custom-call | flops 10000000000 | bytes 1 | tf_op jit(solution)/shard_map/pallas_call | solution.py:82
  28.2 0.6 %collective-permute-start.9 = (bf16[256,512]{1,0:T(8,128)(2,1)S(1)}, bf16[256,512]{1,0:T(8,128)(2,1)S(1)}, u32[]{:S(2)}, u32[]{:S(2)}) collective-permute-start(bf16[256,512]{1,0:T(8,128)(2,1)S(1)} %get-tuple-element.47), channel_id=1, source_target_pairs={{0,2},{1,3},{2,0},{3,1},{4,6},{5,7},{6,4},{7,5},{8,10},{9,11},{10,... | collective-permute-start | bytes 786440 | tf_op jit(solution)/shard_map/ppermute | solution.py:120
  28.8 1.9 %shard_map.148 = (f32[512,512]{1,0:T(8,128)S(1)}, f32[64,512]{1,0:T(8,128)S(1)}, bf16[64,512]{1,0:T(8,128)(2,1)S(1)}, bf16[64,512]{1,0:T(8,128)(2,1)S(1)}, bf16[64,512]{1,0:T(8,128)(2,1)S(1)}) custom-call(s32[2]{0:T(128)S(1)} %pad_add_fusion.refs_0_, bf16[512,256]{1,0:T(8,128)(2,1)S(1)} %copy-done.4, bf16[512,256]{1,0:T(8,128)(2,1)S(1)} %copy-done.3, ...), custom_call_target="tpu_custom_call" | custom-call | flops 1 | bytes 1 | tf_op jit(solution)/shard_map/pallas_call | solution.py:82
  30.8 2.7 %collective-permute-start.14 = (bf16[64,512]{1,0:T(8,128)(2,1)S(1)}, bf16[64,512]{1,0:T(8,128)(2,1)S(1)}, u32[]{:S(2)}, u32[]{:S(2)}) collective-permute-start(bf16[64,512]{1,0:T(8,128)(2,1)S(1)} %get-tuple-element.56), channel_id=1, source_target_pairs={{0,4},{1,5},{2,6},{3,7},{4,0},{5,1},{6,2},{7,3},{8,12},{9,13},{10,... | collective-permute-start | bytes 196616 | tf_op jit(solution)/shard_map/ppermute | solution.py:120
  33.5 2.2 %collective-permute-start.15 = (bf16[64,512]{1,0:T(8,128)(2,1)S(1)}, bf16[64,512]{1,0:T(8,128)(2,1)S(1)}, u32[]{:S(2)}, u32[]{:S(2)}) collective-permute-start(bf16[64,512]{1,0:T(8,128)(2,1)S(1)} %get-tuple-element.57), channel_id=1, source_target_pairs={{0,8},{1,9},{2,10},{3,11},{4,12},{5,13},{6,14},{7,15},{8,0},{9,1},... | collective-permute-start | bytes 196616 | tf_op jit(solution)/shard_map/ppermute | solution.py:120
  35.7 0.2 collective-permute-start.16
  36.0 1.9 %shard_map.149 = (f32[512,512]{1,0:T(8,128)S(1)}, bf16[256,512]{1,0:T(8,128)(2,1)S(1)}) custom-call(s32[2]{0:T(128)S(1)} %pad_add_fusion.refs_0_, bf16[512,256]{1,0:T(8,128)(2,1)S(1)} %copy-done.4, bf16[512,256]{1,0:T(8,128)(2,1)S(1)} %copy-done.3, bf16[256,512]{1,0:T(8,128)(2,1)S(1)} %copy-done.6, bf16[256,512]{1,0:T(8,128)(2,1)S(1)} %copy-done.5, ...), custom_call_target="tpu_custom_call" | custom-call | flops 1 | bytes 1 | tf_op jit(solution)/shard_map/pallas_call | solution.py:82
  37.8 1.5 %collective-permute-start.12 = (bf16[256,512]{1,0:T(8,128)(2,1)S(1)}, bf16[256,512]{1,0:T(8,128)(2,1)S(1)}, u32[]{:S(2)}, u32[]{:S(2)}) collective-permute-start(bf16[256,512]{1,0:T(8,128)(2,1)S(1)} %get-tuple-element.52), channel_id=1, source_target_pairs={{0,2},{1,3},{2,0},{3,1},{4,6},{5,7},{6,4},{7,5},{8,10},{9,11},{10,... | collective-permute-start | bytes 786440 | tf_op jit(solution)/shard_map/ppermute | solution.py:120
  39.4 2.2 %shard_map.150 = (bf16[128,512]{1,0:T(8,128)(2,1)S(1)}, bf16[128,512]{1,0:T(8,128)(2,1)S(1)}, bf16[256,512]{1,0:T(8,128)(2,1)S(1)}) custom-call(s32[2]{0:T(128)S(1)} %pad_add_fusion.refs_0_, bf16[256,512]{1,0:T(8,128)(2,1)S(1)} %copy-done.6, bf16[256,512]{1,0:T(8,128)(2,1)S(1)} %copy-done.5, f32[512,512]{1,0:T(8,128)S(1)} %get-tuple-element.39.refs_5_.refs_3_, ...), custom_call_target="tpu_custom_call" | custom-call | flops 1 | bytes 1 | tf_op jit(solution)/shard_map/pallas_call | solution.py:82
  41.7 0.1 collective-permute-start.13
  41.8 0.0 collective-permute-done.16.refs_4_
  41.8 0.6 %shard_map.152 = (f32[16,512]{1,0:T(8,128)S(1)}, f32[16,512]{1,0:T(8,128)S(1)}, f32[32,512]{1,0:T(8,128)S(1)}) custom-call(s32[2]{0:T(128)S(1)} %pad_add_fusion.refs_0_, f32[64,512]{1,0:T(8,128)S(1)} %get-tuple-element.55.refs_1_, bf16[64,512]{1,0:T(8,128)(2,1)S(1)} %collective-permute-done.14.refs_2_, bf16[64,512]{1,0:T(8,128)(2,1)S(1)} %collective-permute-done.15.refs_3_, ...), custom_call_target="tpu_custom_call" | custom-call | flops 10000000000 | bytes 1 | tf_op jit(solution)/shard_map/pallas_call | solution.py:82
  42.4 1.5 %collective-permute-start.17 = (f32[32,512]{1,0:T(8,128)S(1)}, f32[32,512]{1,0:T(8,128)S(1)}, u32[]{:S(2)}, u32[]{:S(2)}) collective-permute-start(f32[32,512]{1,0:T(8,128)S(1)} %get-tuple-element.61), channel_id=1, source_target_pairs={{0,2},{1,3},{2,0},{3,1},{4,6},{5,7},{6,4},{7,5},{8,10},{9,11},{10,... | collective-permute-start | bytes 196616 | tf_op jit(solution)/shard_map/ppermute | solution.py:120
  43.9 1.5 %shard_map.153 = (bf16[128,2048]{1,0:T(8,128)(2,1)}, bf16[128,2048]{1,0:T(8,128)(2,1)}, bf16[128,2048]{1,0:T(8,128)(2,1)}, f32[8,128]{1,0:T(8,128)S(1)}) custom-call(s32[2]{0:T(128)S(1)} %pad_add_fusion.refs_0_, bf16[128,512]{1,0:T(8,128)(2,1)S(1)} %get-tuple-element.62.refs_1_, bf16[128,512]{1,0:T(8,128)(2,1)S(1)} %get-tuple-element.59.refs_5_.refs_2_, ...), custom_call_target="tpu_custom_call" | custom-call | flops 1 | bytes 1 | tf_op jit(solution)/shard_map/pallas_call | solution.py:82
  45.5 1.5 %collective-permute-done.17.refs_2_.refs_10_ = f32[32,512]{1,0:T(8,128)S(1)} collective-permute-done((f32[32,512]{1,0:T(8,128)S(1)}, f32[32,512]{1,0:T(8,128)S(1)}, u32[]{:S(2)}, u32[]{:S(2)}) %collective-permute-start.17) | collective-permute-done | bytes 65568 | tf_op jit(solution)/shard_map/ppermute | solution.py:120
  47.0 0.1 collective-permute-start.18
  47.0 0.5 collective-permute-start.19
  47.5 0.9 %collective-permute-done.19.refs_9_ = f32[32,512]{1,0:T(8,128)S(1)} collective-permute-done((f32[32,512]{1,0:T(8,128)S(1)}, f32[32,512]{1,0:T(8,128)S(1)}, u32[]{:S(2)}, u32[]{:S(2)}) %collective-permute-start.19) | collective-permute-done | bytes 65568 | tf_op jit(solution)/shard_map/ppermute | solution.py:120
  48.5 1.6 %shard_map.155 = (bf16[128,2048]{1,0:T(8,128)(2,1)}, bf16[128,2048]{1,0:T(8,128)(2,1)}, bf16[128,2048]{1,0:T(8,128)(2,1)}, f32[16,2048]{1,0:T(8,128)}) custom-call(s32[2]{0:T(128)S(1)} %pad_add_fusion.refs_0_, bf16[256,512]{1,0:T(8,128)(2,1)S(1)} %collective-permute-done.9.refs_10_.refs_1_, ...), custom_call_target="tpu_custom_call", output_to_operand_aliasing={{0}: (11, {}), {1}: (12, {}), {2}: (13, {})} | custom-call | flops 1 | bytes 1 | tf_op jit(solution)/shard_map/pallas_call | solution.py:82
  (34 shorter events, 0.2 us)
Async XLA Ops:
  0.7 1.5 %copy-start.2 = (bf16[128,2048]{1,0:T(8,128)(2,1)S(1)}, bf16[128,2048]{1,0:T(8,128)(2,1)}, u32[]{:S(2)}) copy-start(bf16[128,2048]{1,0:T(8,128)(2,1)} %refs_5_.3) | copy-start | bytes 1572868
  0.8 1.6 %copy-start.7 = (bf16[128,2048]{1,0:T(8,128)(2,1)S(1)}, bf16[128,2048]{1,0:T(8,128)(2,1)}, u32[]{:S(2)}) copy-start(bf16[128,2048]{1,0:T(8,128)(2,1)} %refs_2_.5) | copy-start | bytes 1572868
  2.4 3.9 %copy-start.8 = (f32[16,2048]{1,0:T(8,128)S(1)}, f32[16,2048]{1,0:T(8,128)}, u32[]{:S(2)}) copy-start(f32[16,2048]{1,0:T(8,128)} %refs_0_.3) | copy-start | bytes 393220
  3.0 3.2 %collective-permute-start = (bf16[384,512]{1,0:T(8,128)(2,1)S(1)}, bf16[384,512]{1,0:T(8,128)(2,1)S(1)}, u32[]{:S(2)}, u32[]{:S(2)}) collective-permute-start(bf16[384,512]{1,0:T(8,128)(2,1)S(1)} %get-tuple-element.37), channel_id=1, source_target_pairs={{0,1},{1,0},{2,3},{3,2},{4,5},{5,4},{6,7},{7,6},{8,9},{9,8},{10,11... | collective-permute-start | bytes 1179656 | tf_op jit(solution)/shard_map/ppermute | solution.py:120
  3.6 7.5 %collective-permute-start.2 = (bf16[128,512]{1,0:T(8,128)(2,1)S(1)}, bf16[128,512]{1,0:T(8,128)(2,1)S(1)}, u32[]{:S(2)}, u32[]{:S(2)}) collective-permute-start(bf16[128,512]{1,0:T(8,128)(2,1)S(1)} %get-tuple-element.70), channel_id=1, source_target_pairs={{0,3},{1,2},{2,1},{3,0},{4,7},{5,6},{6,5},{7,4},{8,11},{9,10},{10,... | collective-permute-start | bytes 393224 | tf_op jit(solution)/shard_map/ppermute | solution.py:120
  6.2 6.8 %collective-permute-start.1 = (bf16[128,512]{1,0:T(8,128)(2,1)S(1)}, bf16[128,512]{1,0:T(8,128)(2,1)S(1)}, u32[]{:S(2)}, u32[]{:S(2)}) collective-permute-start(bf16[128,512]{1,0:T(8,128)(2,1)S(1)} %get-tuple-element.71), channel_id=1, source_target_pairs={{0,2},{1,3},{2,0},{3,1},{4,6},{5,7},{6,4},{7,5},{8,10},{9,11},{10,... | collective-permute-start | bytes 393224 | tf_op jit(solution)/shard_map/ppermute | solution.py:120
  6.2 7.4 %collective-permute-start.6 = (bf16[16,2048]{1,0:T(8,128)(2,1)S(1)}, bf16[16,2048]{1,0:T(8,128)(2,1)S(1)}, u32[]{:S(2)}, u32[]{:S(2)}) collective-permute-start(bf16[16,2048]{1,0:T(8,128)(2,1)S(1)} %shard_map.142.refs_1_), channel_id=1, source_target_pairs={{0,12},{1,13},{2,14},{3,15},{4,8},{5,9},{6,10},{7,11},{8,4},{9,5},... | collective-permute-start | bytes 196616 | tf_op jit(solution)/shard_map/ppermute | solution.py:120
  10.4 5.6 %collective-permute-start.5 = (bf16[16,2048]{1,0:T(8,128)(2,1)S(1)}, bf16[16,2048]{1,0:T(8,128)(2,1)S(1)}, u32[]{:S(2)}, u32[]{:S(2)}) collective-permute-start(bf16[16,2048]{1,0:T(8,128)(2,1)S(1)} %shard_map.142.refs_1_), channel_id=1, source_target_pairs={{0,8},{1,9},{2,10},{3,11},{4,12},{5,13},{6,14},{7,15},{8,0},{9,1},... | collective-permute-start | bytes 196616 | tf_op jit(solution)/shard_map/ppermute | solution.py:120
  10.4 5.6 %collective-permute-start.4 = (bf16[16,2048]{1,0:T(8,128)(2,1)S(1)}, bf16[16,2048]{1,0:T(8,128)(2,1)S(1)}, u32[]{:S(2)}, u32[]{:S(2)}) collective-permute-start(bf16[16,2048]{1,0:T(8,128)(2,1)S(1)} %shard_map.142.refs_1_), channel_id=1, source_target_pairs={{0,4},{1,5},{2,6},{3,7},{4,0},{5,1},{6,2},{7,3},{8,12},{9,13},{10,... | collective-permute-start | bytes 196616 | tf_op jit(solution)/shard_map/ppermute | solution.py:120
  11.1 12.2 %collective-permute-start.3 = (bf16[256,512]{1,0:T(8,128)(2,1)S(1)}, bf16[256,512]{1,0:T(8,128)(2,1)S(1)}, u32[]{:S(2)}, u32[]{:S(2)}) collective-permute-start(bf16[256,512]{1,0:T(8,128)(2,1)S(1)} %shard_map.141), channel_id=1, source_target_pairs={{0,2},{1,3},{2,0},{3,1},{4,6},{5,7},{6,4},{7,5},{8,10},{9,11},{10,... | collective-permute-start | bytes 786440 | tf_op jit(solution)/shard_map/ppermute | solution.py:120
  16.0 6.6 %copy-start.4 = (bf16[512,256]{1,0:T(8,128)(2,1)S(1)}, bf16[512,256]{1,0:T(8,128)(2,1)}, u32[]{:S(2)}) copy-start(bf16[512,256]{1,0:T(8,128)(2,1)} %constant.50.clone.refs_0_.refs_1_) | copy-start | bytes 786436
  16.5 6.0 %copy-start.3 = (bf16[512,256]{1,0:T(8,128)(2,1)S(1)}, bf16[512,256]{1,0:T(8,128)(2,1)}, u32[]{:S(2)}) copy-start(bf16[512,256]{1,0:T(8,128)(2,1)} %constant.51.clone.refs_1_.refs_2_) | copy-start | bytes 786436
  16.6 1.4 %collective-permute-start.7 = (bf16[128,512]{1,0:T(8,128)(2,1)S(1)}, bf16[128,512]{1,0:T(8,128)(2,1)S(1)}, u32[]{:S(2)}, u32[]{:S(2)}) collective-permute-start(bf16[128,512]{1,0:T(8,128)(2,1)S(1)} %get-tuple-element.43), channel_id=1, source_target_pairs={{0,1},{1,0},{2,3},{3,2},{4,5},{5,4},{6,7},{7,6},{8,9},{9,8},{10,11... | collective-permute-start | bytes 393224 | tf_op jit(solution)/shard_map/ppermute | solution.py:120
  18.0 8.0 %collective-permute-start.8 = (bf16[128,512]{1,0:T(8,128)(2,1)S(1)}, bf16[128,512]{1,0:T(8,128)(2,1)S(1)}, u32[]{:S(2)}, u32[]{:S(2)}) collective-permute-start(bf16[128,512]{1,0:T(8,128)(2,1)S(1)} %shard_map.144.refs_4_), channel_id=1, source_target_pairs={{0,2},{1,3},{2,0},{3,1},{4,6},{5,7},{6,4},{7,5},{8,10},{9,11},{10,... | collective-permute-start | bytes 393224 | tf_op jit(solution)/shard_map/ppermute | solution.py:120
  19.6 9.3 %collective-permute-start.10 = (bf16[256,512]{1,0:T(8,128)(2,1)S(1)}, bf16[256,512]{1,0:T(8,128)(2,1)S(1)}, u32[]{:S(2)}, u32[]{:S(2)}) collective-permute-start(bf16[256,512]{1,0:T(8,128)(2,1)S(1)} %get-tuple-element.48), channel_id=1, source_target_pairs={{0,4},{1,5},{2,6},{3,7},{4,8},{5,9},{6,10},{7,11},{8,12},{9,13},{1... | collective-permute-start | bytes 786440 | tf_op jit(solution)/shard_map/ppermute | solution.py:123
  23.9 12.1 %collective-permute-start.11 = (bf16[256,512]{1,0:T(8,128)(2,1)S(1)}, bf16[256,512]{1,0:T(8,128)(2,1)S(1)}, u32[]{:S(2)}, u32[]{:S(2)}) collective-permute-start(bf16[256,512]{1,0:T(8,128)(2,1)S(1)} %get-tuple-element.51), channel_id=1, source_target_pairs={{4,0},{5,1},{6,2},{7,3},{8,4},{9,5},{10,6},{11,7},{12,8},{13,9},{1... | collective-permute-start | bytes 786440 | tf_op jit(solution)/shard_map/ppermute | solution.py:123
  25.2 1.0 %copy-start.5 = (bf16[256,512]{1,0:T(8,128)(2,1)S(1)}, bf16[256,512]{1,0:T(8,128)(2,1)}, u32[]{:S(2)}) copy-start(bf16[256,512]{1,0:T(8,128)(2,1)} %constant.53.clone.refs_4_.refs_2_) | copy-start | bytes 786436
  25.2 1.0 %copy-start.6 = (bf16[256,512]{1,0:T(8,128)(2,1)S(1)}, bf16[256,512]{1,0:T(8,128)(2,1)}, u32[]{:S(2)}) copy-start(bf16[256,512]{1,0:T(8,128)(2,1)} %constant.52.clone.refs_3_.refs_1_) | copy-start | bytes 786436
  25.2 1.1 %copy-start.9 = (bf16[512,256]{1,0:T(8,128)(2,1)S(1)}, bf16[512,256]{1,0:T(8,128)(2,1)}, u32[]{:S(2)}) copy-start(bf16[512,256]{1,0:T(8,128)(2,1)} %constant.55.clone.refs_2_) | copy-start | bytes 786436
  25.2 1.2 %copy-start.10 = (bf16[512,256]{1,0:T(8,128)(2,1)S(1)}, bf16[512,256]{1,0:T(8,128)(2,1)}, u32[]{:S(2)}) copy-start(bf16[512,256]{1,0:T(8,128)(2,1)} %constant.54.clone.refs_1_) | copy-start | bytes 786436
  28.2 11.1 %collective-permute-start.9 = (bf16[256,512]{1,0:T(8,128)(2,1)S(1)}, bf16[256,512]{1,0:T(8,128)(2,1)S(1)}, u32[]{:S(2)}, u32[]{:S(2)}) collective-permute-start(bf16[256,512]{1,0:T(8,128)(2,1)S(1)} %get-tuple-element.47), channel_id=1, source_target_pairs={{0,2},{1,3},{2,0},{3,1},{4,6},{5,7},{6,4},{7,5},{8,10},{9,11},{10,... | collective-permute-start | bytes 786440 | tf_op jit(solution)/shard_map/ppermute | solution.py:120
  30.8 11.0 %collective-permute-start.14 = (bf16[64,512]{1,0:T(8,128)(2,1)S(1)}, bf16[64,512]{1,0:T(8,128)(2,1)S(1)}, u32[]{:S(2)}, u32[]{:S(2)}) collective-permute-start(bf16[64,512]{1,0:T(8,128)(2,1)S(1)} %get-tuple-element.56), channel_id=1, source_target_pairs={{0,4},{1,5},{2,6},{3,7},{4,0},{5,1},{6,2},{7,3},{8,12},{9,13},{10,... | collective-permute-start | bytes 196616 | tf_op jit(solution)/shard_map/ppermute | solution.py:120
  33.5 8.2 %collective-permute-start.15 = (bf16[64,512]{1,0:T(8,128)(2,1)S(1)}, bf16[64,512]{1,0:T(8,128)(2,1)S(1)}, u32[]{:S(2)}, u32[]{:S(2)}) collective-permute-start(bf16[64,512]{1,0:T(8,128)(2,1)S(1)} %get-tuple-element.57), channel_id=1, source_target_pairs={{0,8},{1,9},{2,10},{3,11},{4,12},{5,13},{6,14},{7,15},{8,0},{9,1},... | collective-permute-start | bytes 196616 | tf_op jit(solution)/shard_map/ppermute | solution.py:120
  35.7 6.1 %collective-permute-start.16 = (bf16[64,512]{1,0:T(8,128)(2,1)S(1)}, bf16[64,512]{1,0:T(8,128)(2,1)S(1)}, u32[]{:S(2)}, u32[]{:S(2)}) collective-permute-start(bf16[64,512]{1,0:T(8,128)(2,1)S(1)} %get-tuple-element.58), channel_id=1, source_target_pairs={{0,12},{1,13},{2,14},{3,15},{4,8},{5,9},{6,10},{7,11},{8,4},{9,5},... | collective-permute-start | bytes 196616 | tf_op jit(solution)/shard_map/ppermute | solution.py:120
  37.8 9.1 %collective-permute-start.12 = (bf16[256,512]{1,0:T(8,128)(2,1)S(1)}, bf16[256,512]{1,0:T(8,128)(2,1)S(1)}, u32[]{:S(2)}, u32[]{:S(2)}) collective-permute-start(bf16[256,512]{1,0:T(8,128)(2,1)S(1)} %get-tuple-element.52), channel_id=1, source_target_pairs={{0,2},{1,3},{2,0},{3,1},{4,6},{5,7},{6,4},{7,5},{8,10},{9,11},{10,... | collective-permute-start | bytes 786440 | tf_op jit(solution)/shard_map/ppermute | solution.py:120
  41.7 2.3 %collective-permute-start.13 = (bf16[384,512]{1,0:T(8,128)(2,1)S(1)}, bf16[384,512]{1,0:T(8,128)(2,1)S(1)}, u32[]{:S(2)}, u32[]{:S(2)}) collective-permute-start(bf16[384,512]{1,0:T(8,128)(2,1)S(1)} %shard_map.151), channel_id=1, source_target_pairs={{0,1},{1,0},{2,3},{3,2},{4,5},{5,4},{6,7},{7,6},{8,9},{9,8},{10,11... | collective-permute-start | bytes 1179656 | tf_op jit(solution)/shard_map/ppermute | solution.py:120
  41.8 2.2 %copy-start = (bf16[128,2048]{1,0:T(8,128)(2,1)S(1)}, bf16[128,2048]{1,0:T(8,128)(2,1)}, u32[]{:S(2)}) copy-start(bf16[128,2048]{1,0:T(8,128)(2,1)} %refs_6_.3) | copy-start | bytes 1572868
  41.8 2.2 %copy-start.1 = (bf16[128,2048]{1,0:T(8,128)(2,1)S(1)}, bf16[128,2048]{1,0:T(8,128)(2,1)}, u32[]{:S(2)}) copy-start(bf16[128,2048]{1,0:T(8,128)(2,1)} %refs_7_.1) | copy-start | bytes 1572868
  42.4 4.5 %collective-permute-start.17 = (f32[32,512]{1,0:T(8,128)S(1)}, f32[32,512]{1,0:T(8,128)S(1)}, u32[]{:S(2)}, u32[]{:S(2)}) collective-permute-start(f32[32,512]{1,0:T(8,128)S(1)} %get-tuple-element.61), channel_id=1, source_target_pairs={{0,2},{1,3},{2,0},{3,1},{4,6},{5,7},{6,4},{7,5},{8,10},{9,11},{10,... | collective-permute-start | bytes 196616 | tf_op jit(solution)/shard_map/ppermute | solution.py:120
  47.0 1.5 %collective-permute-start.18 = (bf16[128,512]{1,0:T(8,128)(2,1)S(1)}, bf16[128,512]{1,0:T(8,128)(2,1)S(1)}, u32[]{:S(2)}, u32[]{:S(2)}) collective-permute-start(bf16[128,512]{1,0:T(8,128)(2,1)S(1)} %get-tuple-element.64), channel_id=1, source_target_pairs={{0,1},{1,0},{2,3},{3,2},{4,5},{5,4},{6,7},{7,6},{8,9},{9,8},{10,11... | collective-permute-start | bytes 393224 | tf_op jit(solution)/shard_map/ppermute | solution.py:120
  47.0 1.4 %collective-permute-start.19 = (f32[32,512]{1,0:T(8,128)S(1)}, f32[32,512]{1,0:T(8,128)S(1)}, u32[]{:S(2)}, u32[]{:S(2)}) collective-permute-start(f32[32,512]{1,0:T(8,128)S(1)} %get-tuple-element.66), channel_id=1, source_target_pairs={{0,1},{1,0},{2,3},{3,2},{4,5},{5,4},{6,7},{7,6},{8,9},{9,8},{10,11... | collective-permute-start | bytes 196616 | tf_op jit(solution)/shard_map/ppermute | solution.py:120

commit v2 on v1

--- a/solution.py
+++ b/solution.py
@@ -37,8 +37,7 @@
 def restore(high, low, real, imag):
     spec = jnp.concatenate([real, imag], 0)
     top = spec.astype(jnp.bfloat16)
-    rest = (spec - top.astype(jnp.float32)).astype(jnp.bfloat16)
-    return dot(high[...], top) + dot(low[...], top) + dot(high[...], rest)
+    return dot(high[...], top) + dot(low[...], top)
 
 
 def parts(spec):
@@ -67,16 +66,25 @@
     return left[0] * right[0] + left[1] * right[1], left[1] * right[0] - left[0] * right[1]
 
 
+class Here:
+    def __getitem__(self, index):
+        me = lax.axis_index("seq")
+        return me // PLANE if index else me % PLANE
+
+
 def call(body, outs, args, scratch=(), spaces=None, after=(), flops=1, aliases=()):
+    located = args[0] is None
+    args = args[1:] if located else args
     specs = [
-        pl.BlockSpec(memory_space=pltpu.SMEM if a.ndim == 1 else pltpu.VMEM) for a in args
+        pl.BlockSpec(memory_space=pltpu.VMEM) for _ in args
     ]
     after = [*after, *aliases]
     specs += [pl.BlockSpec(memory_space=pl.ANY)] * len(after)
     base = len(args) + len(after) - len(aliases)
 
     def run(*refs):
-        body(*refs[: len(args)], *refs[len(args) + len(after) :])
+        first = [Here()] if located else []
+        body(*first, *refs[: len(args)], *refs[len(args) + len(after) :])
 
     spaces = spaces or [pltpu.VMEM] * len(outs)
     return pl.pallas_call(
@@ -105,7 +113,6 @@
     column = planes * pad_taps
     assert tokens == 2 * taps
     me = lax.axis_index("seq")
-    place = jnp.stack([me % PLANE, me // PLANE]).astype(jnp.int32)
     devices = range(nseq)
 
     forward, inverse = tables(taps)
@@ -113,8 +120,11 @@
     inv = pair(inverse)
     lag_of = np.full((planes * PLANE, pad_taps), -1)
     lag_of[:, :own_taps] = np.arange(taps).reshape(planes * PLANE, own_taps)
-    lag_of = lag_of.reshape(planes, PLANE, pad_taps).transpose(1, 0, 2).reshape(-1)
-    fwd_lag = pair(np.where(lag_of[None, :] >= 0, forward[:, np.maximum(lag_of, 0)], 0.0))
+    lag_of = lag_of.reshape(-1)
+    if pad_taps == own_taps:
+        fwd_lag = fwd
+    else:
+        fwd_lag = pair(np.where(lag_of[None, :] >= 0, forward[:, np.maximum(lag_of, 0)], 0.0))
 
     def swap(array, distance):
         return lax.ppermute(array, "seq", [(i, i ^ distance) for i in devices])
@@ -131,19 +141,29 @@
         return pl.ds(pl.multiple_of(index * size, size), size)
 
     def lay_taps(place_ref, *refs):
-        ins, (keep, side, full) = refs[:planes], refs[planes:]
+        ins, (keep, ship) = refs[:planes], refs[planes:]
         q, z = place_ref[0], place_ref[1]
         for step in range(planes):
-            full[block_at(z ^ step, pad_taps)] = ins[step][...]
-        for step, (out, half) in enumerate(((keep, 0), (side, 0), (keep, 1), (side, 1))):
-            out[half * column : (half + 1) * column] = full[:, block_at(q ^ step, width)]
-
-    def narrow_taps(taps_ref, out):
-        out[:own_taps] = taps_ref[...].astype(bf16)
+            for core in range(2):
+                at = block_at(2 * (z ^ step) + (q % 2 ^ core), pad_taps)
+                first = 2 * core * pad_taps
+                keep[at] = ins[step][first : first + pad_taps]
+                ship[at] = ins[step][first + pad_taps : first + 2 * pad_taps]
+
+    def taps_block(taps_ref, at):
+        block = taps_ref[:, at]
         if pad_taps > own_taps:
-            out[own_taps:] = jnp.zeros((pad_taps - own_taps, channels), bf16)
-
-    def gate_grad(place_ref, o_ref, q_ref, p_ref, keep, side):
+            fill = jnp.zeros((pad_taps - own_taps, width), f32)
+            block = jnp.concatenate([block, fill], 0)
+        return block.astype(bf16)
+
+    def pack_taps(place_ref, taps_ref, near_ref, out):
+        q = place_ref[0]
+        out[:pad_taps] = taps_block(taps_ref, block_at(q, width))
+        out[pad_taps : 2 * pad_taps] = taps_block(taps_ref, block_at(q ^ 2, width))
+        out[2 * pad_taps :] = near_ref[3 * rows :]
+
+    def gate_grad(place_ref, o_ref, q_ref, p_ref, taps_ref, keep, side):
         q = place_ref[0]
         side[:rows] = p_ref[...]
         for step, (out, first) in enumerate(((keep, 0), (side, rows), (keep, rows), (side, 2 * rows))):
@@ -151,11 +171,14 @@
             out[first : first + rows] = (
                 o_ref[:, at].astype(f32) * q_ref[:, at].astype(f32)
             ).astype(bf16)
+        for n, step in enumerate((1, 3)):
+            first = 3 * rows + n * pad_taps
+            side[first : first + pad_taps] = taps_block(taps_ref, block_at(q ^ step, width))
 
     def join(left, right, after=(), flops=1):
         def body(left_ref, right_ref, out):
-            out[:rows] = left_ref[left.shape[0] - rows :]
-            out[rows:] = right_ref[right.shape[0] - rows :]
+            out[:rows] = left_ref[rows : 2 * rows]
+            out[rows:] = right_ref[2 * rows : 3 * rows]
 
         return call(body, [struct(2 * rows, width, bf16)], [left, right], after=after, flops=flops)[0]
 
@@ -165,10 +188,6 @@
         for step in range(PLANE):
             product[block_at(q ^ step, rows)] = ins[step][:rows]
         top[...] = product[tokens - taps :]
-
-    def join_taps(keep, near, ship):
-        ship[:column] = keep[column:]
-        ship[column:] = near[column:]
 
     def gather_grad(place_ref, keep, near, far, grad, bottom):
         q = place_ref[0]
@@ -196,24 +215,37 @@
             block = full[block_at(place_ref[1] ^ step, plane_taps)]
             outs[step][...] = block.astype(outs[step].dtype)
 
-    def signal(inv_refs, taps_spec, near, far, sign):
-        real, imag = parts(taps_spec)
-        value = times((real, sign * imag), window(near, far, sign))
+    def mixed_of(inv_refs, taps_spec, near, far):
+        value = times(parts(taps_spec), window(near[...], far[...], 1.0))
         return restore(*inv_refs, *value).astype(bf16)
 
+    def corr_of(inv_refs, taps_spec, near, far):
+        value = times_conj(window(near[...], far[...], -1.0), parts(taps_spec))
+        return restore(*inv_refs, *value).astype(bf16)
+
+    def by_side(q, left, right):
+        pl.when(q < 2)(left)
+        pl.when(q >= 2)(right)
+
     def inner(place_ref, high, low, inv_high, inv_low, p0, p1, g0, g1, *refs):
-        keep, near_taps, far_taps, spec, ship, filt, held = refs
-        q = place_ref[0]
-        filt[block_at(q, column)] = keep[:column]
-        filt[block_at(q ^ 1, column)] = near_taps[:column]
-        filt[block_at(q ^ 2, column)] = far_taps[:column]
-        filt[block_at(q ^ 3, column)] = far_taps[column:]
+        keep, far_taps, spec, ship, filt, held = refs
+        q = place_ref[0]
+        chip = 2 * pad_taps
+        for z in range(planes):
+            at = slice(z * chip, (z + 1) * chip)
+            filt[block_at(2 * z + q // 2, chip)] = keep[at]
+            filt[block_at(2 * z + 1 - q // 2, chip)] = far_taps[at]
         taps_spec = spectrum(high, low, filt[...])
         spec[...] = taps_spec
-        left = q < 2
-        near = jnp.where(left, p1[...], g0[...])
-        far = jnp.where(left, p0[...], g1[...])
-        held[...] = signal((inv_high, inv_low), taps_spec, near, far, jnp.where(left, 1.0, -1.0))
+        inv_refs = (inv_high, inv_low)
+
+        def left():
+            held[...] = mixed_of(inv_refs, spec[...], p1, p0)
+
+        def right():
+            held[...] = corr_of(inv_refs, spec[...], g0, g1)
+
+        by_side(q, left, right)
         ship[:rows] = held[block_at(q % 2, rows)]
         ship[rows:] = held[block_at(1 - q % 2, rows)]
 
@@ -222,29 +254,32 @@
         q = place_ref[0]
         ahead = spectrum(high, low, halo[...])
         spec[...] = ahead
-        left = q < 2
-        near = jnp.where(left, g1[...], p0[...])
-        far = jnp.where(left, ahead, behind[...])
-        sign = jnp.where(left, -1.0, 1.0)
-        held[...] = signal((inv_high, inv_low), taps_ref[...], near, far, sign)
+        inv_refs = (inv_high, inv_low)
+
+        def left():
+            held[...] = corr_of(inv_refs, taps_ref[...], g1, spec)
+
+        def right():
+            held[...] = mixed_of(inv_refs, taps_ref[...], p0, behind)
+
+        by_side(q, left, right)
         ship[:rows] = held[block_at(q % 2, rows)]
         ship[rows:] = held[block_at(1 - q % 2, rows)]
 
     def kept(place_ref, inv_high, inv_low, p0, p1, g0, g1, behind, ahead, taps_ref, *refs):
         mixed_own, corr_own, side, held = refs
         q = place_ref[0]
-        left = q < 2
         inv_refs = (inv_high, inv_low)
-        near = jnp.where(left, p0[...], p1[...])
-        far = jnp.where(left, behind[...], p0[...])
-        held[...] = signal(inv_refs, taps_ref[...], near, far, 1.0)
-        mixed_own[...] = held[block_at(q % 2, rows)]
-        side[:rows] = held[block_at(1 - q % 2, rows)]
-        near = jnp.where(left, g0[...], g1[...])
-        far = jnp.where(left, g1[...], ahead[...])
-        held[...] = signal(inv_refs, taps_ref[...], near, far, -1.0)
-        corr_own[...] = held[block_at(q % 2, rows)]
-        side[rows:] = held[block_at(1 - q % 2, rows)]
+
+        def run(p_near, p_far, g_near, g_far):
+            held[...] = mixed_of(inv_refs, taps_ref[...], p_near, p_far)
+            mixed_own[...] = held[block_at(q % 2, rows)]
+            side[:rows] = held[block_at(1 - q % 2, rows)]
+            held[...] = corr_of(inv_refs, taps_ref[...], g_near, g_far)
+            corr_own[...] = held[block_at(q % 2, rows)]
+            side[rows:] = held[block_at(1 - q % 2, rows)]
+
+        by_side(q, lambda: run(p0, behind, g0, g1), lambda: run(p1, p0, g1, ahead))
 
     def pick(ref, index):
         if own_taps % 8 == 0:
@@ -318,7 +353,7 @@
     halo = struct(taps, width, bf16)
 
     def product_block(step):
-        start = (place[0] ^ step) * width
+        start = (me % PLANE ^ step) * width
         left = lax.dynamic_slice_in_dim(keys, start, width, 1).astype(f32)
         right = lax.dynamic_slice_in_dim(values, start, width, 1).astype(f32)
         return (left * right).astype(bf16)
@@ -328,51 +363,43 @@
     keep, side = call(
         gate_grad,
         flops=1,
-        outs=[double, struct(3 * rows, width, bf16)],
-        args=[place, out_grad, queries, sent[1]],
+        outs=[double, struct(3 * rows + 2 * pad_taps, width, bf16)],
+        args=[None, out_grad, queries, sent[1], filter_taps],
         after=[],
     )
     near = swap(side, 1)
-    far = swap(join(keep, near, after=[far_p[1]], flops=1000000000), 2)
 
     product, top = call(
         gather_product,
         [struct(tokens, width, bf16), halo],
-        [place, sent[0], near, *far_p],
-        flops=1,
-    )
-    (narrow,) = call(
-        narrow_taps,
-        [struct(pad_taps, channels, bf16)],
-        [filter_taps],
-        after=[near],
-        flops=1,
-    )
-    far_taps = [swap(narrow, PLANE * step) for step in range(1, planes)]
-    taps_keep, taps_side = call(
+        [None, sent[0], near, *far_p],
+        flops=1,
+    )
+    p_spec = own_spectra(product, 1, [])
+    (packed,) = call(
+        pack_taps,
+        [struct(4 * pad_taps, width, bf16)],
+        [None, filter_taps, near],
+        after=[],
+        flops=1,
+    )
+    far_taps = [swap(packed, PLANE * step) for step in range(1, planes)]
+    far = swap(join(keep, near, after=[], flops=1000000000), 2)
+    taps_keep, taps_ship = call(
         lay_taps,
         [struct(2 * column, width, bf16)] * 2,
-        [place, narrow, *far_taps],
-        scratch=[pltpu.VMEM((column, channels), bf16)],
-        after=[product],
-        flops=1,
-    )
-    taps_near = swap(taps_side, 1)
-    (taps_ship,) = call(
-        join_taps,
-        [struct(2 * column, width, bf16)],
-        [taps_keep, taps_near],
-        flops=1,
+        [None, packed, *far_taps],
+        after=[p_spec[0]],
+        flops=1000000000,
     )
     taps_far = swap(taps_ship, 2)
 
     behind = shift(top, PLANE)
-    p_spec = own_spectra(product, 1, [])
 
     grad, bottom = call(
         gather_grad,
         [struct(tokens, width, bf16), halo],
-        [place, keep, near, far],
+        [None, keep, near, far],
         after=[taps_ship],
         flops=1,
     )
@@ -382,17 +409,17 @@
     taps_spec, ship = call(
         inner,
         [spectral, double],
-        [place, *fwd_lag, *inv, *p_spec, *g_spec, taps_keep, taps_near, taps_far],
+        [None, *fwd_lag, *inv, *p_spec, *g_spec, taps_keep, taps_far],
         scratch=[pltpu.VMEM((PLANE * column, width), bf16), pltpu.VMEM((taps, width), bf16)],
         after=[],
-        flops=10000000000,
+        flops=1,
     )
     first = swap(ship, 2)
     behind_spec, own_lags, *away = call(
         lags,
         [spectral, struct(plane_taps, width, f32)]
         + [struct(plane_taps, width, bf16)] * (planes - 1),
-        [place, *fwd, *inv, *p_spec, *g_spec, behind],
+        [None, *fwd, *inv, *p_spec, *g_spec, behind],
         scratch=[pltpu.VMEM((taps, width), f32)],
         after=[taps_spec],
         flops=1,
@@ -401,7 +428,7 @@
     ahead_spec, ship = call(
         outer,
         [spectral, double],
-        [place, *fwd, *inv, p_spec[0], g_spec[1], behind_spec, ahead, taps_spec],
+        [None, *fwd, *inv, p_spec[0], g_spec[1], behind_spec, ahead, taps_spec],
         scratch=[pltpu.VMEM((taps, width), bf16)],
         after=[taps_spec],
         flops=1,
@@ -410,7 +437,7 @@
     mixed_own, corr_own, side = call(
         kept,
         [block, block, double],
-        [place, *inv, *p_spec, *g_spec, behind_spec, ahead_spec, taps_spec],
+        [None, *inv, *p_spec, *g_spec, behind_spec, ahead_spec, taps_spec],
         scratch=[pltpu.VMEM((taps, width), bf16)],
         after=[first],
         flops=1,
@@ -424,7 +451,7 @@
     lag_own, lag_side, lag_ship = call(
         add_lags,
         [struct(own_taps, width, f32)] * 2 + [lag_double],
-        [place, own_lags, *away],
+        [None, own_lags, *away],
         scratch=[pltpu.VMEM((plane_taps, width), f32)],
         after=[corr_own],
         flops=10000000000,
@@ -434,7 +461,7 @@
     *partial, mark = call(
         finish_near,
         [whole] * 3 + [struct(8, 128, f32)],
-        [place, mixed_own, corr_own, near, out_grad, values, keys],
+        [None, mixed_own, corr_own, near, out_grad, values, keys],
         scratch=[
             pltpu.VMEM((3, 2, rows, width), bf16),
             pltpu.SemaphoreType.DMA((3, 2)),
@@ -454,7 +481,7 @@
     return call(
         finish_far,
         [whole] * 3 + [struct(own_taps, channels, f32)],
-        [place, first, second, near, last, out_grad, values, keys, lag_own, lag_near, lag_far],
+        [None, first, second, near, last, out_grad, values, keys, lag_own, lag_near, lag_far],
         scratch=[
             pltpu.VMEM((3, 2, rows, width), bf16),
             pltpu.VMEM((own_taps, channels), f32),

time: 50.2 us -> 44.2 us (0.88)
  Pallas kernels: 15.5 us -> 8.19 us
  waiting for transfers between devices: 6.37 us -> 7.74 us
  starting transfers between devices: 25.1 us -> 23.9 us
  local copies, waits for them, and re-layouts: 0.57 us -> 1.69 us
    pallas_call x18 -> x17, Pallas kernels: 15.5 us -> 8.19 us  [call(): pl.pallas_call(run, out_shape=outs, in_specs=specs, out_specs=[pl.BlockSp...]
    ppermute x18 -> x17, starting transfers between devices: 20.8 us -> 19.6 us  [swap(): return lax.ppermute(array, 'seq', [(i, i ^ distance) for i in devices])]
    unnamed x22 -> x18, local copies, waits for them, and re-layouts: 0.57 us -> 1.69 us
    ppermute x18 -> x17, waiting for transfers between devices: 6.37 us -> 7.33 us  [swap(): return lax.ppermute(array, 'seq', [(i, i ^ distance) for i in devices])]
  transfers between devices with their start and end apart: 20 -> 19, of which waited for: 5 -> 7; matrix products, arithmetic and copies ran while one was open for 0% -> 0% of each run, Pallas kernels for 27% -> 16%
where the time goes in v2:
time: 44.2 us; the launch traced here: 43.9 us
  starting transfers between devices  23.9 us (54%)
  Pallas kernels  8.19 us (19%)
  waiting for transfers between devices  7.74 us (18%)
  local copies, waits for them, and re-layouts  1.69 us (4%)
  other arithmetic  1.52 us (3%)
  between operations  0.91 us (2%)
    ppermute x17, starting transfers between devices, swap(): return lax.ppermute(array, 'seq', [(i, i ^ distance) for i in devices])  19.6 us
    pallas_call x17, Pallas kernels, call(): pl.pallas_call(run, out_shape=outs, in_specs=specs, out_specs=[pl.BlockSp...  8.19 us
    ppermute x17, waiting for transfers between devices, swap(): return lax.ppermute(array, 'seq', [(i, i ^ distance) for i in devices])  7.33 us
    ppermute x2, starting transfers between devices, shift(): lax.ppermute(array, 'seq', [(i, i + distance) for i in devices if i + dis...  4.25 us
    unnamed x18, local copies, waits for them, and re-layouts  1.69 us
    convert_element_type x1, other arithmetic, product_block(): return (left * right).astype(bf16)  1.52 us
  transfers between devices with their start and end apart: 19, of which 7 were waited for; matrix products, arithmetic and copies ran while one was open for 0% of the time, Pallas kernels for 16%

profile of v2, /device:TPU:0, one launch (start us, length us, event | category | flops | bytes accessed | tf_op | source)
XLA Modules:
  0.0 43.9 jit_solution(17580381652319523110)
XLA Ops:
  0.7 1.5 %multiply_convert_fusion = (bf16[128,512]{1,0:T(8,128)(2,1)S(1)}, bf16[128,512]{1,0:T(8,128)(2,1)S(1)}, bf16[128,512]{1,0:T(8,128)(2,1)S(1)}, bf16[128,512]{1,0:T(8,128)(2,1)S(1)}) fusion(bf16[128,2048]{1,0:T(8,128)(2,1)} %refs_5_.3, s32[]{:T(128)S(6)} %select_n.33, bf16[128,2048]{1,0:T(8,128)(2,1)} %refs_6_.1, s32[]{:T(128)S(6)} %select_n.32, ...), kind=kLoop, calls=%fused_computation | loop fusion | flops 1048576 | bytes 1572880 | tf_op jit(solution)/shard_map/convert_element_type | solution.py:359
  2.2 0.1 copy-done.8
  2.3 0.1 shard_map.120
  2.5 0.5 %collective-permute-start = (bf16[416,512]{1,0:T(8,128)(2,1)S(1)}, bf16[416,512]{1,0:T(8,128)(2,1)S(1)}, u32[]{:S(2)}, u32[]{:S(2)}) collective-permute-start(bf16[416,512]{1,0:T(8,128)(2,1)S(1)} %get-tuple-element.37), channel_id=1, source_target_pairs={{0,1},{1,0},{2,3},{3,2},{4,5},{5,4},{6,7},{7,6},{8,9},{9,8},{10,11... | collective-permute-start | bytes 1277960 | tf_op jit(solution)/shard_map/ppermute | solution.py:130
  3.0 2.6 %collective-permute-start.2 = (bf16[128,512]{1,0:T(8,128)(2,1)S(1)}, bf16[128,512]{1,0:T(8,128)(2,1)S(1)}, u32[]{:S(2)}, u32[]{:S(2)}) collective-permute-start(bf16[128,512]{1,0:T(8,128)(2,1)S(1)} %get-tuple-element.70), channel_id=1, source_target_pairs={{0,3},{1,2},{2,1},{3,0},{4,7},{5,6},{6,5},{7,4},{8,11},{9,10},{10,... | collective-permute-start | bytes 393224 | tf_op jit(solution)/shard_map/ppermute | solution.py:130
  5.6 0.0 collective-permute-start.1
  5.6 0.0 collective-permute-done.refs_1_
  5.7 4.2 %collective-permute-start.6 = (bf16[64,512]{1,0:T(8,128)(2,1)S(1)}, bf16[64,512]{1,0:T(8,128)(2,1)S(1)}, u32[]{:S(2)}, u32[]{:S(2)}) collective-permute-start(bf16[64,512]{1,0:T(8,128)(2,1)S(1)} %shard_map.124.refs_0_), channel_id=1, source_target_pairs={{0,12},{1,13},{2,14},{3,15},{4,8},{5,9},{6,10},{7,11},{8,4},{9,5},... | collective-permute-start | bytes 196616 | tf_op jit(solution)/shard_map/ppermute | solution.py:130
  9.8 0.0 collective-permute-start.5
  9.8 0.6 %collective-permute-start.4 = (bf16[64,512]{1,0:T(8,128)(2,1)S(1)}, bf16[64,512]{1,0:T(8,128)(2,1)S(1)}, u32[]{:S(2)}, u32[]{:S(2)}) collective-permute-start(bf16[64,512]{1,0:T(8,128)(2,1)S(1)} %shard_map.124.refs_0_), channel_id=1, source_target_pairs={{0,4},{1,5},{2,6},{3,7},{4,0},{5,1},{6,2},{7,3},{8,12},{9,13},{10,... | collective-permute-start | bytes 196616 | tf_op jit(solution)/shard_map/ppermute | solution.py:130
  10.5 1.7 %collective-permute-start.3 = (bf16[256,512]{1,0:T(8,128)(2,1)S(1)}, bf16[256,512]{1,0:T(8,128)(2,1)S(1)}, u32[]{:S(2)}, u32[]{:S(2)}) collective-permute-start(bf16[256,512]{1,0:T(8,128)(2,1)S(1)} %shard_map.123), channel_id=1, source_target_pairs={{0,2},{1,3},{2,0},{3,1},{4,6},{5,7},{6,4},{7,5},{8,10},{9,11},{10,... | collective-permute-start | bytes 786440 | tf_op jit(solution)/shard_map/ppermute | solution.py:130
  12.2 0.3 collective-permute-done.1.refs_2_
  12.4 0.1 shard_map.121
  12.5 0.9 %copy-done = bf16[512,256]{1,0:T(8,128)(2,1)S(1)} copy-done((bf16[512,256]{1,0:T(8,128)(2,1)S(1)}, bf16[512,256]{1,0:T(8,128)(2,1)}, u32[]{:S(2)}) %copy-start) | copy-done | bytes 262168
  13.4 0.1 copy-done.1
  13.5 0.7 %shard_map.122 = (f32[512,512]{1,0:T(8,128)S(1)}, f32[512,512]{1,0:T(8,128)S(1)}) custom-call(bf16[512,256]{1,0:T(8,128)(2,1)S(1)} %copy-done.1, bf16[512,256]{1,0:T(8,128)(2,1)S(1)} %copy-done, bf16[512,512]{1,0:T(8,128)(2,1)S(1)} %get-tuple-element.38.refs_2_), custom_call_target="tpu_custom_call" | custom-call | flops 1 | bytes 1 | tf_op jit(solution)/shard_map/pallas_call | solution.py:90
  14.2 1.2 %collective-permute-done.5.refs_2_ = bf16[64,512]{1,0:T(8,128)(2,1)S(1)} collective-permute-done((bf16[64,512]{1,0:T(8,128)(2,1)S(1)}, bf16[64,512]{1,0:T(8,128)(2,1)S(1)}, u32[]{:S(2)}, u32[]{:S(2)}) %collective-permute-start.5) | collective-permute-done | bytes 65568 | tf_op jit(solution)/shard_map/ppermute | solution.py:130
  15.4 1.6 %collective-permute-start.7 = (bf16[128,512]{1,0:T(8,128)(2,1)S(1)}, bf16[128,512]{1,0:T(8,128)(2,1)S(1)}, u32[]{:S(2)}, u32[]{:S(2)}) collective-permute-start(bf16[128,512]{1,0:T(8,128)(2,1)S(1)} %get-tuple-element.42.refs_3_), channel_id=1, source_target_pairs={{0,2},{1,3},{2,0},{3,1},{4,6},{5,7},{6,4},{7,5},{8,10},{9,11},{10,... | collective-permute-start | bytes 393224 | tf_op jit(solution)/shard_map/ppermute | solution.py:130
  17.0 3.0 %collective-permute-start.9 = (bf16[256,512]{1,0:T(8,128)(2,1)S(1)}, bf16[256,512]{1,0:T(8,128)(2,1)S(1)}, u32[]{:S(2)}, u32[]{:S(2)}) collective-permute-start(bf16[256,512]{1,0:T(8,128)(2,1)S(1)} %get-tuple-element.48), channel_id=1, source_target_pairs={{0,4},{1,5},{2,6},{3,7},{4,8},{5,9},{6,10},{7,11},{8,12},{9,13},{1... | collective-permute-start | bytes 786440 | tf_op jit(solution)/shard_map/ppermute | solution.py:133
  20.0 0.1 shard_map.126
  20.1 1.3 %collective-permute-start.10 = (bf16[256,512]{1,0:T(8,128)(2,1)S(1)}, bf16[256,512]{1,0:T(8,128)(2,1)S(1)}, u32[]{:S(2)}, u32[]{:S(2)}) collective-permute-start(bf16[256,512]{1,0:T(8,128)(2,1)S(1)} %get-tuple-element.51), channel_id=1, source_target_pairs={{4,0},{5,1},{6,2},{7,3},{8,4},{9,5},{10,6},{11,7},{12,8},{13,9},{1... | collective-permute-start | bytes 786440 | tf_op jit(solution)/shard_map/ppermute | solution.py:133
  21.4 0.0 copy-start.5
  21.4 0.0 copy-start.6
  21.4 0.7 %shard_map.127 = (f32[512,512]{1,0:T(8,128)S(1)}, f32[512,512]{1,0:T(8,128)S(1)}) custom-call(bf16[512,256]{1,0:T(8,128)(2,1)S(1)} %copy-done.1, bf16[512,256]{1,0:T(8,128)(2,1)S(1)} %copy-done, bf16[512,512]{1,0:T(8,128)(2,1)S(1)} %get-tuple-element.43.refs_2_), custom_call_target="tpu_custom_call" | custom-call | flops 1 | bytes 1 | tf_op jit(solution)/shard_map/pallas_call | solution.py:90
  22.1 0.2 copy-done.5
  22.3 0.1 copy-done.6
  22.4 1.1 %shard_map.128 = (f32[512,512]{1,0:T(8,128)S(1)}, bf16[256,512]{1,0:T(8,128)(2,1)S(1)}) custom-call(bf16[512,256]{1,0:T(8,128)(2,1)S(1)} %copy-done.1, bf16[512,256]{1,0:T(8,128)(2,1)S(1)} %copy-done, bf16[256,512]{1,0:T(8,128)(2,1)S(1)} %copy-done.6, bf16[256,512]{1,0:T(8,128)(2,1)S(1)} %copy-done.5, f32[512,512]{1,0:T(8,128)S(1)} %get-tuple-element.39.refs_4_.refs_2_, ...), custom_call_target="tpu_custom_call" | custom-call | flops 1 | bytes 1 | tf_op jit(solution)/shard_map/pallas_call | solution.py:90
  23.5 0.6 %collective-permute-start.8 = (bf16[256,512]{1,0:T(8,128)(2,1)S(1)}, bf16[256,512]{1,0:T(8,128)(2,1)S(1)}, u32[]{:S(2)}, u32[]{:S(2)}) collective-permute-start(bf16[256,512]{1,0:T(8,128)(2,1)S(1)} %get-tuple-element.47), channel_id=1, source_target_pairs={{0,2},{1,3},{2,0},{3,1},{4,6},{5,7},{6,4},{7,5},{8,10},{9,11},{10,... | collective-permute-start | bytes 786440 | tf_op jit(solution)/shard_map/ppermute | solution.py:130
  24.1 0.4 collective-permute-done.9.refs_8_
  24.5 1.1 %shard_map.129 = (f32[512,512]{1,0:T(8,128)S(1)}, f32[64,512]{1,0:T(8,128)S(1)}, bf16[64,512]{1,0:T(8,128)(2,1)S(1)}, bf16[64,512]{1,0:T(8,128)(2,1)S(1)}, bf16[64,512]{1,0:T(8,128)(2,1)S(1)}) custom-call(bf16[512,256]{1,0:T(8,128)(2,1)S(1)} %copy-done.1, bf16[512,256]{1,0:T(8,128)(2,1)S(1)} %copy-done, bf16[256,512]{1,0:T(8,128)(2,1)S(1)} %copy-done.6, ...), custom_call_target="tpu_custom_call" | custom-call | flops 1 | bytes 1 | tf_op jit(solution)/shard_map/pallas_call | solution.py:90
  25.6 2.5 %collective-permute-start.13 = (bf16[64,512]{1,0:T(8,128)(2,1)S(1)}, bf16[64,512]{1,0:T(8,128)(2,1)S(1)}, u32[]{:S(2)}, u32[]{:S(2)}) collective-permute-start(bf16[64,512]{1,0:T(8,128)(2,1)S(1)} %get-tuple-element.56), channel_id=1, source_target_pairs={{0,4},{1,5},{2,6},{3,7},{4,0},{5,1},{6,2},{7,3},{8,12},{9,13},{10,... | collective-permute-start | bytes 196616 | tf_op jit(solution)/shard_map/ppermute | solution.py:130
  28.2 2.7 %collective-permute-start.14 = (bf16[64,512]{1,0:T(8,128)(2,1)S(1)}, bf16[64,512]{1,0:T(8,128)(2,1)S(1)}, u32[]{:S(2)}, u32[]{:S(2)}) collective-permute-start(bf16[64,512]{1,0:T(8,128)(2,1)S(1)} %get-tuple-element.57), channel_id=1, source_target_pairs={{0,8},{1,9},{2,10},{3,11},{4,12},{5,13},{6,14},{7,15},{8,0},{9,1},... | collective-permute-start | bytes 196616 | tf_op jit(solution)/shard_map/ppermute | solution.py:130
  30.9 0.0 collective-permute-start.15
  30.9 1.1 %shard_map.130 = (f32[512,512]{1,0:T(8,128)S(1)}, bf16[256,512]{1,0:T(8,128)(2,1)S(1)}) custom-call(bf16[512,256]{1,0:T(8,128)(2,1)S(1)} %copy-done.1, bf16[512,256]{1,0:T(8,128)(2,1)S(1)} %copy-done, bf16[256,512]{1,0:T(8,128)(2,1)S(1)} %copy-done.6, bf16[256,512]{1,0:T(8,128)(2,1)S(1)} %copy-done.5, f32[512,512]{1,0:T(8,128)S(1)} %get-tuple-element.39.refs_4_.refs_2_, ...), custom_call_target="tpu_custom_call" | custom-call | flops 1 | bytes 1 | tf_op jit(solution)/shard_map/pallas_call | solution.py:90
  32.0 1.0 %collective-permute-start.11 = (bf16[256,512]{1,0:T(8,128)(2,1)S(1)}, bf16[256,512]{1,0:T(8,128)(2,1)S(1)}, u32[]{:S(2)}, u32[]{:S(2)}) collective-permute-start(bf16[256,512]{1,0:T(8,128)(2,1)S(1)} %get-tuple-element.52), channel_id=1, source_target_pairs={{0,2},{1,3},{2,0},{3,1},{4,6},{5,7},{6,4},{7,5},{8,10},{9,11},{10,... | collective-permute-start | bytes 786440 | tf_op jit(solution)/shard_map/ppermute | solution.py:130
  33.0 1.1 %shard_map.131 = (bf16[128,512]{1,0:T(8,128)(2,1)S(1)}, bf16[128,512]{1,0:T(8,128)(2,1)S(1)}, bf16[256,512]{1,0:T(8,128)(2,1)S(1)}) custom-call(bf16[256,512]{1,0:T(8,128)(2,1)S(1)} %copy-done.6, bf16[256,512]{1,0:T(8,128)(2,1)S(1)} %copy-done.5, f32[512,512]{1,0:T(8,128)S(1)} %get-tuple-element.39.refs_4_.refs_2_, ...), custom_call_target="tpu_custom_call" | custom-call | flops 1 | bytes 1 | tf_op jit(solution)/shard_map/pallas_call | solution.py:90
  34.2 0.1 collective-permute-start.12
  34.2 0.5 %collective-permute-done.14.refs_2_ = bf16[64,512]{1,0:T(8,128)(2,1)S(1)} collective-permute-done((bf16[64,512]{1,0:T(8,128)(2,1)S(1)}, bf16[64,512]{1,0:T(8,128)(2,1)S(1)}, u32[]{:S(2)}, u32[]{:S(2)}) %collective-permute-start.14) | collective-permute-done | bytes 65568 | tf_op jit(solution)/shard_map/ppermute | solution.py:130
  34.8 2.2 %collective-permute-done.15.refs_3_ = bf16[64,512]{1,0:T(8,128)(2,1)S(1)} collective-permute-done((bf16[64,512]{1,0:T(8,128)(2,1)S(1)}, bf16[64,512]{1,0:T(8,128)(2,1)S(1)}, u32[]{:S(2)}, u32[]{:S(2)}) %collective-permute-start.15) | collective-permute-done | bytes 65568 | tf_op jit(solution)/shard_map/ppermute | solution.py:130
  37.0 0.8 %collective-permute-start.16 = (f32[32,512]{1,0:T(8,128)S(1)}, f32[32,512]{1,0:T(8,128)S(1)}, u32[]{:S(2)}, u32[]{:S(2)}) collective-permute-start(f32[32,512]{1,0:T(8,128)S(1)} %get-tuple-element.61), channel_id=1, source_target_pairs={{0,2},{1,3},{2,0},{3,1},{4,6},{5,7},{6,4},{7,5},{8,10},{9,11},{10,... | collective-permute-start | bytes 196616 | tf_op jit(solution)/shard_map/ppermute | solution.py:130
  37.8 0.2 copy-done.2
  38.0 0.2 copy-done.3
  38.2 1.0 %shard_map.134 = (bf16[128,2048]{1,0:T(8,128)(2,1)}, bf16[128,2048]{1,0:T(8,128)(2,1)}, bf16[128,2048]{1,0:T(8,128)(2,1)}, f32[8,128]{1,0:T(8,128)S(1)}) custom-call(bf16[128,512]{1,0:T(8,128)(2,1)S(1)} %get-tuple-element.62.refs_0_, bf16[128,512]{1,0:T(8,128)(2,1)S(1)} %get-tuple-element.59.refs_4_.refs_1_, ...), custom_call_target="tpu_custom_call" | custom-call | flops 1 | bytes 1 | tf_op jit(solution)/shard_map/pallas_call | solution.py:90
  39.1 2.2 %collective-permute-done.16.refs_2_.refs_9_ = f32[32,512]{1,0:T(8,128)S(1)} collective-permute-done((f32[32,512]{1,0:T(8,128)S(1)}, f32[32,512]{1,0:T(8,128)S(1)}, u32[]{:S(2)}, u32[]{:S(2)}) %collective-permute-start.16) | collective-permute-done | bytes 65568 | tf_op jit(solution)/shard_map/ppermute | solution.py:130
  41.4 0.1 collective-permute-start.17
  41.5 0.5 %collective-permute-start.18 = (f32[32,512]{1,0:T(8,128)S(1)}, f32[32,512]{1,0:T(8,128)S(1)}, u32[]{:S(2)}, u32[]{:S(2)}) collective-permute-start(f32[32,512]{1,0:T(8,128)S(1)} %get-tuple-element.66), channel_id=1, source_target_pairs={{0,1},{1,0},{2,3},{3,2},{4,5},{5,4},{6,7},{7,6},{8,9},{9,8},{10,11... | collective-permute-start | bytes 196616 | tf_op jit(solution)/shard_map/ppermute | solution.py:130
  42.0 0.9 %collective-permute-done.18.refs_8_ = f32[32,512]{1,0:T(8,128)S(1)} collective-permute-done((f32[32,512]{1,0:T(8,128)S(1)}, f32[32,512]{1,0:T(8,128)S(1)}, u32[]{:S(2)}, u32[]{:S(2)}) %collective-permute-start.18) | collective-permute-done | bytes 65568 | tf_op jit(solution)/shard_map/ppermute | solution.py:130
  42.9 1.0 %shard_map.136 = (bf16[128,2048]{1,0:T(8,128)(2,1)}, bf16[128,2048]{1,0:T(8,128)(2,1)}, bf16[128,2048]{1,0:T(8,128)(2,1)}, f32[16,2048]{1,0:T(8,128)}) custom-call(bf16[256,512]{1,0:T(8,128)(2,1)S(1)} %collective-permute-done.8.refs_9_.refs_1_.refs_0_, ...), custom_call_target="tpu_custom_call", output_to_operand_aliasing={{0}: (10, {}), {1}: (11, {}), {2}: (12, {})} | custom-call | flops 1 | bytes 1 | tf_op jit(solution)/shard_map/pallas_call | solution.py:90
  (26 shorter events, 0.2 us)
Async XLA Ops:
  0.7 1.6 %copy-start.4 = (bf16[128,2048]{1,0:T(8,128)(2,1)S(1)}, bf16[128,2048]{1,0:T(8,128)(2,1)}, u32[]{:S(2)}) copy-start(bf16[128,2048]{1,0:T(8,128)(2,1)} %refs_4_.3) | copy-start | bytes 1572868
  0.7 1.6 %copy-start.7 = (f32[16,2048]{1,0:T(8,128)S(1)}, f32[16,2048]{1,0:T(8,128)}, u32[]{:S(2)}) copy-start(f32[16,2048]{1,0:T(8,128)} %refs_0_.9) | copy-start | bytes 393220
  0.7 1.6 %copy-start.8 = (bf16[128,2048]{1,0:T(8,128)(2,1)S(1)}, bf16[128,2048]{1,0:T(8,128)(2,1)}, u32[]{:S(2)}) copy-start(bf16[128,2048]{1,0:T(8,128)(2,1)} %refs_1_.7) | copy-start | bytes 1572868
  2.5 3.2 %collective-permute-start = (bf16[416,512]{1,0:T(8,128)(2,1)S(1)}, bf16[416,512]{1,0:T(8,128)(2,1)S(1)}, u32[]{:S(2)}, u32[]{:S(2)}) collective-permute-start(bf16[416,512]{1,0:T(8,128)(2,1)S(1)} %get-tuple-element.37), channel_id=1, source_target_pairs={{0,1},{1,0},{2,3},{3,2},{4,5},{5,4},{6,7},{7,6},{8,9},{9,8},{10,11... | collective-permute-start | bytes 1277960 | tf_op jit(solution)/shard_map/ppermute | solution.py:130
  3.0 7.5 %collective-permute-start.2 = (bf16[128,512]{1,0:T(8,128)(2,1)S(1)}, bf16[128,512]{1,0:T(8,128)(2,1)S(1)}, u32[]{:S(2)}, u32[]{:S(2)}) collective-permute-start(bf16[128,512]{1,0:T(8,128)(2,1)S(1)} %get-tuple-element.70), channel_id=1, source_target_pairs={{0,3},{1,2},{2,1},{3,0},{4,7},{5,6},{6,5},{7,4},{8,11},{9,10},{10,... | collective-permute-start | bytes 393224 | tf_op jit(solution)/shard_map/ppermute | solution.py:130
  5.6 6.8 %collective-permute-start.1 = (bf16[128,512]{1,0:T(8,128)(2,1)S(1)}, bf16[128,512]{1,0:T(8,128)(2,1)S(1)}, u32[]{:S(2)}, u32[]{:S(2)}) collective-permute-start(bf16[128,512]{1,0:T(8,128)(2,1)S(1)} %get-tuple-element.71), channel_id=1, source_target_pairs={{0,2},{1,3},{2,0},{3,1},{4,6},{5,7},{6,4},{7,5},{8,10},{9,11},{10,... | collective-permute-start | bytes 393224 | tf_op jit(solution)/shard_map/ppermute | solution.py:130
  5.7 8.5 %collective-permute-start.6 = (bf16[64,512]{1,0:T(8,128)(2,1)S(1)}, bf16[64,512]{1,0:T(8,128)(2,1)S(1)}, u32[]{:S(2)}, u32[]{:S(2)}) collective-permute-start(bf16[64,512]{1,0:T(8,128)(2,1)S(1)} %shard_map.124.refs_0_), channel_id=1, source_target_pairs={{0,12},{1,13},{2,14},{3,15},{4,8},{5,9},{6,10},{7,11},{8,4},{9,5},... | collective-permute-start | bytes 196616 | tf_op jit(solution)/shard_map/ppermute | solution.py:130
  9.8 5.6 %collective-permute-start.5 = (bf16[64,512]{1,0:T(8,128)(2,1)S(1)}, bf16[64,512]{1,0:T(8,128)(2,1)S(1)}, u32[]{:S(2)}, u32[]{:S(2)}) collective-permute-start(bf16[64,512]{1,0:T(8,128)(2,1)S(1)} %shard_map.124.refs_0_), channel_id=1, source_target_pairs={{0,8},{1,9},{2,10},{3,11},{4,12},{5,13},{6,14},{7,15},{8,0},{9,1},... | collective-permute-start | bytes 196616 | tf_op jit(solution)/shard_map/ppermute | solution.py:130
  9.8 5.6 %collective-permute-start.4 = (bf16[64,512]{1,0:T(8,128)(2,1)S(1)}, bf16[64,512]{1,0:T(8,128)(2,1)S(1)}, u32[]{:S(2)}, u32[]{:S(2)}) collective-permute-start(bf16[64,512]{1,0:T(8,128)(2,1)S(1)} %shard_map.124.refs_0_), channel_id=1, source_target_pairs={{0,4},{1,5},{2,6},{3,7},{4,0},{5,1},{6,2},{7,3},{8,12},{9,13},{10,... | collective-permute-start | bytes 196616 | tf_op jit(solution)/shard_map/ppermute | solution.py:130
  10.5 9.5 %collective-permute-start.3 = (bf16[256,512]{1,0:T(8,128)(2,1)S(1)}, bf16[256,512]{1,0:T(8,128)(2,1)S(1)}, u32[]{:S(2)}, u32[]{:S(2)}) collective-permute-start(bf16[256,512]{1,0:T(8,128)(2,1)S(1)} %shard_map.123), channel_id=1, source_target_pairs={{0,2},{1,3},{2,0},{3,1},{4,6},{5,7},{6,4},{7,5},{8,10},{9,11},{10,... | collective-permute-start | bytes 786440 | tf_op jit(solution)/shard_map/ppermute | solution.py:130
  12.4 1.0 %copy-start = (bf16[512,256]{1,0:T(8,128)(2,1)S(1)}, bf16[512,256]{1,0:T(8,128)(2,1)}, u32[]{:S(2)}) copy-start(bf16[512,256]{1,0:T(8,128)(2,1)} %constant.42.clone.refs_1_) | copy-start | bytes 786436
  12.4 1.0 %copy-start.1 = (bf16[512,256]{1,0:T(8,128)(2,1)S(1)}, bf16[512,256]{1,0:T(8,128)(2,1)}, u32[]{:S(2)}) copy-start(bf16[512,256]{1,0:T(8,128)(2,1)} %constant.41.clone.refs_0_) | copy-start | bytes 786436
  15.4 6.7 %collective-permute-start.7 = (bf16[128,512]{1,0:T(8,128)(2,1)S(1)}, bf16[128,512]{1,0:T(8,128)(2,1)S(1)}, u32[]{:S(2)}, u32[]{:S(2)}) collective-permute-start(bf16[128,512]{1,0:T(8,128)(2,1)S(1)} %get-tuple-element.42.refs_3_), channel_id=1, source_target_pairs={{0,2},{1,3},{2,0},{3,1},{4,6},{5,7},{6,4},{7,5},{8,10},{9,11},{10,... | collective-permute-start | bytes 393224 | tf_op jit(solution)/shard_map/ppermute | solution.py:130
  17.0 7.5 %collective-permute-start.9 = (bf16[256,512]{1,0:T(8,128)(2,1)S(1)}, bf16[256,512]{1,0:T(8,128)(2,1)S(1)}, u32[]{:S(2)}, u32[]{:S(2)}) collective-permute-start(bf16[256,512]{1,0:T(8,128)(2,1)S(1)} %get-tuple-element.48), channel_id=1, source_target_pairs={{0,4},{1,5},{2,6},{3,7},{4,8},{5,9},{6,10},{7,11},{8,12},{9,13},{1... | collective-permute-start | bytes 786440 | tf_op jit(solution)/shard_map/ppermute | solution.py:133
  20.1 10.9 %collective-permute-start.10 = (bf16[256,512]{1,0:T(8,128)(2,1)S(1)}, bf16[256,512]{1,0:T(8,128)(2,1)S(1)}, u32[]{:S(2)}, u32[]{:S(2)}) collective-permute-start(bf16[256,512]{1,0:T(8,128)(2,1)S(1)} %get-tuple-element.51), channel_id=1, source_target_pairs={{4,0},{5,1},{6,2},{7,3},{8,4},{9,5},{10,6},{11,7},{12,8},{13,9},{1... | collective-permute-start | bytes 786440 | tf_op jit(solution)/shard_map/ppermute | solution.py:133
  21.4 1.0 %copy-start.5 = (bf16[256,512]{1,0:T(8,128)(2,1)S(1)}, bf16[256,512]{1,0:T(8,128)(2,1)}, u32[]{:S(2)}) copy-start(bf16[256,512]{1,0:T(8,128)(2,1)} %constant.44.clone.refs_3_.refs_1_) | copy-start | bytes 786436
  21.4 1.0 %copy-start.6 = (bf16[256,512]{1,0:T(8,128)(2,1)S(1)}, bf16[256,512]{1,0:T(8,128)(2,1)}, u32[]{:S(2)}) copy-start(bf16[256,512]{1,0:T(8,128)(2,1)} %constant.43.clone.refs_2_.refs_0_) | copy-start | bytes 786436
  23.5 9.5 %collective-permute-start.8 = (bf16[256,512]{1,0:T(8,128)(2,1)S(1)}, bf16[256,512]{1,0:T(8,128)(2,1)S(1)}, u32[]{:S(2)}, u32[]{:S(2)}) collective-permute-start(bf16[256,512]{1,0:T(8,128)(2,1)S(1)} %get-tuple-element.47), channel_id=1, source_target_pairs={{0,2},{1,3},{2,0},{3,1},{4,6},{5,7},{6,4},{7,5},{8,10},{9,11},{10,... | collective-permute-start | bytes 786440 | tf_op jit(solution)/shard_map/ppermute | solution.py:130
  25.6 8.6 %collective-permute-start.13 = (bf16[64,512]{1,0:T(8,128)(2,1)S(1)}, bf16[64,512]{1,0:T(8,128)(2,1)S(1)}, u32[]{:S(2)}, u32[]{:S(2)}) collective-permute-start(bf16[64,512]{1,0:T(8,128)(2,1)S(1)} %get-tuple-element.56), channel_id=1, source_target_pairs={{0,4},{1,5},{2,6},{3,7},{4,0},{5,1},{6,2},{7,3},{8,12},{9,13},{10,... | collective-permute-start | bytes 196616 | tf_op jit(solution)/shard_map/ppermute | solution.py:130
  28.2 6.6 %collective-permute-start.14 = (bf16[64,512]{1,0:T(8,128)(2,1)S(1)}, bf16[64,512]{1,0:T(8,128)(2,1)S(1)}, u32[]{:S(2)}, u32[]{:S(2)}) collective-permute-start(bf16[64,512]{1,0:T(8,128)(2,1)S(1)} %get-tuple-element.57), channel_id=1, source_target_pairs={{0,8},{1,9},{2,10},{3,11},{4,12},{5,13},{6,14},{7,15},{8,0},{9,1},... | collective-permute-start | bytes 196616 | tf_op jit(solution)/shard_map/ppermute | solution.py:130
  30.9 6.1 %collective-permute-start.15 = (bf16[64,512]{1,0:T(8,128)(2,1)S(1)}, bf16[64,512]{1,0:T(8,128)(2,1)S(1)}, u32[]{:S(2)}, u32[]{:S(2)}) collective-permute-start(bf16[64,512]{1,0:T(8,128)(2,1)S(1)} %get-tuple-element.58), channel_id=1, source_target_pairs={{0,12},{1,13},{2,14},{3,15},{4,8},{5,9},{6,10},{7,11},{8,4},{9,5},... | collective-permute-start | bytes 196616 | tf_op jit(solution)/shard_map/ppermute | solution.py:130
  32.0 9.4 %collective-permute-start.11 = (bf16[256,512]{1,0:T(8,128)(2,1)S(1)}, bf16[256,512]{1,0:T(8,128)(2,1)S(1)}, u32[]{:S(2)}, u32[]{:S(2)}) collective-permute-start(bf16[256,512]{1,0:T(8,128)(2,1)S(1)} %get-tuple-element.52), channel_id=1, source_target_pairs={{0,2},{1,3},{2,0},{3,1},{4,6},{5,7},{6,4},{7,5},{8,10},{9,11},{10,... | collective-permute-start | bytes 786440 | tf_op jit(solution)/shard_map/ppermute | solution.py:130
  34.2 3.7 %collective-permute-start.12 = (bf16[384,512]{1,0:T(8,128)(2,1)S(1)}, bf16[384,512]{1,0:T(8,128)(2,1)S(1)}, u32[]{:S(2)}, u32[]{:S(2)}) collective-permute-start(bf16[384,512]{1,0:T(8,128)(2,1)S(1)} %shard_map.132), channel_id=1, source_target_pairs={{0,1},{1,0},{2,3},{3,2},{4,5},{5,4},{6,7},{7,6},{8,9},{9,8},{10,11... | collective-permute-start | bytes 1179656 | tf_op jit(solution)/shard_map/ppermute | solution.py:130
  37.0 1.0 %copy-start.2 = (bf16[128,2048]{1,0:T(8,128)(2,1)S(1)}, bf16[128,2048]{1,0:T(8,128)(2,1)}, u32[]{:S(2)}) copy-start(bf16[128,2048]{1,0:T(8,128)(2,1)} %refs_5_.3) | copy-start | bytes 1572868
  37.0 1.2 %copy-start.3 = (bf16[128,2048]{1,0:T(8,128)(2,1)S(1)}, bf16[128,2048]{1,0:T(8,128)(2,1)}, u32[]{:S(2)}) copy-start(bf16[128,2048]{1,0:T(8,128)(2,1)} %refs_6_.1) | copy-start | bytes 1572868
  37.0 4.3 %collective-permute-start.16 = (f32[32,512]{1,0:T(8,128)S(1)}, f32[32,512]{1,0:T(8,128)S(1)}, u32[]{:S(2)}, u32[]{:S(2)}) collective-permute-start(f32[32,512]{1,0:T(8,128)S(1)} %get-tuple-element.61), channel_id=1, source_target_pairs={{0,2},{1,3},{2,0},{3,1},{4,6},{5,7},{6,4},{7,5},{8,10},{9,11},{10,... | collective-permute-start | bytes 196616 | tf_op jit(solution)/shard_map/ppermute | solution.py:130
  41.4 1.5 %collective-permute-start.17 = (bf16[128,512]{1,0:T(8,128)(2,1)S(1)}, bf16[128,512]{1,0:T(8,128)(2,1)S(1)}, u32[]{:S(2)}, u32[]{:S(2)}) collective-permute-start(bf16[128,512]{1,0:T(8,128)(2,1)S(1)} %get-tuple-element.64), channel_id=1, source_target_pairs={{0,1},{1,0},{2,3},{3,2},{4,5},{5,4},{6,7},{7,6},{8,9},{9,8},{10,11... | collective-permute-start | bytes 393224 | tf_op jit(solution)/shard_map/ppermute | solution.py:130
  41.5 1.4 %collective-permute-start.18 = (f32[32,512]{1,0:T(8,128)S(1)}, f32[32,512]{1,0:T(8,128)S(1)}, u32[]{:S(2)}, u32[]{:S(2)}) collective-permute-start(f32[32,512]{1,0:T(8,128)S(1)} %get-tuple-element.66), channel_id=1, source_target_pairs={{0,1},{1,0},{2,3},{3,2},{4,5},{5,4},{6,7},{7,6},{8,9},{9,8},{10,11... | collective-permute-start | bytes 196616 | tf_op jit(solution)/shard_map/ppermute | solution.py:130

commit v3 on v2

--- a/solution.py
+++ b/solution.py
@@ -400,7 +400,7 @@
         gather_grad,
         [struct(tokens, width, bf16), halo],
         [None, keep, near, far],
-        after=[taps_ship],
+        after=[],
         flops=1,
     )
     ahead = shift(bottom, -PLANE)
@@ -422,7 +422,7 @@
         [None, *fwd, *inv, *p_spec, *g_spec, behind],
         scratch=[pltpu.VMEM((taps, width), f32)],
         after=[taps_spec],
-        flops=1,
+        flops=10000000000,
     )
     away = [swap(part, PLANE * (step + 1)) for step, part in enumerate(away)]
     ahead_spec, ship = call(

time: 44.2 us -> 43.5 us (0.984)
  local copies, waits for them, and re-layouts: 1.69 us -> 0.65 us
    unnamed x18, local copies, waits for them, and re-layouts: 1.69 us -> 0.65 us
    ppermute x2, starting transfers between devices: 4.25 us -> 5.14 us  [shift(): lax.ppermute(array, 'seq', [(i, i + distance) for i in devices if i + dis...]
    ppermute x17, starting transfers between devices: 19.6 us -> 19.1 us  [swap(): return lax.ppermute(array, 'seq', [(i, i ^ distance) for i in devices])]
  transfers between devices with their start and end apart: 19 -> 19, of which waited for: 7 -> 6; matrix products, arithmetic and copies ran while one was open for 0% -> 0% of each run, Pallas kernels for 16% -> 16%
where the time goes in v3:
time: 43.5 us; the launch traced here: 43.3 us
  starting transfers between devices  24.2 us (56%)
  Pallas kernels  8.21 us (19%)
  waiting for transfers between devices  7.74 us (18%)
  other arithmetic  1.52 us (3%)
  between operations  0.92 us (2%)
  local copies, waits for them, and re-layouts  0.65 us (1%)
    ppermute x17, starting transfers between devices, swap(): return lax.ppermute(array, 'seq', [(i, i ^ distance) for i in devices])  19.1 us
    pallas_call x17, Pallas kernels, call(): pl.pallas_call(run, out_shape=outs, in_specs=specs, out_specs=[pl.BlockSp...  8.21 us
    ppermute x17, waiting for transfers between devices, swap(): return lax.ppermute(array, 'seq', [(i, i ^ distance) for i in devices])  7.73 us
    ppermute x2, starting transfers between devices, shift(): lax.ppermute(array, 'seq', [(i, i + distance) for i in devices if i + dis...  5.14 us
    convert_element_type x1, other arithmetic, product_block(): return (left * right).astype(bf16)  1.52 us
  transfers between devices with their start and end apart: 19, of which 6 were waited for; matrix products, arithmetic and copies ran while one was open for 0% of the time, Pallas kernels for 16%

profile of v3, /device:TPU:0, one launch (start us, length us, event | category | flops | bytes accessed | tf_op | source)
XLA Modules:
  0.0 43.3 jit_solution(16678289086562365439)
XLA Ops:
  0.7 1.5 %multiply_convert_fusion = (bf16[128,512]{1,0:T(8,128)(2,1)S(1)}, bf16[128,512]{1,0:T(8,128)(2,1)S(1)}, bf16[128,512]{1,0:T(8,128)(2,1)S(1)}, bf16[128,512]{1,0:T(8,128)(2,1)S(1)}) fusion(bf16[128,2048]{1,0:T(8,128)(2,1)} %refs_5_.3, s32[]{:T(128)S(6)} %select_n.33, bf16[128,2048]{1,0:T(8,128)(2,1)} %refs_6_.1, s32[]{:T(128)S(6)} %select_n.32, ...), kind=kLoop, calls=%fused_computation | loop fusion | flops 1048576 | bytes 1572880 | tf_op jit(solution)/shard_map/convert_element_type | solution.py:359
  2.2 0.1 copy-done.8
  2.3 0.1 shard_map.120
  2.5 0.5 %collective-permute-start = (bf16[416,512]{1,0:T(8,128)(2,1)S(1)}, bf16[416,512]{1,0:T(8,128)(2,1)S(1)}, u32[]{:S(2)}, u32[]{:S(2)}) collective-permute-start(bf16[416,512]{1,0:T(8,128)(2,1)S(1)} %get-tuple-element.37), channel_id=1, source_target_pairs={{0,1},{1,0},{2,3},{3,2},{4,5},{5,4},{6,7},{7,6},{8,9},{9,8},{10,11... | collective-permute-start | bytes 1277960 | tf_op jit(solution)/shard_map/ppermute | solution.py:130
  3.0 2.6 %collective-permute-start.2 = (bf16[128,512]{1,0:T(8,128)(2,1)S(1)}, bf16[128,512]{1,0:T(8,128)(2,1)S(1)}, u32[]{:S(2)}, u32[]{:S(2)}) collective-permute-start(bf16[128,512]{1,0:T(8,128)(2,1)S(1)} %get-tuple-element.70), channel_id=1, source_target_pairs={{0,3},{1,2},{2,1},{3,0},{4,7},{5,6},{6,5},{7,4},{8,11},{9,10},{10,... | collective-permute-start | bytes 393224 | tf_op jit(solution)/shard_map/ppermute | solution.py:130
  5.6 0.0 collective-permute-start.1
  5.6 0.0 collective-permute-done.refs_1_
  5.7 4.2 %collective-permute-start.6 = (bf16[64,512]{1,0:T(8,128)(2,1)S(1)}, bf16[64,512]{1,0:T(8,128)(2,1)S(1)}, u32[]{:S(2)}, u32[]{:S(2)}) collective-permute-start(bf16[64,512]{1,0:T(8,128)(2,1)S(1)} %shard_map.126.refs_0_), channel_id=1, source_target_pairs={{0,12},{1,13},{2,14},{3,15},{4,8},{5,9},{6,10},{7,11},{8,4},{9,5},... | collective-permute-start | bytes 196616 | tf_op jit(solution)/shard_map/ppermute | solution.py:130
  9.8 0.0 collective-permute-start.5
  9.8 0.6 %collective-permute-start.4 = (bf16[64,512]{1,0:T(8,128)(2,1)S(1)}, bf16[64,512]{1,0:T(8,128)(2,1)S(1)}, u32[]{:S(2)}, u32[]{:S(2)}) collective-permute-start(bf16[64,512]{1,0:T(8,128)(2,1)S(1)} %shard_map.126.refs_0_), channel_id=1, source_target_pairs={{0,4},{1,5},{2,6},{3,7},{4,0},{5,1},{6,2},{7,3},{8,12},{9,13},{10,... | collective-permute-start | bytes 196616 | tf_op jit(solution)/shard_map/ppermute | solution.py:130
  10.5 1.7 %collective-permute-start.3 = (bf16[256,512]{1,0:T(8,128)(2,1)S(1)}, bf16[256,512]{1,0:T(8,128)(2,1)S(1)}, u32[]{:S(2)}, u32[]{:S(2)}) collective-permute-start(bf16[256,512]{1,0:T(8,128)(2,1)S(1)} %shard_map.123), channel_id=1, source_target_pairs={{0,2},{1,3},{2,0},{3,1},{4,6},{5,7},{6,4},{7,5},{8,10},{9,11},{10,... | collective-permute-start | bytes 786440 | tf_op jit(solution)/shard_map/ppermute | solution.py:130
  12.2 0.3 collective-permute-done.1.refs_2_
  12.4 0.1 shard_map.121
  12.5 3.8 %collective-permute-start.9 = (bf16[256,512]{1,0:T(8,128)(2,1)S(1)}, bf16[256,512]{1,0:T(8,128)(2,1)S(1)}, u32[]{:S(2)}, u32[]{:S(2)}) collective-permute-start(bf16[256,512]{1,0:T(8,128)(2,1)S(1)} %get-tuple-element.48), channel_id=1, source_target_pairs={{0,4},{1,5},{2,6},{3,7},{4,8},{5,9},{6,10},{7,11},{8,12},{9,13},{1... | collective-permute-start | bytes 786440 | tf_op jit(solution)/shard_map/ppermute | solution.py:133
  16.4 0.7 %shard_map.122 = (f32[512,512]{1,0:T(8,128)S(1)}, f32[512,512]{1,0:T(8,128)S(1)}) custom-call(bf16[512,256]{1,0:T(8,128)(2,1)S(1)} %copy-done.4, bf16[512,256]{1,0:T(8,128)(2,1)S(1)} %copy-done.3, bf16[512,512]{1,0:T(8,128)(2,1)S(1)} %get-tuple-element.38.refs_2_), custom_call_target="tpu_custom_call" | custom-call | flops 1 | bytes 1 | tf_op jit(solution)/shard_map/pallas_call | solution.py:90
  17.1 0.0 collective-permute-done.6.refs_3_
  17.1 0.0 collective-permute-done.4.refs_1_
  17.2 1.6 %collective-permute-start.7 = (bf16[128,512]{1,0:T(8,128)(2,1)S(1)}, bf16[128,512]{1,0:T(8,128)(2,1)S(1)}, u32[]{:S(2)}, u32[]{:S(2)}) collective-permute-start(bf16[128,512]{1,0:T(8,128)(2,1)S(1)} %get-tuple-element.46), channel_id=1, source_target_pairs={{0,2},{1,3},{2,0},{3,1},{4,6},{5,7},{6,4},{7,5},{8,10},{9,11},{10,... | collective-permute-start | bytes 393224 | tf_op jit(solution)/shard_map/ppermute | solution.py:130
  18.7 0.1 shard_map.124
  18.8 1.3 %collective-permute-start.10 = (bf16[256,512]{1,0:T(8,128)(2,1)S(1)}, bf16[256,512]{1,0:T(8,128)(2,1)S(1)}, u32[]{:S(2)}, u32[]{:S(2)}) collective-permute-start(bf16[256,512]{1,0:T(8,128)(2,1)S(1)} %get-tuple-element.51), channel_id=1, source_target_pairs={{4,0},{5,1},{6,2},{7,3},{8,4},{9,5},{10,6},{11,7},{12,8},{13,9},{1... | collective-permute-start | bytes 786440 | tf_op jit(solution)/shard_map/ppermute | solution.py:133
  20.1 0.0 copy-start.5
  20.1 0.0 copy-start.6
  20.1 0.7 %shard_map.125 = (f32[512,512]{1,0:T(8,128)S(1)}, f32[512,512]{1,0:T(8,128)S(1)}) custom-call(bf16[512,256]{1,0:T(8,128)(2,1)S(1)} %copy-done.4, bf16[512,256]{1,0:T(8,128)(2,1)S(1)} %copy-done.3, bf16[512,512]{1,0:T(8,128)(2,1)S(1)} %get-tuple-element.42.refs_2_), custom_call_target="tpu_custom_call" | custom-call | flops 1 | bytes 1 | tf_op jit(solution)/shard_map/pallas_call | solution.py:90
  20.8 1.4 %collective-permute-done.7.refs_9_ = bf16[128,512]{1,0:T(8,128)(2,1)S(1)} collective-permute-done((bf16[128,512]{1,0:T(8,128)(2,1)S(1)}, bf16[128,512]{1,0:T(8,128)(2,1)S(1)}, u32[]{:S(2)}, u32[]{:S(2)}) %collective-permute-start.7) | collective-permute-done | bytes 131104 | tf_op jit(solution)/shard_map/ppermute | solution.py:130
  22.2 1.1 %shard_map.128 = (f32[512,512]{1,0:T(8,128)S(1)}, bf16[256,512]{1,0:T(8,128)(2,1)S(1)}) custom-call(bf16[512,256]{1,0:T(8,128)(2,1)S(1)} %copy-done.4, bf16[512,256]{1,0:T(8,128)(2,1)S(1)} %copy-done.3, bf16[256,512]{1,0:T(8,128)(2,1)S(1)} %copy-done.6, bf16[256,512]{1,0:T(8,128)(2,1)S(1)} %copy-done.5, f32[512,512]{1,0:T(8,128)S(1)} %get-tuple-element.39.refs_4_.refs_2_, ...), custom_call_target="tpu_custom_call" | custom-call | flops 1 | bytes 1 | tf_op jit(solution)/shard_map/pallas_call | solution.py:90
  23.3 1.5 %collective-permute-start.8 = (bf16[256,512]{1,0:T(8,128)(2,1)S(1)}, bf16[256,512]{1,0:T(8,128)(2,1)S(1)}, u32[]{:S(2)}, u32[]{:S(2)}) collective-permute-start(bf16[256,512]{1,0:T(8,128)(2,1)S(1)} %get-tuple-element.47), channel_id=1, source_target_pairs={{0,2},{1,3},{2,0},{3,1},{4,6},{5,7},{6,4},{7,5},{8,10},{9,11},{10,... | collective-permute-start | bytes 786440 | tf_op jit(solution)/shard_map/ppermute | solution.py:130
  24.9 0.0 collective-permute-done.9.refs_8_
  24.9 1.1 %shard_map.129 = (f32[512,512]{1,0:T(8,128)S(1)}, f32[64,512]{1,0:T(8,128)S(1)}, bf16[64,512]{1,0:T(8,128)(2,1)S(1)}, bf16[64,512]{1,0:T(8,128)(2,1)S(1)}, bf16[64,512]{1,0:T(8,128)(2,1)S(1)}) custom-call(bf16[512,256]{1,0:T(8,128)(2,1)S(1)} %copy-done.4, bf16[512,256]{1,0:T(8,128)(2,1)S(1)} %copy-done.3, bf16[256,512]{1,0:T(8,128)(2,1)S(1)} %copy-done.6, ...), custom_call_target="tpu_custom_call" | custom-call | flops 10000000000 | bytes 1 | tf_op jit(solution)/shard_map/pallas_call | solution.py:90
  26.0 1.6 %collective-permute-start.13 = (bf16[64,512]{1,0:T(8,128)(2,1)S(1)}, bf16[64,512]{1,0:T(8,128)(2,1)S(1)}, u32[]{:S(2)}, u32[]{:S(2)}) collective-permute-start(bf16[64,512]{1,0:T(8,128)(2,1)S(1)} %get-tuple-element.56), channel_id=1, source_target_pairs={{0,4},{1,5},{2,6},{3,7},{4,0},{5,1},{6,2},{7,3},{8,12},{9,13},{10,... | collective-permute-start | bytes 196616 | tf_op jit(solution)/shard_map/ppermute | solution.py:130
  27.7 2.6 %collective-permute-start.14 = (bf16[64,512]{1,0:T(8,128)(2,1)S(1)}, bf16[64,512]{1,0:T(8,128)(2,1)S(1)}, u32[]{:S(2)}, u32[]{:S(2)}) collective-permute-start(bf16[64,512]{1,0:T(8,128)(2,1)S(1)} %get-tuple-element.57), channel_id=1, source_target_pairs={{0,8},{1,9},{2,10},{3,11},{4,12},{5,13},{6,14},{7,15},{8,0},{9,1},... | collective-permute-start | bytes 196616 | tf_op jit(solution)/shard_map/ppermute | solution.py:130
  30.3 0.2 collective-permute-start.15
  30.5 1.1 %shard_map.130 = (f32[512,512]{1,0:T(8,128)S(1)}, bf16[256,512]{1,0:T(8,128)(2,1)S(1)}) custom-call(bf16[512,256]{1,0:T(8,128)(2,1)S(1)} %copy-done.4, bf16[512,256]{1,0:T(8,128)(2,1)S(1)} %copy-done.3, bf16[256,512]{1,0:T(8,128)(2,1)S(1)} %copy-done.6, bf16[256,512]{1,0:T(8,128)(2,1)S(1)} %copy-done.5, f32[512,512]{1,0:T(8,128)S(1)} %get-tuple-element.39.refs_4_.refs_2_, ...), custom_call_target="tpu_custom_call" | custom-call | flops 1 | bytes 1 | tf_op jit(solution)/shard_map/pallas_call | solution.py:90
  31.6 0.6 %collective-permute-start.11 = (bf16[256,512]{1,0:T(8,128)(2,1)S(1)}, bf16[256,512]{1,0:T(8,128)(2,1)S(1)}, u32[]{:S(2)}, u32[]{:S(2)}) collective-permute-start(bf16[256,512]{1,0:T(8,128)(2,1)S(1)} %get-tuple-element.52), channel_id=1, source_target_pairs={{0,2},{1,3},{2,0},{3,1},{4,6},{5,7},{6,4},{7,5},{8,10},{9,11},{10,... | collective-permute-start | bytes 786440 | tf_op jit(solution)/shard_map/ppermute | solution.py:130
  32.2 0.0 collective-permute-done.8.refs_9_.refs_1_.refs_0_
  32.2 1.1 %shard_map.131 = (bf16[128,512]{1,0:T(8,128)(2,1)S(1)}, bf16[128,512]{1,0:T(8,128)(2,1)S(1)}, bf16[256,512]{1,0:T(8,128)(2,1)S(1)}) custom-call(bf16[256,512]{1,0:T(8,128)(2,1)S(1)} %copy-done.6, bf16[256,512]{1,0:T(8,128)(2,1)S(1)} %copy-done.5, f32[512,512]{1,0:T(8,128)S(1)} %get-tuple-element.39.refs_4_.refs_2_, ...), custom_call_target="tpu_custom_call" | custom-call | flops 1 | bytes 1 | tf_op jit(solution)/shard_map/pallas_call | solution.py:90
  33.3 0.1 collective-permute-start.12
  33.4 0.0 collective-permute-done.13.refs_1_
  33.4 1.1 %collective-permute-done.14.refs_2_ = bf16[64,512]{1,0:T(8,128)(2,1)S(1)} collective-permute-done((bf16[64,512]{1,0:T(8,128)(2,1)S(1)}, bf16[64,512]{1,0:T(8,128)(2,1)S(1)}, u32[]{:S(2)}, u32[]{:S(2)}) %collective-permute-start.14) | collective-permute-done | bytes 65568 | tf_op jit(solution)/shard_map/ppermute | solution.py:130
  34.5 1.8 %collective-permute-done.15.refs_3_ = bf16[64,512]{1,0:T(8,128)(2,1)S(1)} collective-permute-done((bf16[64,512]{1,0:T(8,128)(2,1)S(1)}, bf16[64,512]{1,0:T(8,128)(2,1)S(1)}, u32[]{:S(2)}, u32[]{:S(2)}) %collective-permute-start.15) | collective-permute-done | bytes 65568 | tf_op jit(solution)/shard_map/ppermute | solution.py:130
  36.4 0.6 %collective-permute-start.16 = (f32[32,512]{1,0:T(8,128)S(1)}, f32[32,512]{1,0:T(8,128)S(1)}, u32[]{:S(2)}, u32[]{:S(2)}) collective-permute-start(f32[32,512]{1,0:T(8,128)S(1)} %get-tuple-element.61), channel_id=1, source_target_pairs={{0,2},{1,3},{2,0},{3,1},{4,6},{5,7},{6,4},{7,5},{8,10},{9,11},{10,... | collective-permute-start | bytes 196616 | tf_op jit(solution)/shard_map/ppermute | solution.py:130
  37.0 0.4 copy-done
  37.4 0.2 copy-done.1
  37.5 1.0 %shard_map.134 = (bf16[128,2048]{1,0:T(8,128)(2,1)}, bf16[128,2048]{1,0:T(8,128)(2,1)}, bf16[128,2048]{1,0:T(8,128)(2,1)}, f32[8,128]{1,0:T(8,128)S(1)}) custom-call(bf16[128,512]{1,0:T(8,128)(2,1)S(1)} %get-tuple-element.62.refs_0_, bf16[128,512]{1,0:T(8,128)(2,1)S(1)} %get-tuple-element.59.refs_4_.refs_1_, ...), custom_call_target="tpu_custom_call" | custom-call | flops 1 | bytes 1 | tf_op jit(solution)/shard_map/pallas_call | solution.py:90
  38.5 2.2 %collective-permute-done.16.refs_2_.refs_9_ = f32[32,512]{1,0:T(8,128)S(1)} collective-permute-done((f32[32,512]{1,0:T(8,128)S(1)}, f32[32,512]{1,0:T(8,128)S(1)}, u32[]{:S(2)}, u32[]{:S(2)}) %collective-permute-start.16) | collective-permute-done | bytes 65568 | tf_op jit(solution)/shard_map/ppermute | solution.py:130
  40.7 0.1 collective-permute-start.17
  40.8 0.5 %collective-permute-start.18 = (f32[32,512]{1,0:T(8,128)S(1)}, f32[32,512]{1,0:T(8,128)S(1)}, u32[]{:S(2)}, u32[]{:S(2)}) collective-permute-start(f32[32,512]{1,0:T(8,128)S(1)} %get-tuple-element.66), channel_id=1, source_target_pairs={{0,1},{1,0},{2,3},{3,2},{4,5},{5,4},{6,7},{7,6},{8,9},{9,8},{10,11... | collective-permute-start | bytes 196616 | tf_op jit(solution)/shard_map/ppermute | solution.py:130
  41.3 0.9 %collective-permute-done.18.refs_8_ = f32[32,512]{1,0:T(8,128)S(1)} collective-permute-done((f32[32,512]{1,0:T(8,128)S(1)}, f32[32,512]{1,0:T(8,128)S(1)}, u32[]{:S(2)}, u32[]{:S(2)}) %collective-permute-start.18) | collective-permute-done | bytes 65568 | tf_op jit(solution)/shard_map/ppermute | solution.py:130
  42.2 1.0 %shard_map.136 = (bf16[128,2048]{1,0:T(8,128)(2,1)}, bf16[128,2048]{1,0:T(8,128)(2,1)}, bf16[128,2048]{1,0:T(8,128)(2,1)}, f32[16,2048]{1,0:T(8,128)}) custom-call(bf16[256,512]{1,0:T(8,128)(2,1)S(1)} %collective-permute-done.8.refs_9_.refs_1_.refs_0_, ...), custom_call_target="tpu_custom_call", output_to_operand_aliasing={{0}: (10, {}), {1}: (11, {}), {2}: (12, {})} | custom-call | flops 1 | bytes 1 | tf_op jit(solution)/shard_map/pallas_call | solution.py:90
  (26 shorter events, 0.2 us)
Async XLA Ops:
  0.7 1.6 %copy-start.2 = (bf16[128,2048]{1,0:T(8,128)(2,1)S(1)}, bf16[128,2048]{1,0:T(8,128)(2,1)}, u32[]{:S(2)}) copy-start(bf16[128,2048]{1,0:T(8,128)(2,1)} %refs_4_.3) | copy-start | bytes 1572868
  0.7 1.6 %copy-start.7 = (f32[16,2048]{1,0:T(8,128)S(1)}, f32[16,2048]{1,0:T(8,128)}, u32[]{:S(2)}) copy-start(f32[16,2048]{1,0:T(8,128)} %refs_0_.9) | copy-start | bytes 393220
  0.7 1.6 %copy-start.8 = (bf16[128,2048]{1,0:T(8,128)(2,1)S(1)}, bf16[128,2048]{1,0:T(8,128)(2,1)}, u32[]{:S(2)}) copy-start(bf16[128,2048]{1,0:T(8,128)(2,1)} %refs_1_.7) | copy-start | bytes 1572868
  2.5 3.2 %collective-permute-start = (bf16[416,512]{1,0:T(8,128)(2,1)S(1)}, bf16[416,512]{1,0:T(8,128)(2,1)S(1)}, u32[]{:S(2)}, u32[]{:S(2)}) collective-permute-start(bf16[416,512]{1,0:T(8,128)(2,1)S(1)} %get-tuple-element.37), channel_id=1, source_target_pairs={{0,1},{1,0},{2,3},{3,2},{4,5},{5,4},{6,7},{7,6},{8,9},{9,8},{10,11... | collective-permute-start | bytes 1277960 | tf_op jit(solution)/shard_map/ppermute | solution.py:130
  3.0 7.5 %collective-permute-start.2 = (bf16[128,512]{1,0:T(8,128)(2,1)S(1)}, bf16[128,512]{1,0:T(8,128)(2,1)S(1)}, u32[]{:S(2)}, u32[]{:S(2)}) collective-permute-start(bf16[128,512]{1,0:T(8,128)(2,1)S(1)} %get-tuple-element.70), channel_id=1, source_target_pairs={{0,3},{1,2},{2,1},{3,0},{4,7},{5,6},{6,5},{7,4},{8,11},{9,10},{10,... | collective-permute-start | bytes 393224 | tf_op jit(solution)/shard_map/ppermute | solution.py:130
  5.6 6.8 %collective-permute-start.1 = (bf16[128,512]{1,0:T(8,128)(2,1)S(1)}, bf16[128,512]{1,0:T(8,128)(2,1)S(1)}, u32[]{:S(2)}, u32[]{:S(2)}) collective-permute-start(bf16[128,512]{1,0:T(8,128)(2,1)S(1)} %get-tuple-element.71), channel_id=1, source_target_pairs={{0,2},{1,3},{2,0},{3,1},{4,6},{5,7},{6,4},{7,5},{8,10},{9,11},{10,... | collective-permute-start | bytes 393224 | tf_op jit(solution)/shard_map/ppermute | solution.py:130
  5.7 11.4 %collective-permute-start.6 = (bf16[64,512]{1,0:T(8,128)(2,1)S(1)}, bf16[64,512]{1,0:T(8,128)(2,1)S(1)}, u32[]{:S(2)}, u32[]{:S(2)}) collective-permute-start(bf16[64,512]{1,0:T(8,128)(2,1)S(1)} %shard_map.126.refs_0_), channel_id=1, source_target_pairs={{0,12},{1,13},{2,14},{3,15},{4,8},{5,9},{6,10},{7,11},{8,4},{9,5},... | collective-permute-start | bytes 196616 | tf_op jit(solution)/shard_map/ppermute | solution.py:130
  9.8 7.3 %collective-permute-start.5 = (bf16[64,512]{1,0:T(8,128)(2,1)S(1)}, bf16[64,512]{1,0:T(8,128)(2,1)S(1)}, u32[]{:S(2)}, u32[]{:S(2)}) collective-permute-start(bf16[64,512]{1,0:T(8,128)(2,1)S(1)} %shard_map.126.refs_0_), channel_id=1, source_target_pairs={{0,8},{1,9},{2,10},{3,11},{4,12},{5,13},{6,14},{7,15},{8,0},{9,1},... | collective-permute-start | bytes 196616 | tf_op jit(solution)/shard_map/ppermute | solution.py:130
  9.8 7.3 %collective-permute-start.4 = (bf16[64,512]{1,0:T(8,128)(2,1)S(1)}, bf16[64,512]{1,0:T(8,128)(2,1)S(1)}, u32[]{:S(2)}, u32[]{:S(2)}) collective-permute-start(bf16[64,512]{1,0:T(8,128)(2,1)S(1)} %shard_map.126.refs_0_), channel_id=1, source_target_pairs={{0,4},{1,5},{2,6},{3,7},{4,0},{5,1},{6,2},{7,3},{8,12},{9,13},{10,... | collective-permute-start | bytes 196616 | tf_op jit(solution)/shard_map/ppermute | solution.py:130
  10.5 8.3 %collective-permute-start.3 = (bf16[256,512]{1,0:T(8,128)(2,1)S(1)}, bf16[256,512]{1,0:T(8,128)(2,1)S(1)}, u32[]{:S(2)}, u32[]{:S(2)}) collective-permute-start(bf16[256,512]{1,0:T(8,128)(2,1)S(1)} %shard_map.123), channel_id=1, source_target_pairs={{0,2},{1,3},{2,0},{3,1},{4,6},{5,7},{6,4},{7,5},{8,10},{9,11},{10,... | collective-permute-start | bytes 786440 | tf_op jit(solution)/shard_map/ppermute | solution.py:130
  12.4 3.9 %copy-start.3 = (bf16[512,256]{1,0:T(8,128)(2,1)S(1)}, bf16[512,256]{1,0:T(8,128)(2,1)}, u32[]{:S(2)}) copy-start(bf16[512,256]{1,0:T(8,128)(2,1)} %constant.42.clone.refs_1_) | copy-start | bytes 786436
  12.4 3.9 %copy-start.4 = (bf16[512,256]{1,0:T(8,128)(2,1)S(1)}, bf16[512,256]{1,0:T(8,128)(2,1)}, u32[]{:S(2)}) copy-start(bf16[512,256]{1,0:T(8,128)(2,1)} %constant.41.clone.refs_0_) | copy-start | bytes 786436
  12.5 12.4 %collective-permute-start.9 = (bf16[256,512]{1,0:T(8,128)(2,1)S(1)}, bf16[256,512]{1,0:T(8,128)(2,1)S(1)}, u32[]{:S(2)}, u32[]{:S(2)}) collective-permute-start(bf16[256,512]{1,0:T(8,128)(2,1)S(1)} %get-tuple-element.48), channel_id=1, source_target_pairs={{0,4},{1,5},{2,6},{3,7},{4,8},{5,9},{6,10},{7,11},{8,12},{9,13},{1... | collective-permute-start | bytes 786440 | tf_op jit(solution)/shard_map/ppermute | solution.py:133
  17.2 5.0 %collective-permute-start.7 = (bf16[128,512]{1,0:T(8,128)(2,1)S(1)}, bf16[128,512]{1,0:T(8,128)(2,1)S(1)}, u32[]{:S(2)}, u32[]{:S(2)}) collective-permute-start(bf16[128,512]{1,0:T(8,128)(2,1)S(1)} %get-tuple-element.46), channel_id=1, source_target_pairs={{0,2},{1,3},{2,0},{3,1},{4,6},{5,7},{6,4},{7,5},{8,10},{9,11},{10,... | collective-permute-start | bytes 393224 | tf_op jit(solution)/shard_map/ppermute | solution.py:130
  18.8 11.7 %collective-permute-start.10 = (bf16[256,512]{1,0:T(8,128)(2,1)S(1)}, bf16[256,512]{1,0:T(8,128)(2,1)S(1)}, u32[]{:S(2)}, u32[]{:S(2)}) collective-permute-start(bf16[256,512]{1,0:T(8,128)(2,1)S(1)} %get-tuple-element.51), channel_id=1, source_target_pairs={{4,0},{5,1},{6,2},{7,3},{8,4},{9,5},{10,6},{11,7},{12,8},{13,9},{1... | collective-permute-start | bytes 786440 | tf_op jit(solution)/shard_map/ppermute | solution.py:133
  20.1 2.1 %copy-start.5 = (bf16[256,512]{1,0:T(8,128)(2,1)S(1)}, bf16[256,512]{1,0:T(8,128)(2,1)}, u32[]{:S(2)}) copy-start(bf16[256,512]{1,0:T(8,128)(2,1)} %constant.44.clone.refs_3_.refs_1_) | copy-start | bytes 786436
  20.1 2.1 %copy-start.6 = (bf16[256,512]{1,0:T(8,128)(2,1)S(1)}, bf16[256,512]{1,0:T(8,128)(2,1)}, u32[]{:S(2)}) copy-start(bf16[256,512]{1,0:T(8,128)(2,1)} %constant.43.clone.refs_2_.refs_0_) | copy-start | bytes 786436
  23.3 8.8 %collective-permute-start.8 = (bf16[256,512]{1,0:T(8,128)(2,1)S(1)}, bf16[256,512]{1,0:T(8,128)(2,1)S(1)}, u32[]{:S(2)}, u32[]{:S(2)}) collective-permute-start(bf16[256,512]{1,0:T(8,128)(2,1)S(1)} %get-tuple-element.47), channel_id=1, source_target_pairs={{0,2},{1,3},{2,0},{3,1},{4,6},{5,7},{6,4},{7,5},{8,10},{9,11},{10,... | collective-permute-start | bytes 786440 | tf_op jit(solution)/shard_map/ppermute | solution.py:130
  26.0 7.3 %collective-permute-start.13 = (bf16[64,512]{1,0:T(8,128)(2,1)S(1)}, bf16[64,512]{1,0:T(8,128)(2,1)S(1)}, u32[]{:S(2)}, u32[]{:S(2)}) collective-permute-start(bf16[64,512]{1,0:T(8,128)(2,1)S(1)} %get-tuple-element.56), channel_id=1, source_target_pairs={{0,4},{1,5},{2,6},{3,7},{4,0},{5,1},{6,2},{7,3},{8,12},{9,13},{10,... | collective-permute-start | bytes 196616 | tf_op jit(solution)/shard_map/ppermute | solution.py:130
  27.7 6.8 %collective-permute-start.14 = (bf16[64,512]{1,0:T(8,128)(2,1)S(1)}, bf16[64,512]{1,0:T(8,128)(2,1)S(1)}, u32[]{:S(2)}, u32[]{:S(2)}) collective-permute-start(bf16[64,512]{1,0:T(8,128)(2,1)S(1)} %get-tuple-element.57), channel_id=1, source_target_pairs={{0,8},{1,9},{2,10},{3,11},{4,12},{5,13},{6,14},{7,15},{8,0},{9,1},... | collective-permute-start | bytes 196616 | tf_op jit(solution)/shard_map/ppermute | solution.py:130
  30.3 6.1 %collective-permute-start.15 = (bf16[64,512]{1,0:T(8,128)(2,1)S(1)}, bf16[64,512]{1,0:T(8,128)(2,1)S(1)}, u32[]{:S(2)}, u32[]{:S(2)}) collective-permute-start(bf16[64,512]{1,0:T(8,128)(2,1)S(1)} %get-tuple-element.58), channel_id=1, source_target_pairs={{0,12},{1,13},{2,14},{3,15},{4,8},{5,9},{6,10},{7,11},{8,4},{9,5},... | collective-permute-start | bytes 196616 | tf_op jit(solution)/shard_map/ppermute | solution.py:130
  31.6 9.1 %collective-permute-start.11 = (bf16[256,512]{1,0:T(8,128)(2,1)S(1)}, bf16[256,512]{1,0:T(8,128)(2,1)S(1)}, u32[]{:S(2)}, u32[]{:S(2)}) collective-permute-start(bf16[256,512]{1,0:T(8,128)(2,1)S(1)} %get-tuple-element.52), channel_id=1, source_target_pairs={{0,2},{1,3},{2,0},{3,1},{4,6},{5,7},{6,4},{7,5},{8,10},{9,11},{10,... | collective-permute-start | bytes 786440 | tf_op jit(solution)/shard_map/ppermute | solution.py:130
  33.3 3.7 %collective-permute-start.12 = (bf16[384,512]{1,0:T(8,128)(2,1)S(1)}, bf16[384,512]{1,0:T(8,128)(2,1)S(1)}, u32[]{:S(2)}, u32[]{:S(2)}) collective-permute-start(bf16[384,512]{1,0:T(8,128)(2,1)S(1)} %shard_map.132), channel_id=1, source_target_pairs={{0,1},{1,0},{2,3},{3,2},{4,5},{5,4},{6,7},{7,6},{8,9},{9,8},{10,11... | collective-permute-start | bytes 1179656 | tf_op jit(solution)/shard_map/ppermute | solution.py:130
  36.3 1.0 %copy-start = (bf16[128,2048]{1,0:T(8,128)(2,1)S(1)}, bf16[128,2048]{1,0:T(8,128)(2,1)}, u32[]{:S(2)}) copy-start(bf16[128,2048]{1,0:T(8,128)(2,1)} %refs_5_.3) | copy-start | bytes 1572868
  36.3 1.2 %copy-start.1 = (bf16[128,2048]{1,0:T(8,128)(2,1)S(1)}, bf16[128,2048]{1,0:T(8,128)(2,1)}, u32[]{:S(2)}) copy-start(bf16[128,2048]{1,0:T(8,128)(2,1)} %refs_6_.1) | copy-start | bytes 1572868
  36.4 4.3 %collective-permute-start.16 = (f32[32,512]{1,0:T(8,128)S(1)}, f32[32,512]{1,0:T(8,128)S(1)}, u32[]{:S(2)}, u32[]{:S(2)}) collective-permute-start(f32[32,512]{1,0:T(8,128)S(1)} %get-tuple-element.61), channel_id=1, source_target_pairs={{0,2},{1,3},{2,0},{3,1},{4,6},{5,7},{6,4},{7,5},{8,10},{9,11},{10,... | collective-permute-start | bytes 196616 | tf_op jit(solution)/shard_map/ppermute | solution.py:130
  40.7 1.5 %collective-permute-start.17 = (bf16[128,512]{1,0:T(8,128)(2,1)S(1)}, bf16[128,512]{1,0:T(8,128)(2,1)S(1)}, u32[]{:S(2)}, u32[]{:S(2)}) collective-permute-start(bf16[128,512]{1,0:T(8,128)(2,1)S(1)} %get-tuple-element.64), channel_id=1, source_target_pairs={{0,1},{1,0},{2,3},{3,2},{4,5},{5,4},{6,7},{7,6},{8,9},{9,8},{10,11... | collective-permute-start | bytes 393224 | tf_op jit(solution)/shard_map/ppermute | solution.py:130
  40.8 1.4 %collective-permute-start.18 = (f32[32,512]{1,0:T(8,128)S(1)}, f32[32,512]{1,0:T(8,128)S(1)}, u32[]{:S(2)}, u32[]{:S(2)}) collective-permute-start(f32[32,512]{1,0:T(8,128)S(1)} %get-tuple-element.66), channel_id=1, source_target_pairs={{0,1},{1,0},{2,3},{3,2},{4,5},{5,4},{6,7},{7,6},{8,9},{9,8},{10,11... | collective-permute-start | bytes 196616 | tf_op jit(solution)/shard_map/ppermute | solution.py:130

commit v4 on v3

--- a/solution.py
+++ b/solution.py
@@ -358,7 +358,8 @@
         right = lax.dynamic_slice_in_dim(values, start, width, 1).astype(f32)
         return (left * right).astype(bf16)
 
-    sent = [product_block(step) for step in range(PLANE)]
+    sent = [product_block(step) for step in (2, 3)]
+    sent = [product_block(0), product_block(1)] + list(lax.optimization_barrier(tuple(sent)))
     far_p = [swap(sent[step], step) for step in (2, 3)]
     keep, side = call(
         gate_grad,

time: 43.5 us -> 43.2 us (level)
  no operation moved by 1% of the time
where the time goes in v4:
time: 43.2 us; the launch traced here: 43 us
  starting transfers between devices  23.8 us (55%)
  Pallas kernels  8.21 us (19%)
  waiting for transfers between devices  7.9 us (18%)
  other arithmetic  1.52 us (4%)
  between operations  0.92 us (2%)
  local copies, waits for them, and re-layouts  0.65 us (2%)
    ppermute x17, starting transfers between devices, swap(): return lax.ppermute(array, 'seq', [(i, i ^ distance) for i in devices])  18.8 us
    pallas_call x17, Pallas kernels, call(): pl.pallas_call(run, out_shape=outs, in_specs=specs, out_specs=[pl.BlockSp...  8.21 us
    ppermute x17, waiting for transfers between devices, swap(): return lax.ppermute(array, 'seq', [(i, i ^ distance) for i in devices])  7.9 us
    ppermute x2, starting transfers between devices, shift(): lax.ppermute(array, 'seq', [(i, i + distance) for i in devices if i + dis...  4.99 us
    convert_element_type x1, other arithmetic, product_block(): return (left * right).astype(bf16)  1.52 us
  transfers between devices with their start and end apart: 19, of which 6 were waited for; matrix products, arithmetic and copies ran while one was open for 0% of the time, Pallas kernels for 16%

profile of v4, /device:TPU:0, one launch (start us, length us, event | category | flops | bytes accessed | tf_op | source)
XLA Modules:
  0.0 43.0 jit_solution(15565619985329415642)
XLA Ops:
  0.7 1.5 %multiply_convert_fusion = (bf16[128,512]{1,0:T(8,128)(2,1)S(1)}, bf16[128,512]{1,0:T(8,128)(2,1)S(1)}, bf16[128,512]{1,0:T(8,128)(2,1)S(1)}, bf16[128,512]{1,0:T(8,128)(2,1)S(1)}) fusion(bf16[128,2048]{1,0:T(8,128)(2,1)} %refs_5_.3, s32[]{:T(128)S(6)} %select_n.33, bf16[128,2048]{1,0:T(8,128)(2,1)} %refs_6_.1, s32[]{:T(128)S(6)} %select_n.32, ...), kind=kLoop, calls=%fused_computation | loop fusion | flops 1048576 | bytes 1572880 | tf_op jit(solution)/shard_map/convert_element_type | solution.py:359
  2.2 0.1 copy-done.8
  2.3 0.1 shard_map.120
  2.5 0.5 %collective-permute-start = (bf16[416,512]{1,0:T(8,128)(2,1)S(1)}, bf16[416,512]{1,0:T(8,128)(2,1)S(1)}, u32[]{:S(2)}, u32[]{:S(2)}) collective-permute-start(bf16[416,512]{1,0:T(8,128)(2,1)S(1)} %get-tuple-element.39), channel_id=1, source_target_pairs={{0,1},{1,0},{2,3},{3,2},{4,5},{5,4},{6,7},{7,6},{8,9},{9,8},{10,11... | collective-permute-start | bytes 1277960 | tf_op jit(solution)/shard_map/ppermute | solution.py:130
  3.0 2.6 %collective-permute-start.1 = (bf16[128,512]{1,0:T(8,128)(2,1)S(1)}, bf16[128,512]{1,0:T(8,128)(2,1)S(1)}, u32[]{:S(2)}, u32[]{:S(2)}) collective-permute-start(bf16[128,512]{1,0:T(8,128)(2,1)S(1)} %get-tuple-element.40), channel_id=1, source_target_pairs={{0,2},{1,3},{2,0},{3,1},{4,6},{5,7},{6,4},{7,5},{8,10},{9,11},{10,... | collective-permute-start | bytes 393224 | tf_op jit(solution)/shard_map/ppermute | solution.py:130
  5.5 0.1 collective-permute-start.2
  5.6 0.0 collective-permute-done.refs_1_
  5.6 3.9 %collective-permute-start.6 = (bf16[64,512]{1,0:T(8,128)(2,1)S(1)}, bf16[64,512]{1,0:T(8,128)(2,1)S(1)}, u32[]{:S(2)}, u32[]{:S(2)}) collective-permute-start(bf16[64,512]{1,0:T(8,128)(2,1)S(1)} %shard_map.126.refs_0_), channel_id=1, source_target_pairs={{0,12},{1,13},{2,14},{3,15},{4,8},{5,9},{6,10},{7,11},{8,4},{9,5},... | collective-permute-start | bytes 196616 | tf_op jit(solution)/shard_map/ppermute | solution.py:130
  9.5 0.6 %collective-permute-start.4 = (bf16[64,512]{1,0:T(8,128)(2,1)S(1)}, bf16[64,512]{1,0:T(8,128)(2,1)S(1)}, u32[]{:S(2)}, u32[]{:S(2)}) collective-permute-start(bf16[64,512]{1,0:T(8,128)(2,1)S(1)} %shard_map.126.refs_0_), channel_id=1, source_target_pairs={{0,4},{1,5},{2,6},{3,7},{4,0},{5,1},{6,2},{7,3},{8,12},{9,13},{10,... | collective-permute-start | bytes 196616 | tf_op jit(solution)/shard_map/ppermute | solution.py:130
  10.2 0.0 collective-permute-done.1.refs_2_
  10.2 1.7 %collective-permute-start.3 = (bf16[256,512]{1,0:T(8,128)(2,1)S(1)}, bf16[256,512]{1,0:T(8,128)(2,1)S(1)}, u32[]{:S(2)}, u32[]{:S(2)}) collective-permute-start(bf16[256,512]{1,0:T(8,128)(2,1)S(1)} %shard_map.123), channel_id=1, source_target_pairs={{0,2},{1,3},{2,0},{3,1},{4,6},{5,7},{6,4},{7,5},{8,10},{9,11},{10,... | collective-permute-start | bytes 786440 | tf_op jit(solution)/shard_map/ppermute | solution.py:130
  11.9 0.3 collective-permute-done.2.refs_3_
  12.2 0.1 shard_map.121
  12.3 3.7 %collective-permute-start.9 = (bf16[256,512]{1,0:T(8,128)(2,1)S(1)}, bf16[256,512]{1,0:T(8,128)(2,1)S(1)}, u32[]{:S(2)}, u32[]{:S(2)}) collective-permute-start(bf16[256,512]{1,0:T(8,128)(2,1)S(1)} %get-tuple-element.52), channel_id=1, source_target_pairs={{0,4},{1,5},{2,6},{3,7},{4,8},{5,9},{6,10},{7,11},{8,12},{9,13},{1... | collective-permute-start | bytes 786440 | tf_op jit(solution)/shard_map/ppermute | solution.py:133
  16.0 0.7 %shard_map.122 = (f32[512,512]{1,0:T(8,128)S(1)}, f32[512,512]{1,0:T(8,128)S(1)}) custom-call(bf16[512,256]{1,0:T(8,128)(2,1)S(1)} %copy-done.4, bf16[512,256]{1,0:T(8,128)(2,1)S(1)} %copy-done.3, bf16[512,512]{1,0:T(8,128)(2,1)S(1)} %get-tuple-element.42.refs_2_), custom_call_target="tpu_custom_call" | custom-call | flops 1 | bytes 1 | tf_op jit(solution)/shard_map/pallas_call | solution.py:90
  16.7 0.0 collective-permute-done.6.refs_3_
  16.7 0.0 collective-permute-done.5.refs_2_
  16.8 1.6 %collective-permute-start.7 = (bf16[128,512]{1,0:T(8,128)(2,1)S(1)}, bf16[128,512]{1,0:T(8,128)(2,1)S(1)}, u32[]{:S(2)}, u32[]{:S(2)}) collective-permute-start(bf16[128,512]{1,0:T(8,128)(2,1)S(1)} %get-tuple-element.50), channel_id=1, source_target_pairs={{0,2},{1,3},{2,0},{3,1},{4,6},{5,7},{6,4},{7,5},{8,10},{9,11},{10,... | collective-permute-start | bytes 393224 | tf_op jit(solution)/shard_map/ppermute | solution.py:130
  18.3 0.1 shard_map.124
  18.4 1.3 %collective-permute-start.10 = (bf16[256,512]{1,0:T(8,128)(2,1)S(1)}, bf16[256,512]{1,0:T(8,128)(2,1)S(1)}, u32[]{:S(2)}, u32[]{:S(2)}) collective-permute-start(bf16[256,512]{1,0:T(8,128)(2,1)S(1)} %get-tuple-element.55), channel_id=1, source_target_pairs={{4,0},{5,1},{6,2},{7,3},{8,4},{9,5},{10,6},{11,7},{12,8},{13,9},{1... | collective-permute-start | bytes 786440 | tf_op jit(solution)/shard_map/ppermute | solution.py:133
  19.7 0.0 copy-start.5
  19.7 0.0 copy-start.6
  19.7 0.7 %shard_map.125 = (f32[512,512]{1,0:T(8,128)S(1)}, f32[512,512]{1,0:T(8,128)S(1)}) custom-call(bf16[512,256]{1,0:T(8,128)(2,1)S(1)} %copy-done.4, bf16[512,256]{1,0:T(8,128)(2,1)S(1)} %copy-done.3, bf16[512,512]{1,0:T(8,128)(2,1)S(1)} %get-tuple-element.46.refs_2_), custom_call_target="tpu_custom_call" | custom-call | flops 1 | bytes 1 | tf_op jit(solution)/shard_map/pallas_call | solution.py:90
  20.4 2.3 %collective-permute-done.7.refs_9_ = bf16[128,512]{1,0:T(8,128)(2,1)S(1)} collective-permute-done((bf16[128,512]{1,0:T(8,128)(2,1)S(1)}, bf16[128,512]{1,0:T(8,128)(2,1)S(1)}, u32[]{:S(2)}, u32[]{:S(2)}) %collective-permute-start.7) | collective-permute-done | bytes 131104 | tf_op jit(solution)/shard_map/ppermute | solution.py:130
  22.7 1.1 %shard_map.128 = (f32[512,512]{1,0:T(8,128)S(1)}, bf16[256,512]{1,0:T(8,128)(2,1)S(1)}) custom-call(bf16[512,256]{1,0:T(8,128)(2,1)S(1)} %copy-done.4, bf16[512,256]{1,0:T(8,128)(2,1)S(1)} %copy-done.3, bf16[256,512]{1,0:T(8,128)(2,1)S(1)} %copy-done.6, bf16[256,512]{1,0:T(8,128)(2,1)S(1)} %copy-done.5, f32[512,512]{1,0:T(8,128)S(1)} %get-tuple-element.43.refs_4_.refs_2_, ...), custom_call_target="tpu_custom_call" | custom-call | flops 1 | bytes 1 | tf_op jit(solution)/shard_map/pallas_call | solution.py:90
  23.8 1.5 %collective-permute-start.8 = (bf16[256,512]{1,0:T(8,128)(2,1)S(1)}, bf16[256,512]{1,0:T(8,128)(2,1)S(1)}, u32[]{:S(2)}, u32[]{:S(2)}) collective-permute-start(bf16[256,512]{1,0:T(8,128)(2,1)S(1)} %get-tuple-element.51), channel_id=1, source_target_pairs={{0,2},{1,3},{2,0},{3,1},{4,6},{5,7},{6,4},{7,5},{8,10},{9,11},{10,... | collective-permute-start | bytes 786440 | tf_op jit(solution)/shard_map/ppermute | solution.py:130
  25.4 0.0 collective-permute-done.9.refs_8_
  25.4 1.1 %shard_map.129 = (f32[512,512]{1,0:T(8,128)S(1)}, f32[64,512]{1,0:T(8,128)S(1)}, bf16[64,512]{1,0:T(8,128)(2,1)S(1)}, bf16[64,512]{1,0:T(8,128)(2,1)S(1)}, bf16[64,512]{1,0:T(8,128)(2,1)S(1)}) custom-call(bf16[512,256]{1,0:T(8,128)(2,1)S(1)} %copy-done.4, bf16[512,256]{1,0:T(8,128)(2,1)S(1)} %copy-done.3, bf16[256,512]{1,0:T(8,128)(2,1)S(1)} %copy-done.6, ...), custom_call_target="tpu_custom_call" | custom-call | flops 10000000000 | bytes 1 | tf_op jit(solution)/shard_map/pallas_call | solution.py:90
  26.5 1.7 %collective-permute-start.13 = (bf16[64,512]{1,0:T(8,128)(2,1)S(1)}, bf16[64,512]{1,0:T(8,128)(2,1)S(1)}, u32[]{:S(2)}, u32[]{:S(2)}) collective-permute-start(bf16[64,512]{1,0:T(8,128)(2,1)S(1)} %get-tuple-element.60), channel_id=1, source_target_pairs={{0,4},{1,5},{2,6},{3,7},{4,0},{5,1},{6,2},{7,3},{8,12},{9,13},{10,... | collective-permute-start | bytes 196616 | tf_op jit(solution)/shard_map/ppermute | solution.py:130
  28.3 1.6 %collective-permute-start.14 = (bf16[64,512]{1,0:T(8,128)(2,1)S(1)}, bf16[64,512]{1,0:T(8,128)(2,1)S(1)}, u32[]{:S(2)}, u32[]{:S(2)}) collective-permute-start(bf16[64,512]{1,0:T(8,128)(2,1)S(1)} %get-tuple-element.61), channel_id=1, source_target_pairs={{0,8},{1,9},{2,10},{3,11},{4,12},{5,13},{6,14},{7,15},{8,0},{9,1},... | collective-permute-start | bytes 196616 | tf_op jit(solution)/shard_map/ppermute | solution.py:130
  29.8 1.1 %collective-permute-start.15 = (bf16[64,512]{1,0:T(8,128)(2,1)S(1)}, bf16[64,512]{1,0:T(8,128)(2,1)S(1)}, u32[]{:S(2)}, u32[]{:S(2)}) collective-permute-start(bf16[64,512]{1,0:T(8,128)(2,1)S(1)} %get-tuple-element.62), channel_id=1, source_target_pairs={{0,12},{1,13},{2,14},{3,15},{4,8},{5,9},{6,10},{7,11},{8,4},{9,5},... | collective-permute-start | bytes 196616 | tf_op jit(solution)/shard_map/ppermute | solution.py:130
  31.0 0.0 collective-permute-done.10.refs_7_
  31.0 1.1 %shard_map.130 = (f32[512,512]{1,0:T(8,128)S(1)}, bf16[256,512]{1,0:T(8,128)(2,1)S(1)}) custom-call(bf16[512,256]{1,0:T(8,128)(2,1)S(1)} %copy-done.4, bf16[512,256]{1,0:T(8,128)(2,1)S(1)} %copy-done.3, bf16[256,512]{1,0:T(8,128)(2,1)S(1)} %copy-done.6, bf16[256,512]{1,0:T(8,128)(2,1)S(1)} %copy-done.5, f32[512,512]{1,0:T(8,128)S(1)} %get-tuple-element.43.refs_4_.refs_2_, ...), custom_call_target="tpu_custom_call" | custom-call | flops 1 | bytes 1 | tf_op jit(solution)/shard_map/pallas_call | solution.py:90
  32.1 0.6 %collective-permute-start.11 = (bf16[256,512]{1,0:T(8,128)(2,1)S(1)}, bf16[256,512]{1,0:T(8,128)(2,1)S(1)}, u32[]{:S(2)}, u32[]{:S(2)}) collective-permute-start(bf16[256,512]{1,0:T(8,128)(2,1)S(1)} %get-tuple-element.56), channel_id=1, source_target_pairs={{0,2},{1,3},{2,0},{3,1},{4,6},{5,7},{6,4},{7,5},{8,10},{9,11},{10,... | collective-permute-start | bytes 786440 | tf_op jit(solution)/shard_map/ppermute | solution.py:130
  32.7 0.0 collective-permute-done.8.refs_9_.refs_1_.refs_0_
  32.7 1.1 %shard_map.131 = (bf16[128,512]{1,0:T(8,128)(2,1)S(1)}, bf16[128,512]{1,0:T(8,128)(2,1)S(1)}, bf16[256,512]{1,0:T(8,128)(2,1)S(1)}) custom-call(bf16[256,512]{1,0:T(8,128)(2,1)S(1)} %copy-done.6, bf16[256,512]{1,0:T(8,128)(2,1)S(1)} %copy-done.5, f32[512,512]{1,0:T(8,128)S(1)} %get-tuple-element.43.refs_4_.refs_2_, ...), custom_call_target="tpu_custom_call" | custom-call | flops 1 | bytes 1 | tf_op jit(solution)/shard_map/pallas_call | solution.py:90
  33.8 0.1 collective-permute-start.12
  33.9 1.4 %collective-permute-done.14.refs_2_ = bf16[64,512]{1,0:T(8,128)(2,1)S(1)} collective-permute-done((bf16[64,512]{1,0:T(8,128)(2,1)S(1)}, bf16[64,512]{1,0:T(8,128)(2,1)S(1)}, u32[]{:S(2)}, u32[]{:S(2)}) %collective-permute-start.14) | collective-permute-done | bytes 65568 | tf_op jit(solution)/shard_map/ppermute | solution.py:130
  35.2 0.8 %collective-permute-done.15.refs_3_ = bf16[64,512]{1,0:T(8,128)(2,1)S(1)} collective-permute-done((bf16[64,512]{1,0:T(8,128)(2,1)S(1)}, bf16[64,512]{1,0:T(8,128)(2,1)S(1)}, u32[]{:S(2)}, u32[]{:S(2)}) %collective-permute-start.15) | collective-permute-done | bytes 65568 | tf_op jit(solution)/shard_map/ppermute | solution.py:130
  36.1 0.6 %collective-permute-start.16 = (f32[32,512]{1,0:T(8,128)S(1)}, f32[32,512]{1,0:T(8,128)S(1)}, u32[]{:S(2)}, u32[]{:S(2)}) collective-permute-start(f32[32,512]{1,0:T(8,128)S(1)} %get-tuple-element.65), channel_id=1, source_target_pairs={{0,2},{1,3},{2,0},{3,1},{4,6},{5,7},{6,4},{7,5},{8,10},{9,11},{10,... | collective-permute-start | bytes 196616 | tf_op jit(solution)/shard_map/ppermute | solution.py:130
  36.7 0.4 copy-done
  37.1 0.2 copy-done.1
  37.2 1.0 %shard_map.134 = (bf16[128,2048]{1,0:T(8,128)(2,1)}, bf16[128,2048]{1,0:T(8,128)(2,1)}, bf16[128,2048]{1,0:T(8,128)(2,1)}, f32[8,128]{1,0:T(8,128)S(1)}) custom-call(bf16[128,512]{1,0:T(8,128)(2,1)S(1)} %get-tuple-element.66.refs_0_, bf16[128,512]{1,0:T(8,128)(2,1)S(1)} %get-tuple-element.63.refs_4_.refs_1_, ...), custom_call_target="tpu_custom_call" | custom-call | flops 1 | bytes 1 | tf_op jit(solution)/shard_map/pallas_call | solution.py:90
  38.2 2.3 %collective-permute-done.16.refs_2_.refs_9_ = f32[32,512]{1,0:T(8,128)S(1)} collective-permute-done((f32[32,512]{1,0:T(8,128)S(1)}, f32[32,512]{1,0:T(8,128)S(1)}, u32[]{:S(2)}, u32[]{:S(2)}) %collective-permute-start.16) | collective-permute-done | bytes 65568 | tf_op jit(solution)/shard_map/ppermute | solution.py:130
  40.5 0.1 collective-permute-start.17
  40.5 0.5 %collective-permute-start.18 = (f32[32,512]{1,0:T(8,128)S(1)}, f32[32,512]{1,0:T(8,128)S(1)}, u32[]{:S(2)}, u32[]{:S(2)}) collective-permute-start(f32[32,512]{1,0:T(8,128)S(1)} %get-tuple-element.70), channel_id=1, source_target_pairs={{0,1},{1,0},{2,3},{3,2},{4,5},{5,4},{6,7},{7,6},{8,9},{9,8},{10,11... | collective-permute-start | bytes 196616 | tf_op jit(solution)/shard_map/ppermute | solution.py:130
  41.0 0.9 %collective-permute-done.18.refs_8_ = f32[32,512]{1,0:T(8,128)S(1)} collective-permute-done((f32[32,512]{1,0:T(8,128)S(1)}, f32[32,512]{1,0:T(8,128)S(1)}, u32[]{:S(2)}, u32[]{:S(2)}) %collective-permute-start.18) | collective-permute-done | bytes 65568 | tf_op jit(solution)/shard_map/ppermute | solution.py:130
  42.0 1.0 %shard_map.136 = (bf16[128,2048]{1,0:T(8,128)(2,1)}, bf16[128,2048]{1,0:T(8,128)(2,1)}, bf16[128,2048]{1,0:T(8,128)(2,1)}, f32[16,2048]{1,0:T(8,128)}) custom-call(bf16[256,512]{1,0:T(8,128)(2,1)S(1)} %collective-permute-done.8.refs_9_.refs_1_.refs_0_, ...), custom_call_target="tpu_custom_call", output_to_operand_aliasing={{0}: (10, {}), {1}: (11, {}), {2}: (12, {})} | custom-call | flops 1 | bytes 1 | tf_op jit(solution)/shard_map/pallas_call | solution.py:90
  (26 shorter events, 0.2 us)
Async XLA Ops:
  0.7 1.6 %copy-start.2 = (bf16[128,2048]{1,0:T(8,128)(2,1)S(1)}, bf16[128,2048]{1,0:T(8,128)(2,1)}, u32[]{:S(2)}) copy-start(bf16[128,2048]{1,0:T(8,128)(2,1)} %refs_4_.3) | copy-start | bytes 1572868
  0.7 1.6 %copy-start.7 = (f32[16,2048]{1,0:T(8,128)S(1)}, f32[16,2048]{1,0:T(8,128)}, u32[]{:S(2)}) copy-start(f32[16,2048]{1,0:T(8,128)} %refs_0_.9) | copy-start | bytes 393220
  0.7 1.6 %copy-start.8 = (bf16[128,2048]{1,0:T(8,128)(2,1)S(1)}, bf16[128,2048]{1,0:T(8,128)(2,1)}, u32[]{:S(2)}) copy-start(bf16[128,2048]{1,0:T(8,128)(2,1)} %refs_1_.7) | copy-start | bytes 1572868
  2.5 3.2 %collective-permute-start = (bf16[416,512]{1,0:T(8,128)(2,1)S(1)}, bf16[416,512]{1,0:T(8,128)(2,1)S(1)}, u32[]{:S(2)}, u32[]{:S(2)}) collective-permute-start(bf16[416,512]{1,0:T(8,128)(2,1)S(1)} %get-tuple-element.39), channel_id=1, source_target_pairs={{0,1},{1,0},{2,3},{3,2},{4,5},{5,4},{6,7},{7,6},{8,9},{9,8},{10,11... | collective-permute-start | bytes 1277960 | tf_op jit(solution)/shard_map/ppermute | solution.py:130
  3.0 7.2 %collective-permute-start.1 = (bf16[128,512]{1,0:T(8,128)(2,1)S(1)}, bf16[128,512]{1,0:T(8,128)(2,1)S(1)}, u32[]{:S(2)}, u32[]{:S(2)}) collective-permute-start(bf16[128,512]{1,0:T(8,128)(2,1)S(1)} %get-tuple-element.40), channel_id=1, source_target_pairs={{0,2},{1,3},{2,0},{3,1},{4,6},{5,7},{6,4},{7,5},{8,10},{9,11},{10,... | collective-permute-start | bytes 393224 | tf_op jit(solution)/shard_map/ppermute | solution.py:130
  5.5 6.6 %collective-permute-start.2 = (bf16[128,512]{1,0:T(8,128)(2,1)S(1)}, bf16[128,512]{1,0:T(8,128)(2,1)S(1)}, u32[]{:S(2)}, u32[]{:S(2)}) collective-permute-start(bf16[128,512]{1,0:T(8,128)(2,1)S(1)} %get-tuple-element.41), channel_id=1, source_target_pairs={{0,3},{1,2},{2,1},{3,0},{4,7},{5,6},{6,5},{7,4},{8,11},{9,10},{10,... | collective-permute-start | bytes 393224 | tf_op jit(solution)/shard_map/ppermute | solution.py:130
  5.6 11.1 %collective-permute-start.6 = (bf16[64,512]{1,0:T(8,128)(2,1)S(1)}, bf16[64,512]{1,0:T(8,128)(2,1)S(1)}, u32[]{:S(2)}, u32[]{:S(2)}) collective-permute-start(bf16[64,512]{1,0:T(8,128)(2,1)S(1)} %shard_map.126.refs_0_), channel_id=1, source_target_pairs={{0,12},{1,13},{2,14},{3,15},{4,8},{5,9},{6,10},{7,11},{8,4},{9,5},... | collective-permute-start | bytes 196616 | tf_op jit(solution)/shard_map/ppermute | solution.py:130
  9.5 7.2 %collective-permute-start.5 = (bf16[64,512]{1,0:T(8,128)(2,1)S(1)}, bf16[64,512]{1,0:T(8,128)(2,1)S(1)}, u32[]{:S(2)}, u32[]{:S(2)}) collective-permute-start(bf16[64,512]{1,0:T(8,128)(2,1)S(1)} %shard_map.126.refs_0_), channel_id=1, source_target_pairs={{0,8},{1,9},{2,10},{3,11},{4,12},{5,13},{6,14},{7,15},{8,0},{9,1},... | collective-permute-start | bytes 196616 | tf_op jit(solution)/shard_map/ppermute | solution.py:130
  9.5 7.2 %collective-permute-start.4 = (bf16[64,512]{1,0:T(8,128)(2,1)S(1)}, bf16[64,512]{1,0:T(8,128)(2,1)S(1)}, u32[]{:S(2)}, u32[]{:S(2)}) collective-permute-start(bf16[64,512]{1,0:T(8,128)(2,1)S(1)} %shard_map.126.refs_0_), channel_id=1, source_target_pairs={{0,4},{1,5},{2,6},{3,7},{4,0},{5,1},{6,2},{7,3},{8,12},{9,13},{10,... | collective-permute-start | bytes 196616 | tf_op jit(solution)/shard_map/ppermute | solution.py:130
  10.2 8.1 %collective-permute-start.3 = (bf16[256,512]{1,0:T(8,128)(2,1)S(1)}, bf16[256,512]{1,0:T(8,128)(2,1)S(1)}, u32[]{:S(2)}, u32[]{:S(2)}) collective-permute-start(bf16[256,512]{1,0:T(8,128)(2,1)S(1)} %shard_map.123), channel_id=1, source_target_pairs={{0,2},{1,3},{2,0},{3,1},{4,6},{5,7},{6,4},{7,5},{8,10},{9,11},{10,... | collective-permute-start | bytes 786440 | tf_op jit(solution)/shard_map/ppermute | solution.py:130
  12.2 3.8 %copy-start.3 = (bf16[512,256]{1,0:T(8,128)(2,1)S(1)}, bf16[512,256]{1,0:T(8,128)(2,1)}, u32[]{:S(2)}) copy-start(bf16[512,256]{1,0:T(8,128)(2,1)} %constant.42.clone.refs_1_) | copy-start | bytes 786436
  12.2 3.8 %copy-start.4 = (bf16[512,256]{1,0:T(8,128)(2,1)S(1)}, bf16[512,256]{1,0:T(8,128)(2,1)}, u32[]{:S(2)}) copy-start(bf16[512,256]{1,0:T(8,128)(2,1)} %constant.41.clone.refs_0_) | copy-start | bytes 786436
  12.3 13.1 %collective-permute-start.9 = (bf16[256,512]{1,0:T(8,128)(2,1)S(1)}, bf16[256,512]{1,0:T(8,128)(2,1)S(1)}, u32[]{:S(2)}, u32[]{:S(2)}) collective-permute-start(bf16[256,512]{1,0:T(8,128)(2,1)S(1)} %get-tuple-element.52), channel_id=1, source_target_pairs={{0,4},{1,5},{2,6},{3,7},{4,8},{5,9},{6,10},{7,11},{8,12},{9,13},{1... | collective-permute-start | bytes 786440 | tf_op jit(solution)/shard_map/ppermute | solution.py:133
  16.8 5.9 %collective-permute-start.7 = (bf16[128,512]{1,0:T(8,128)(2,1)S(1)}, bf16[128,512]{1,0:T(8,128)(2,1)S(1)}, u32[]{:S(2)}, u32[]{:S(2)}) collective-permute-start(bf16[128,512]{1,0:T(8,128)(2,1)S(1)} %get-tuple-element.50), channel_id=1, source_target_pairs={{0,2},{1,3},{2,0},{3,1},{4,6},{5,7},{6,4},{7,5},{8,10},{9,11},{10,... | collective-permute-start | bytes 393224 | tf_op jit(solution)/shard_map/ppermute | solution.py:130
  18.4 12.6 %collective-permute-start.10 = (bf16[256,512]{1,0:T(8,128)(2,1)S(1)}, bf16[256,512]{1,0:T(8,128)(2,1)S(1)}, u32[]{:S(2)}, u32[]{:S(2)}) collective-permute-start(bf16[256,512]{1,0:T(8,128)(2,1)S(1)} %get-tuple-element.55), channel_id=1, source_target_pairs={{4,0},{5,1},{6,2},{7,3},{8,4},{9,5},{10,6},{11,7},{12,8},{13,9},{1... | collective-permute-start | bytes 786440 | tf_op jit(solution)/shard_map/ppermute | solution.py:133
  19.7 3.0 %copy-start.5 = (bf16[256,512]{1,0:T(8,128)(2,1)S(1)}, bf16[256,512]{1,0:T(8,128)(2,1)}, u32[]{:S(2)}) copy-start(bf16[256,512]{1,0:T(8,128)(2,1)} %constant.44.clone.refs_3_.refs_1_) | copy-start | bytes 786436
  19.7 3.0 %copy-start.6 = (bf16[256,512]{1,0:T(8,128)(2,1)S(1)}, bf16[256,512]{1,0:T(8,128)(2,1)}, u32[]{:S(2)}) copy-start(bf16[256,512]{1,0:T(8,128)(2,1)} %constant.43.clone.refs_2_.refs_0_) | copy-start | bytes 786436
  23.8 8.8 %collective-permute-start.8 = (bf16[256,512]{1,0:T(8,128)(2,1)S(1)}, bf16[256,512]{1,0:T(8,128)(2,1)S(1)}, u32[]{:S(2)}, u32[]{:S(2)}) collective-permute-start(bf16[256,512]{1,0:T(8,128)(2,1)S(1)} %get-tuple-element.51), channel_id=1, source_target_pairs={{0,2},{1,3},{2,0},{3,1},{4,6},{5,7},{6,4},{7,5},{8,10},{9,11},{10,... | collective-permute-start | bytes 786440 | tf_op jit(solution)/shard_map/ppermute | solution.py:130
  26.5 7.3 %collective-permute-start.13 = (bf16[64,512]{1,0:T(8,128)(2,1)S(1)}, bf16[64,512]{1,0:T(8,128)(2,1)S(1)}, u32[]{:S(2)}, u32[]{:S(2)}) collective-permute-start(bf16[64,512]{1,0:T(8,128)(2,1)S(1)} %get-tuple-element.60), channel_id=1, source_target_pairs={{0,4},{1,5},{2,6},{3,7},{4,0},{5,1},{6,2},{7,3},{8,12},{9,13},{10,... | collective-permute-start | bytes 196616 | tf_op jit(solution)/shard_map/ppermute | solution.py:130
  28.3 7.0 %collective-permute-start.14 = (bf16[64,512]{1,0:T(8,128)(2,1)S(1)}, bf16[64,512]{1,0:T(8,128)(2,1)S(1)}, u32[]{:S(2)}, u32[]{:S(2)}) collective-permute-start(bf16[64,512]{1,0:T(8,128)(2,1)S(1)} %get-tuple-element.61), channel_id=1, source_target_pairs={{0,8},{1,9},{2,10},{3,11},{4,12},{5,13},{6,14},{7,15},{8,0},{9,1},... | collective-permute-start | bytes 196616 | tf_op jit(solution)/shard_map/ppermute | solution.py:130
  29.8 6.2 %collective-permute-start.15 = (bf16[64,512]{1,0:T(8,128)(2,1)S(1)}, bf16[64,512]{1,0:T(8,128)(2,1)S(1)}, u32[]{:S(2)}, u32[]{:S(2)}) collective-permute-start(bf16[64,512]{1,0:T(8,128)(2,1)S(1)} %get-tuple-element.62), channel_id=1, source_target_pairs={{0,12},{1,13},{2,14},{3,15},{4,8},{5,9},{6,10},{7,11},{8,4},{9,5},... | collective-permute-start | bytes 196616 | tf_op jit(solution)/shard_map/ppermute | solution.py:130
  32.1 8.4 %collective-permute-start.11 = (bf16[256,512]{1,0:T(8,128)(2,1)S(1)}, bf16[256,512]{1,0:T(8,128)(2,1)S(1)}, u32[]{:S(2)}, u32[]{:S(2)}) collective-permute-start(bf16[256,512]{1,0:T(8,128)(2,1)S(1)} %get-tuple-element.56), channel_id=1, source_target_pairs={{0,2},{1,3},{2,0},{3,1},{4,6},{5,7},{6,4},{7,5},{8,10},{9,11},{10,... | collective-permute-start | bytes 786440 | tf_op jit(solution)/shard_map/ppermute | solution.py:130
  33.8 2.9 %collective-permute-start.12 = (bf16[384,512]{1,0:T(8,128)(2,1)S(1)}, bf16[384,512]{1,0:T(8,128)(2,1)S(1)}, u32[]{:S(2)}, u32[]{:S(2)}) collective-permute-start(bf16[384,512]{1,0:T(8,128)(2,1)S(1)} %shard_map.132), channel_id=1, source_target_pairs={{0,1},{1,0},{2,3},{3,2},{4,5},{5,4},{6,7},{7,6},{8,9},{9,8},{10,11... | collective-permute-start | bytes 1179656 | tf_op jit(solution)/shard_map/ppermute | solution.py:130
  36.0 1.0 %copy-start = (bf16[128,2048]{1,0:T(8,128)(2,1)S(1)}, bf16[128,2048]{1,0:T(8,128)(2,1)}, u32[]{:S(2)}) copy-start(bf16[128,2048]{1,0:T(8,128)(2,1)} %refs_5_.3) | copy-start | bytes 1572868
  36.0 1.2 %copy-start.1 = (bf16[128,2048]{1,0:T(8,128)(2,1)S(1)}, bf16[128,2048]{1,0:T(8,128)(2,1)}, u32[]{:S(2)}) copy-start(bf16[128,2048]{1,0:T(8,128)(2,1)} %refs_6_.1) | copy-start | bytes 1572868
  36.1 4.4 %collective-permute-start.16 = (f32[32,512]{1,0:T(8,128)S(1)}, f32[32,512]{1,0:T(8,128)S(1)}, u32[]{:S(2)}, u32[]{:S(2)}) collective-permute-start(f32[32,512]{1,0:T(8,128)S(1)} %get-tuple-element.65), channel_id=1, source_target_pairs={{0,2},{1,3},{2,0},{3,1},{4,6},{5,7},{6,4},{7,5},{8,10},{9,11},{10,... | collective-permute-start | bytes 196616 | tf_op jit(solution)/shard_map/ppermute | solution.py:130
  40.5 1.5 %collective-permute-start.17 = (bf16[128,512]{1,0:T(8,128)(2,1)S(1)}, bf16[128,512]{1,0:T(8,128)(2,1)S(1)}, u32[]{:S(2)}, u32[]{:S(2)}) collective-permute-start(bf16[128,512]{1,0:T(8,128)(2,1)S(1)} %get-tuple-element.68), channel_id=1, source_target_pairs={{0,1},{1,0},{2,3},{3,2},{4,5},{5,4},{6,7},{7,6},{8,9},{9,8},{10,11... | collective-permute-start | bytes 393224 | tf_op jit(solution)/shard_map/ppermute | solution.py:130
  40.5 1.4 %collective-permute-start.18 = (f32[32,512]{1,0:T(8,128)S(1)}, f32[32,512]{1,0:T(8,128)S(1)}, u32[]{:S(2)}, u32[]{:S(2)}) collective-permute-start(f32[32,512]{1,0:T(8,128)S(1)} %get-tuple-element.70), channel_id=1, source_target_pairs={{0,1},{1,0},{2,3},{3,2},{4,5},{5,4},{6,7},{7,6},{8,9},{9,8},{10,11... | collective-permute-start | bytes 196616 | tf_op jit(solution)/shard_map/ppermute | solution.py:130
